TPU v7x, 32 devices: a whole 2x2x4 slice. The times are simulated.
32 devices in a mesh: dp: 2 (over core), pipe: 4 (over y, x), tensor: 4 (over z).
Axes of the slice: x: 2, y: 2, z: 4, core: 2. Of those that a mesh axis runs over, the one named last changes fastest.
Arguments:
- forward_acts: bfloat16 [256, 8192], P(('dp', 'tensor'), 'pipe'), parts along dimension 0, may hold values from -6 to 6
- backward_grad: bfloat16 [256, 8192], P(('dp', 'tensor'), 'pipe'), parts along dimension 0, may hold values from -6 to 6
- stored_gate: bfloat16 [256, 14336], P(('dp', 'pipe'), 'tensor'), parts along dimension 0, may hold values from -8 to 8
- stored_up: bfloat16 [256, 14336], P(('dp', 'pipe'), 'tensor'), parts along dimension 0, may hold values from -6 to 6
- gate_weight: bfloat16 [8192, 14336], P('pipe', 'tensor'), may hold values from -0.0625 to 0.0625
- up_weight: bfloat16 [8192, 14336], P('pipe', 'tensor'), may hold values from -0.0625 to 0.0625
- down_weight: bfloat16 [14336, 8192], P('tensor', 'pipe'), may hold values from -0.046875 to 0.046875
Outputs:
- layer_output: bfloat16 [256, 8192], P(('dp', 'tensor'), 'pipe'), parts along dimension 0
- input_grad: bfloat16 [256, 8192], P(('dp', 'tensor'), 'pipe'), parts along dimension 0
There are 2 independent parts, one for each index of `dp`. A program takes and returns all parts, laid end to end along the dimension named above; an argument that names none is the same for every part. Nothing has to cross between parts.
All inputs are finite; a program needn't handle non-finite values.
Results may differ from a plain program's by a relative error of at most 0.005.
Values may be sent and summed in bfloat16 or wider, within the bound.
No kernel may reach another device: no remote copies, remote signals or barrier semaphores. Data moves between devices by JAX's collectives and lax.ppermute only.
A program may use at most 128 MiB of HBM per device.

v0:
```python
import functools

import jax
import jax.numpy as jnp
from jax import lax
from jax.experimental import pallas as pl
from jax.experimental.pallas import tpu as pltpu
from jax.sharding import PartitionSpec as P

F32 = jnp.float32
BF16 = jnp.bfloat16
VMEM_BYTES = 16 * 1024 * 1024
LOAD_BYTES = 24 * 1024 * 1024
CONTRACT_LAST = (((1,), (1,)), ((), ()))
IN_VMEM = pl.BlockSpec(memory_space=pltpu.VMEM)
IN_PLACE = pl.BlockSpec(memory_space=pl.ANY)


def exchange(value, axis, size, step):
    return lax.ppermute(value, axis, [(i, i ^ step) for i in range(size)])


def pick_tile(width):
    return 256 if width % 256 == 0 else 128


def cost(flops, moved):
    return pl.CostEstimate(flops=flops, bytes_accessed=moved, transcendentals=0)


def params():
    return pltpu.CompilerParams(vmem_limit_bytes=VMEM_BYTES)


def small_kernel(body, outs, inputs, name, after=()):
    n_in, n_after = len(inputs), len(after)

    def kernel(*refs):
        body(refs[:n_in], refs[n_in + n_after :])

    moved = sum(a.size * a.dtype.itemsize for a in inputs)
    return pl.pallas_call(
        kernel,
        in_specs=[IN_VMEM] * n_in + [IN_PLACE] * n_after,
        out_specs=[IN_VMEM] * len(outs),
        out_shape=[jax.ShapeDtypeStruct(shape, dtype) for shape, dtype in outs],
        cost_estimate=cost(moved, moved),
        compiler_params=params(),
        name=name,
    )(*inputs, *after)


def load_weights(gate_weight, up_weight, down_weight, cores):
    depth = gate_weight.shape[0]
    units = gate_weight.shape[1] // cores
    cuts = 4
    rows, unit_rows = depth // cuts, units // cuts

    def kernel(gate, up, down, wide, tall, sems):
        first = pl.multiple_of(lax.axis_index("dp") * units, units) if cores > 1 else 0
        copies = []
        for i in range(cuts):
            for k, ref in enumerate((gate, up)):
                at = pl.ds(i * rows, rows)
                copies.append((ref.at[at, pl.ds(first, units)], wide.at[k, at]))
        for i in range(cuts):
            at = pl.multiple_of(first + i * unit_rows, unit_rows)
            copies.append((down.at[pl.ds(at, unit_rows)], tall.at[0, pl.ds(i * unit_rows, unit_rows)]))
        copies = [
            pltpu.make_async_copy(source, target, sems.at[i])
            for i, (source, target) in enumerate(copies)
        ]
        for copy in copies:
            copy.start()
        for copy in copies:
            copy.wait()

    return pl.pallas_call(
        kernel,
        in_specs=[IN_PLACE] * 3,
        out_specs=[IN_VMEM] * 2,
        out_shape=[
            jax.ShapeDtypeStruct((2, depth, units), BF16),
            jax.ShapeDtypeStruct((1, units, depth), BF16),
        ],
        scratch_shapes=[pltpu.SemaphoreType.DMA((3 * cuts,))],
        compiler_params=pltpu.CompilerParams(vmem_limit_bytes=LOAD_BYTES),
        cost_estimate=cost(0, 6 * depth * units),
        name="load_weights",
    )(gate_weight, up_weight, down_weight)


def project(inputs, weights, transposed, layout, n_pipe, n_tensor, after=()):
    cores = len(inputs)
    flat = [x for pair in inputs for x in pair]
    n_in, n_after, n_out, kinds = len(flat), len(after), len(layout), weights.shape[0]
    block, depth = inputs[0][0].shape
    tokens = block * n_tensor
    units = weights.shape[1] if transposed else weights.shape[2]
    tile = pick_tile(units)
    count = units // tile
    rows = tokens // n_pipe

    def kernel(*refs):
        x_refs = refs[:n_in]
        held = refs[n_in]
        out_refs = refs[n_in + 1 + n_after : n_in + 1 + n_after + n_out]
        natural, ordered = refs[n_in + 1 + n_after + n_out :]
        t = lax.axis_index("tensor")
        p = lax.axis_index("pipe")

        def work(j, carry):
            at = pl.multiple_of(j * tile, tile)
            for k in range(kinds):
                if transposed:
                    total = lax.dot_general(
                        ordered[...], held[k, pl.ds(at, tile), :], CONTRACT_LAST, preferred_element_type=F32
                    )
                else:
                    total = jnp.dot(
                        ordered[...], held[k, :, pl.ds(at, tile)], preferred_element_type=F32
                    )
                for ref, (_, pieces) in zip(out_refs, layout):
                    for i, (s, a) in enumerate(pieces):
                        row = (s * cores + a) * rows
                        part = total[row : row + rows].astype(ref.dtype)
                        ref[k, i * rows : (i + 1) * rows, pl.ds(at, tile)] = part
            return carry

        def own_block(a, s):
            if s == 0:
                return x_refs[2 * a][...]
            return x_refs[2 * a + 1][(s - 1) * block : s * block, :]

        for a in range(cores):
            if block == rows:
                for s in range(n_tensor):
                    start = pl.multiple_of(((p ^ t ^ s) * cores + a) * rows, rows)
                    ordered[pl.ds(start, rows), :] = own_block(a, s)
                continue
            for s in range(n_tensor):
                start = pl.multiple_of((t ^ s) * block, block)
                natural[pl.ds(start, block), :] = own_block(a, s)
            for s in range(n_pipe):
                start = pl.multiple_of((p ^ s) * rows, rows)
                at = (s * cores + a) * rows
                ordered[at : at + rows, :] = natural[pl.ds(start, rows), :]
        lax.fori_loop(0, count, work, 0, unroll=True)

    return pl.pallas_call(
        kernel,
        in_specs=[IN_VMEM] * (n_in + 1) + [IN_PLACE] * n_after,
        out_specs=[IN_VMEM] * n_out,
        out_shape=[
            jax.ShapeDtypeStruct((kinds, len(pieces) * rows, units), dtype)
            for dtype, pieces in layout
        ],
        scratch_shapes=[
            pltpu.VMEM((tokens, depth), BF16),
            pltpu.VMEM((cores * tokens, depth), BF16),
        ],
        compiler_params=params(),
        cost_estimate=cost(0, 0) if transposed else cost(2 * cores * tokens * depth * units * kinds, 2 * depth * units * kinds),
        name="pull_back" if transposed else "project",
    )(*flat, weights, *after)


def contract(blocks, pieces, weights, transposed, cores, n_pipe, n_tensor, after=()):
    kinds, _, units = blocks[0].shape
    n_in, n_after = len(blocks), len(after)
    from_rows = blocks[0].shape[1] // cores
    tokens = from_rows * n_pipe
    to_rows = tokens // n_tensor
    width = weights.shape[1] if transposed else weights.shape[2]
    tile = pick_tile(width)
    count = width // tile

    def kernel(*refs):
        x_refs = refs[:n_in]
        held = refs[n_in]
        out_refs = refs[n_in + 1 + n_after : n_in + 1 + n_after + cores]
        natural, ordered = refs[n_in + 1 + n_after + cores :]
        t = lax.axis_index("tensor")
        p = lax.axis_index("pipe")

        def work(j, carry):
            at = pl.multiple_of(j * tile, tile)
            total = None
            for k in range(kinds):
                if transposed:
                    part = lax.dot_general(
                        ordered[k], held[k, pl.ds(at, tile), :], CONTRACT_LAST, preferred_element_type=F32
                    )
                else:
                    part = jnp.dot(
                        ordered[k], held[k, :, pl.ds(at, tile)], preferred_element_type=F32
                    )
                total = part if total is None else total + part
            for a in range(cores):
                part = total[a * tokens : (a + 1) * tokens]
                out_refs[a][:, pl.ds(at, tile)] = part.astype(out_refs[a].dtype)
            return carry

        def came(k, a, s):
            place, row = pieces[s][a]
            return x_refs[place][k, row : row + from_rows, :]

        for k in range(kinds):
            for a in range(cores):
                if from_rows == to_rows:
                    for s in range(n_pipe):
                        start = pl.multiple_of(a * tokens + (t ^ p ^ s) * to_rows, to_rows)
                        ordered[k, pl.ds(start, to_rows), :] = came(k, a, s)
                    continue
                for s in range(n_pipe):
                    start = pl.multiple_of((p ^ s) * from_rows, from_rows)
                    natural[pl.ds(start, from_rows), :] = came(k, a, s)
                for s in range(n_tensor):
                    start = pl.multiple_of((t ^ s) * to_rows, to_rows)
                    at = a * tokens + s * to_rows
                    ordered[k, at : at + to_rows, :] = natural[pl.ds(start, to_rows), :]
        lax.fori_loop(0, count, work, 0, unroll=True)

    return pl.pallas_call(
        kernel,
        in_specs=[IN_VMEM] * (n_in + 1) + [IN_PLACE] * n_after,
        out_specs=[IN_VMEM] * cores,
        out_shape=[
            jax.ShapeDtypeStruct((tokens, width), BF16 if a else F32) for a in range(cores)
        ],
        scratch_shapes=[
            pltpu.VMEM((tokens, units), BF16),
            pltpu.VMEM((kinds, cores * tokens, units), BF16),
        ],
        compiler_params=params(),
        cost_estimate=cost(2 * cores * tokens * units * width * kinds, 2 * units * width * kinds),
        name="input_grad" if transposed else "layer_output",
    )(*blocks, weights, *after)


def gather_first(value, n_tensor):
    came = {s: exchange(value, "tensor", n_tensor, s) for s in range(n_tensor - 1, 0, -1)}
    return [value] + [came[s] for s in range(1, n_tensor)]


def gather_tokens(blocks, other, cores, after=()):
    own, came = blocks[0], blocks[1:]
    rows, width = own.shape

    def body(ins, outs):
        for s, ref in enumerate(ins):
            outs[0][s * rows : (s + 1) * rows, :] = ref[...]

    shape = (rows * len(came), width)
    (rest,) = small_kernel(body, [(shape, BF16)], came, "assemble", after)
    if cores == 1:
        return [(own, rest)]
    return [(own, rest), (other, exchange(rest, "dp", cores, 1))]


def finish(partials, cores, n_tensor, after=()):
    if cores > 1:
        other = exchange(partials[1], "dp", cores, 1)
        rows, width = other.shape[0] // n_tensor, other.shape[1]

        def body(ins, outs):
            for s in range(n_tensor):
                at = slice(s * rows, (s + 1) * rows)
                outs[s][...] = (ins[0][at] + ins[1][at].astype(F32)).astype(outs[s].dtype)

        parts = small_kernel(
            body,
            [((rows, width), BF16 if s else F32) for s in range(n_tensor)],
            [partials[0], other],
            "add_core",
            after,
        )
    else:
        rows = partials[0].shape[0] // n_tensor
        parts = [
            partials[0][s * rows : (s + 1) * rows].astype(BF16 if s else F32)
            for s in range(n_tensor)
        ]

    came = [exchange(parts[s], "tensor", n_tensor, s) for s in range(n_tensor - 1, 0, -1)]
    total = parts[0]
    for value in came:
        total = total + value.astype(F32)
    return came, total.astype(BF16)


def slope_values(grad, gate, up):
    gate, up = gate.astype(F32), up.astype(F32)
    sigma = jax.nn.sigmoid(gate)
    gate_slope = (grad * up * sigma * (1.0 + gate * (1.0 - sigma))).astype(BF16)
    up_slope = (grad * gate * sigma).astype(BF16)
    return gate_slope, up_slope


def direct(
    n_pipe, n_tensor, forward_acts, backward_grad, stored_gate, stored_up, gate_weight, up_weight, down_weight
):
    layout = [(BF16 if s else F32, [(s, 0)]) for s in range(n_pipe)]
    pieces = [[(s, 0)] for s in range(n_pipe)]

    def total_of(parts):
        total = parts[0]
        for s in range(1, n_pipe):
            total = total + exchange(parts[s], "pipe", n_pipe, s).astype(F32)
        return total

    def gather(value):
        return [value] + [exchange(value, "pipe", n_pipe, s) for s in range(1, n_pipe)]

    wide, tall = load_weights(gate_weight, up_weight, down_weight, 1)
    grads = gather_tokens(gather_first(backward_grad, n_tensor), None, 1)
    acts = gather_tokens(gather_first(forward_acts, n_tensor), None, 1)
    grad = total_of(project(grads, tall, True, layout, n_pipe, n_tensor))[0]
    slopes = gather(jnp.stack(slope_values(grad, stored_gate, stored_up)))
    summed = total_of(project(acts, wide, False, layout, n_pipe, n_tensor))
    hidden = gather((jax.nn.silu(summed[:1]) * summed[1:]).astype(BF16))
    back = contract(slopes, pieces, wide, True, 1, n_pipe, n_tensor)
    out = contract(hidden, pieces, tall, False, 1, n_pipe, n_tensor)
    return finish(out, 1, n_tensor)[1], finish(back, 1, n_tensor)[1]


def balanced(
    n_tensor, forward_acts, backward_grad, stored_gate, stored_up, gate_weight, up_weight, down_weight
):
    cores, n_pipe, x, y = 2, 4, 1, 2
    units = gate_weight.shape[1] // cores
    rows = stored_gate.shape[0]
    straight = [(BF16 if s else F32, [(s, 0), (s, 1)]) for s in range(n_pipe)]
    balanced_layout = [
        (F32, [(0, 0), (0, 1), (1, 1), (2, 0)]),
        (BF16, [(3, 0), (1, 0)]),
        (BF16, [(3, 1), (2, 1)]),
    ]
    straight_pieces = [[(s, 0), (s, rows)] for s in range(n_pipe)]
    balanced_pieces = straight_pieces[:3] + [[(3, 0), (4, 0)]]


    def swap(value, step):
        return exchange(value, "pipe", n_pipe, step)

    def slopes_body(ins, outs):
        keep, came = ins[0], ins[1:n_pipe]
        for a in range(cores):
            at = slice(a * rows, (a + 1) * rows)
            grad = keep[0, at]
            for ref in came:
                grad = grad + ref[0, at].astype(F32)
            stored = ins[n_pipe + a]
            gate_slope, up_slope = slope_values(grad, stored[0], stored[1])
            outs[0][0, at] = gate_slope
            outs[0][1, at] = up_slope

    def pass_on_body(ins, outs):
        keep, came_x, came_y = ins
        for k in range(2):
            on_x = keep[k, 2 * rows : 3 * rows] + came_y[k, :rows].astype(F32)
            on_y = keep[k, 3 * rows : 4 * rows] + came_x[k, :rows].astype(F32)
            outs[0][k] = on_x.astype(BF16)
            outs[1][k] = on_y.astype(BF16)

    def hidden_body(ins, outs):
        keep, came_x, came_y, then_x, then_y = ins
        for a, near, far in ((0, came_x, then_y), (1, came_y, then_x)):
            at = slice(a * rows, (a + 1) * rows)
            gate, up = [
                keep[k, at] + near[k, rows:].astype(F32) + far[k].astype(F32) for k in range(2)
            ]
            outs[0][0, at] = (jax.nn.silu(gate) * up).astype(BF16)

    def stored_body(ins, outs):
        core = lax.axis_index("dp")
        for k in range(2):
            for c in range(cores):
                start = pl.multiple_of((core ^ c) * units, units)
                outs[c][k] = ins[k][:, pl.ds(start, units)]

    acts = gather_first(forward_acts, n_tensor)
    grads = gather_first(backward_grad, n_tensor)
    wide, tall = load_weights(gate_weight, up_weight, down_weight, cores)
    other_acts = exchange(forward_acts, "dp", cores, 1)
    other_grads = exchange(backward_grad, "dp", cores, 1)
    acts = gather_tokens(acts, other_acts, cores, after=[tall, other_acts, grads[1]])
    keep, for_x, for_y = project(
        acts, wide, False, balanced_layout, n_pipe, n_tensor, after=[other_grads]
    )
    came_x, came_y = swap(for_x, x), swap(for_y, y)
    mine, other = small_kernel(
        stored_body, [((2, rows, units), BF16)] * 2, [stored_gate, stored_up], "stored", after=[keep]
    )
    other = exchange(other, "dp", cores, 1)
    grads = gather_tokens(grads, other_grads, cores, after=[keep])
    parts = project(grads, tall, True, straight, n_pipe, n_tensor, after=[other])
    parts = [parts[0]] + [swap(parts[s], s) for s in (3, 1, 2)]

    half = ((2, rows, units), BF16)
    on_x, on_y = small_kernel(
        pass_on_body, [half, half], [keep, came_x, came_y], "pass_on", after=[parts[0]]
    )
    sums = [keep, came_x, came_y, swap(on_x, x), swap(on_y, y)]
    (hidden,) = small_kernel(hidden_body, [((1, cores * rows, units), BF16)], sums, "hidden")
    hidden_all = [hidden] + [swap(hidden, s) for s in range(1, n_pipe)]

    (slopes,) = small_kernel(
        slopes_body,
        [((2, cores * rows, units), BF16)],
        [*parts, mine, other],
        "slopes",
        after=[hidden],
    )
    slopes_x, slopes_y = swap(slopes, x), swap(slopes, y)

    out = contract(
        hidden_all, straight_pieces, tall, False, cores, n_pipe, n_tensor, after=[slopes]
    )
    slopes_all = [
        slopes,
        slopes_x,
        slopes_y,
        swap(slopes_x[:, :rows], y),
        swap(slopes_y[:, rows:], x),
    ]
    came, layer_output = finish(out, cores, n_tensor)
    back = contract(
        slopes_all,
        balanced_pieces,
        wide,
        True,
        cores,
        n_pipe,
        n_tensor,
    )

    def copy_body(ins, outs):
        outs[0][...] = ins[0][...]

    (held,) = small_kernel(copy_body, [(back[1].shape, BF16)], back[1:], "hold", after=came)
    _, input_grad = finish([back[0], held], cores, n_tensor)
    return layer_output, input_grad


def solution(mesh):
    in_specs = (
        P(("dp", "tensor"), "pipe"),
        P(("dp", "tensor"), "pipe"),
        P(("dp", "pipe"), "tensor"),
        P(("dp", "pipe"), "tensor"),
        P("pipe", "tensor"),
        P("pipe", "tensor"),
        P("tensor", "pipe"),
    )
    out_specs = (P(("dp", "tensor"), "pipe"), P(("dp", "tensor"), "pipe"))

    def whole(*args):
        n_pipe, n_tensor = mesh.shape["pipe"], mesh.shape["tensor"]
        hidden_width = args[4].shape[1] // n_tensor
        if mesh.shape["dp"] == 2 and n_pipe == 4 and hidden_width % 256 == 0:
            body = functools.partial(balanced, n_tensor)
        else:
            body = functools.partial(direct, n_pipe, n_tensor)
        return jax.shard_map(
            body, mesh=mesh, in_specs=in_specs, out_specs=out_specs, check_vma=False
        )(*args)

    return whole
```

profile of v0, /device:TPU:0, one launch (start us, length us, event | category | flops | bytes accessed | tf_op | source)
XLA Modules:
  0.0 106.6 jit_solution(4609140781133758113)
XLA Ops:
  0.7 5.1 %collective-permute-start.2 = (bf16[32,2048]{1,0:T(8,128)(2,1)}, bf16[32,2048]{1,0:T(8,128)(2,1)S(1)}, u32[]{:S(2)}, u32[]{:S(2)}) collective-permute-start(bf16[32,2048]{1,0:T(8,128)(2,1)} %refs_0_.3), channel_id=1, source_target_pairs={{0,3},{1,2},{2,1},{3,0},{4,7},{5,6},{6,5},{7,4},{8,11},{9,10},{10,... | collective-permute-start | bytes 393224 | tf_op jit(solution)/shard_map/ppermute | solution.py:20
  5.8 0.0 collective-permute-start.1
  5.8 0.6 collective-permute-start
  6.4 1.4 %collective-permute-start.4 = (bf16[32,2048]{1,0:T(8,128)(2,1)}, bf16[32,2048]{1,0:T(8,128)(2,1)S(1)}, u32[]{:S(2)}, u32[]{:S(2)}) collective-permute-start(bf16[32,2048]{1,0:T(8,128)(2,1)} %refs_0_.5), channel_id=1, source_target_pairs={{0,1},{1,0},{2,3},{3,2},{4,5},{5,4},{6,7},{7,6},{8,9},{9,8},{10,11... | collective-permute-start | bytes 393224 | tf_op jit(solution)/shard_map/ppermute | solution.py:20
  7.8 7.6 %load_weights.1 = (bf16[2,2048,1792]{2,1,0:T(8,128)(2,1)S(1)}, bf16[1,1792,2048]{2,1,0:T(8,128)(2,1)S(1)}) custom-call(bf16[2048,3584]{1,0:T(8,128)(2,1)} %gate.1, bf16[2048,3584]{1,0:T(8,128)(2,1)} %up.1, bf16[3584,2048]{1,0:T(8,128)(2,1)} %down.1), custom_call_target="tpu_custom_call" | custom-call | bytes 22020096 | tf_op jit(solution)/shard_map/load_weights/pallas_call | solution.py:78
  15.4 0.0 copy-start
  15.4 0.0 copy-start.1
  15.4 1.8 %collective-permute-done.1.refs_1_ = bf16[32,2048]{1,0:T(8,128)(2,1)S(1)} collective-permute-done((bf16[32,2048]{1,0:T(8,128)(2,1)}, bf16[32,2048]{1,0:T(8,128)(2,1)S(1)}, u32[]{:S(2)}, u32[]{:S(2)}) %collective-permute-start.1) | collective-permute-done | bytes 131104 | tf_op jit(solution)/shard_map/ppermute | solution.py:20
  17.2 0.8 collective-permute-done.4.refs_5_.refs_0_
  18.0 0.1 collective-permute-start.5
  18.1 0.5 collective-permute-start.6
  18.6 1.6 %collective-permute-start.9 = (bf16[32,2048]{1,0:T(8,128)(2,1)S(1)}, bf16[32,2048]{1,0:T(8,128)(2,1)S(1)}, u32[]{:S(2)}, u32[]{:S(2)}) collective-permute-start(bf16[32,2048]{1,0:T(8,128)(2,1)S(1)} %copy-done.3), channel_id=1, source_target_pairs={{0,2},{1,3},{2,0},{3,1},{4,6},{5,7},{6,4},{7,5},{8,10},{9,11},{10,... | collective-permute-start | bytes 393224 | tf_op jit(solution)/shard_map/ppermute | solution.py:20
  20.2 2.5 %collective-permute-start.10 = (bf16[32,2048]{1,0:T(8,128)(2,1)S(1)}, bf16[32,2048]{1,0:T(8,128)(2,1)S(1)}, u32[]{:S(2)}, u32[]{:S(2)}) collective-permute-start(bf16[32,2048]{1,0:T(8,128)(2,1)S(1)} %copy-done.3), channel_id=1, source_target_pairs={{0,3},{1,2},{2,1},{3,0},{4,7},{5,6},{6,5},{7,4},{8,11},{9,10},{10,... | collective-permute-start | bytes 393224 | tf_op jit(solution)/shard_map/ppermute | solution.py:20
  22.7 4.0 %project.1 = (f32[2,128,1792]{2,1,0:T(8,128)S(1)}, bf16[2,64,1792]{2,1,0:T(8,128)(2,1)S(1)}, bf16[2,64,1792]{2,1,0:T(8,128)(2,1)S(1)}) custom-call(bf16[32,2048]{1,0:T(8,128)(2,1)S(1)} %copy-done.2, bf16[96,2048]{1,0:T(8,128)(2,1)S(1)} %assemble.2.refs_1_, bf16[32,2048]{1,0:T(8,128)(2,1)S(1)} %collective-permute-done.3.refs_4_.refs_2_, ...), custom_call_target="tpu_custom_call" | custom-call | flops 3758096384 | bytes 14680064 | tf_op jit(solution)/shard_map/project/pallas_call | solution.py:150
  26.7 1.6 %collective-permute-start.7 = (bf16[2,64,1792]{2,1,0:T(8,128)(2,1)S(1)}, bf16[2,64,1792]{2,1,0:T(8,128)(2,1)S(1)}, u32[]{:S(2)}, u32[]{:S(2)}) collective-permute-start(bf16[2,64,1792]{2,1,0:T(8,128)(2,1)S(1)} %get-tuple-element.30), channel_id=1, source_target_pairs={{0,4},{4,0},{8,12},{12,8},{1,5},{5,1},{9,13},{13,9},{2,6},{6,2},{1... | collective-permute-start | bytes 1376264 | tf_op jit(solution)/shard_map/ppermute | solution.py:20
  28.2 1.5 %collective-permute-start.8 = (bf16[2,64,1792]{2,1,0:T(8,128)(2,1)S(1)}, bf16[2,64,1792]{2,1,0:T(8,128)(2,1)S(1)}, u32[]{:S(2)}, u32[]{:S(2)}) collective-permute-start(bf16[2,64,1792]{2,1,0:T(8,128)(2,1)S(1)} %get-tuple-element.31), channel_id=1, source_target_pairs={{0,8},{4,12},{8,0},{12,4},{1,9},{5,13},{9,1},{13,5},{2,10},{6,14},... | collective-permute-start | bytes 1376264 | tf_op jit(solution)/shard_map/ppermute | solution.py:20
  29.8 1.7 %collective-permute-done.9.refs_1_ = bf16[32,2048]{1,0:T(8,128)(2,1)S(1)} collective-permute-done((bf16[32,2048]{1,0:T(8,128)(2,1)S(1)}, bf16[32,2048]{1,0:T(8,128)(2,1)S(1)}, u32[]{:S(2)}, u32[]{:S(2)}) %collective-permute-start.9) | collective-permute-done | bytes 131104 | tf_op jit(solution)/shard_map/ppermute | solution.py:20
  31.5 0.0 collective-permute-done.10.refs_2_
  31.5 0.1 collective-permute-start.11
  31.7 0.5 collective-permute-start.12
  32.2 1.4 %collective-permute-done.12.refs_5_ = bf16[2,32,1792]{2,1,0:T(8,128)(2,1)S(1)} collective-permute-done((bf16[2,32,1792]{2,1,0:T(8,128)(2,1)S(1)}, bf16[2,32,1792]{2,1,0:T(8,128)(2,1)S(1)}, u32[]{:S(2)}, u32[]{:S(2)}) %collective-permute-start.12) | collective-permute-done | bytes 229408 | tf_op jit(solution)/shard_map/ppermute | solution.py:20
  33.6 0.0 collective-permute-done.11.refs_3_
  33.6 2.1 %pull_back.1 = (f32[1,64,1792]{2,1,0:T(8,128)S(1)}, bf16[1,64,1792]{2,1,0:T(8,128)(2,1)S(1)}, bf16[1,64,1792]{2,1,0:T(8,128)(2,1)S(1)}, bf16[1,64,1792]{2,1,0:T(8,128)(2,1)S(1)}) custom-call(bf16[32,2048]{1,0:T(8,128)(2,1)S(1)} %copy-done.3, bf16[96,2048]{1,0:T(8,128)(2,1)S(1)} %assemble.3.refs_1_, ...), custom_call_target="tpu_custom_call" | custom-call | tf_op jit(solution)/shard_map/pull_back/pallas_call | solution.py:150
  35.7 2.9 %collective-permute-done.7.refs_1_ = bf16[2,64,1792]{2,1,0:T(8,128)(2,1)S(1)} collective-permute-done((bf16[2,64,1792]{2,1,0:T(8,128)(2,1)S(1)}, bf16[2,64,1792]{2,1,0:T(8,128)(2,1)S(1)}, u32[]{:S(2)}, u32[]{:S(2)}) %collective-permute-start.7) | collective-permute-done | bytes 458784 | tf_op jit(solution)/shard_map/ppermute | solution.py:20
  38.7 1.2 %collective-permute-done.8.refs_2_ = bf16[2,64,1792]{2,1,0:T(8,128)(2,1)S(1)} collective-permute-done((bf16[2,64,1792]{2,1,0:T(8,128)(2,1)S(1)}, bf16[2,64,1792]{2,1,0:T(8,128)(2,1)S(1)}, u32[]{:S(2)}, u32[]{:S(2)}) %collective-permute-start.8) | collective-permute-done | bytes 458784 | tf_op jit(solution)/shard_map/ppermute | solution.py:20
  39.9 0.1 pass_on.1
  40.0 0.6 collective-permute-start.13
  40.6 1.5 %collective-permute-start.14 = (bf16[2,32,1792]{2,1,0:T(8,128)(2,1)S(1)}, bf16[2,32,1792]{2,1,0:T(8,128)(2,1)S(1)}, u32[]{:S(2)}, u32[]{:S(2)}) collective-permute-start(bf16[2,32,1792]{2,1,0:T(8,128)(2,1)S(1)} %get-tuple-element.35), channel_id=1, source_target_pairs={{0,8},{4,12},{8,0},{12,4},{1,9},{5,13},{9,1},{13,5},{2,10},{6,14},... | collective-permute-start | bytes 688136 | tf_op jit(solution)/shard_map/ppermute | solution.py:20
  42.1 1.4 %collective-permute-start.18 = (bf16[1,64,1792]{2,1,0:T(8,128)(2,1)S(1)}, bf16[1,64,1792]{2,1,0:T(8,128)(2,1)S(1)}, u32[]{:S(2)}, u32[]{:S(2)}) collective-permute-start(bf16[1,64,1792]{2,1,0:T(8,128)(2,1)S(1)} %get-tuple-element.36), channel_id=1, source_target_pairs={{0,12},{4,8},{8,4},{12,0},{1,13},{5,9},{9,5},{13,1},{2,14},{6,10},... | collective-permute-start | bytes 688136 | tf_op jit(solution)/shard_map/ppermute | solution.py:20
  43.5 0.5 collective-permute-start.19
  44.1 1.5 %collective-permute-start.20 = (bf16[1,64,1792]{2,1,0:T(8,128)(2,1)S(1)}, bf16[1,64,1792]{2,1,0:T(8,128)(2,1)S(1)}, u32[]{:S(2)}, u32[]{:S(2)}) collective-permute-start(bf16[1,64,1792]{2,1,0:T(8,128)(2,1)S(1)} %get-tuple-element.38), channel_id=1, source_target_pairs={{0,8},{4,12},{8,0},{12,4},{1,9},{5,13},{9,1},{13,5},{2,10},{6,14},... | collective-permute-start | bytes 688136 | tf_op jit(solution)/shard_map/ppermute | solution.py:20
  45.6 3.0 %collective-permute-done.13.refs_3_ = bf16[2,32,1792]{2,1,0:T(8,128)(2,1)S(1)} collective-permute-done((bf16[2,32,1792]{2,1,0:T(8,128)(2,1)S(1)}, bf16[2,32,1792]{2,1,0:T(8,128)(2,1)S(1)}, u32[]{:S(2)}, u32[]{:S(2)}) %collective-permute-start.13) | collective-permute-done | bytes 229408 | tf_op jit(solution)/shard_map/ppermute | solution.py:20
  48.6 4.9 %collective-permute-done.14.refs_4_ = bf16[2,32,1792]{2,1,0:T(8,128)(2,1)S(1)} collective-permute-done((bf16[2,32,1792]{2,1,0:T(8,128)(2,1)S(1)}, bf16[2,32,1792]{2,1,0:T(8,128)(2,1)S(1)}, u32[]{:S(2)}, u32[]{:S(2)}) %collective-permute-start.14) | collective-permute-done | bytes 229408 | tf_op jit(solution)/shard_map/ppermute | solution.py:20
  53.5 0.2 hidden.1.refs_6_.refs_0_
  53.7 3.1 %collective-permute-start.17 = (bf16[1,64,1792]{2,1,0:T(8,128)(2,1)S(1)}, bf16[1,64,1792]{2,1,0:T(8,128)(2,1)S(1)}, u32[]{:S(2)}, u32[]{:S(2)}) collective-permute-start(bf16[1,64,1792]{2,1,0:T(8,128)(2,1)S(1)} %hidden.1.refs_6_.refs_0_), channel_id=1, source_target_pairs={{0,12},{4,8},{8,4},{12,0},{1,13},{5,9},{9,5},{13,1},{2,14},{6,10},... | collective-permute-start | bytes 688136 | tf_op jit(solution)/shard_map/ppermute | solution.py:20
  56.8 0.5 collective-permute-start.16
  57.3 0.1 collective-permute-start.15
  57.5 1.0 collective-permute-done.19.refs_2_
  58.4 4.9 %collective-permute-done.20.refs_3_ = bf16[1,64,1792]{2,1,0:T(8,128)(2,1)S(1)} collective-permute-done((bf16[1,64,1792]{2,1,0:T(8,128)(2,1)S(1)}, bf16[1,64,1792]{2,1,0:T(8,128)(2,1)S(1)}, u32[]{:S(2)}, u32[]{:S(2)}) %collective-permute-start.20) | collective-permute-done | bytes 229408 | tf_op jit(solution)/shard_map/ppermute | solution.py:20
  63.3 0.3 slopes.1.refs_5_.refs_0_
  63.6 1.2 %collective-permute-start.26 = (bf16[2,64,1792]{2,1,0:T(8,128)(2,1)S(1)}, bf16[2,64,1792]{2,1,0:T(8,128)(2,1)S(1)}, u32[]{:S(2)}, u32[]{:S(2)}) collective-permute-start(bf16[2,64,1792]{2,1,0:T(8,128)(2,1)S(1)} %slopes.1.refs_5_.refs_0_), channel_id=1, source_target_pairs={{0,8},{4,12},{8,0},{12,4},{1,9},{5,13},{9,1},{13,5},{2,10},{6,14},... | collective-permute-start | bytes 1376264 | tf_op jit(solution)/shard_map/ppermute | solution.py:20
  64.8 0.6 collective-permute-start.25
  65.4 3.3 %collective-permute-done.16.refs_2_ = bf16[1,64,1792]{2,1,0:T(8,128)(2,1)S(1)} collective-permute-done((bf16[1,64,1792]{2,1,0:T(8,128)(2,1)S(1)}, bf16[1,64,1792]{2,1,0:T(8,128)(2,1)S(1)}, u32[]{:S(2)}, u32[]{:S(2)}) %collective-permute-start.16) | collective-permute-done | bytes 229408 | tf_op jit(solution)/shard_map/ppermute | solution.py:20
  68.7 0.1 collective-permute-done.15.refs_1_
  68.8 2.1 %layer_output.1 = (f32[128,2048]{1,0:T(8,128)S(1)}, bf16[128,2048]{1,0:T(8,128)(2,1)S(1)}) custom-call(bf16[1,64,1792]{2,1,0:T(8,128)(2,1)S(1)} %hidden.1.refs_6_.refs_0_, bf16[1,64,1792]{2,1,0:T(8,128)(2,1)S(1)} %collective-permute-done.15.refs_1_, bf16[1,64,1792]{2,1,0:T(8,128)(2,1)S(1)} %collective-permute-done.16.refs_2_, ...), custom_call_target="tpu_custom_call" | custom-call | flops 1879048192 | bytes 7340032 | tf_op jit(solution)/shard_map/layer_output/pallas_call | solution.py:224
  70.9 0.1 collective-permute-start.21
  71.0 4.9 %collective-permute-done.26.refs_2_ = bf16[2,64,1792]{2,1,0:T(8,128)(2,1)S(1)} collective-permute-done((bf16[2,64,1792]{2,1,0:T(8,128)(2,1)S(1)}, bf16[2,64,1792]{2,1,0:T(8,128)(2,1)S(1)}, u32[]{:S(2)}, u32[]{:S(2)}) %collective-permute-start.26) | collective-permute-done | bytes 458784 | tf_op jit(solution)/shard_map/ppermute | solution.py:20
  75.9 1.3 %collective-permute-start.28 = (bf16[2,32,1792]{2,1,0:T(8,128)(2,1)S(1)}, bf16[2,32,1792]{2,1,0:T(8,128)(2,1)S(1)}, u32[]{:S(2)}, u32[]{:S(2)}) collective-permute-start(bf16[2,32,1792]{2,1,0:T(8,128)(2,1)S(1)} %slice.9), channel_id=1, source_target_pairs={{0,4},{4,0},{8,12},{12,8},{1,5},{5,1},{9,13},{13,9},{2,6},{6,2},{1... | collective-permute-start | bytes 688136 | tf_op jit(solution)/shard_map/ppermute | solution.py:20
  77.2 1.6 %collective-permute-start.27 = (bf16[2,32,1792]{2,1,0:T(8,128)(2,1)S(1)}, bf16[2,32,1792]{2,1,0:T(8,128)(2,1)S(1)}, u32[]{:S(2)}, u32[]{:S(2)}) collective-permute-start(bf16[2,32,1792]{2,1,0:T(8,128)(2,1)S(1)} %slice.8), channel_id=1, source_target_pairs={{0,8},{4,12},{8,0},{12,4},{1,9},{5,13},{9,1},{13,5},{2,10},{6,14},... | collective-permute-start | bytes 688136 | tf_op jit(solution)/shard_map/ppermute | solution.py:20
  78.8 0.1 add_core.2
  78.9 1.4 %collective-permute-start.22 = (bf16[32,2048]{1,0:T(8,128)(2,1)S(1)}, bf16[32,2048]{1,0:T(8,128)(2,1)S(1)}, u32[]{:S(2)}, u32[]{:S(2)}) collective-permute-start(bf16[32,2048]{1,0:T(8,128)(2,1)S(1)} %get-tuple-element.43), channel_id=1, source_target_pairs={{0,3},{1,2},{2,1},{3,0},{4,7},{5,6},{6,5},{7,4},{8,11},{9,10},{10,... | collective-permute-start | bytes 393224 | tf_op jit(solution)/shard_map/ppermute | solution.py:20
  80.3 0.8 collective-permute-start.23
  81.1 2.3 %collective-permute-start.24 = (bf16[32,2048]{1,0:T(8,128)(2,1)S(1)}, bf16[32,2048]{1,0:T(8,128)(2,1)S(1)}, u32[]{:S(2)}, u32[]{:S(2)}) collective-permute-start(bf16[32,2048]{1,0:T(8,128)(2,1)S(1)} %get-tuple-element.45), channel_id=1, source_target_pairs={{0,1},{1,0},{2,3},{3,2},{4,5},{5,4},{6,7},{7,6},{8,9},{9,8},{10,11... | collective-permute-start | bytes 393224 | tf_op jit(solution)/shard_map/ppermute | solution.py:20
  83.4 4.0 %input_grad.1 = (f32[128,2048]{1,0:T(8,128)S(1)}, bf16[128,2048]{1,0:T(8,128)(2,1)S(1)}) custom-call(bf16[2,64,1792]{2,1,0:T(8,128)(2,1)S(1)} %slopes.1.refs_5_.refs_0_, bf16[2,64,1792]{2,1,0:T(8,128)(2,1)S(1)} %collective-permute-done.25.refs_1_, bf16[2,64,1792]{2,1,0:T(8,128)(2,1)S(1)} %collective-permute-done.26.refs_2_, ...), custom_call_target="tpu_custom_call" | custom-call | flops 3758096384 | bytes 14680064 | tf_op jit(solution)/shard_map/input_grad/pallas_call | solution.py:224
  87.4 3.3 %collective-permute-done.23.refs_2_ = bf16[32,2048]{1,0:T(8,128)(2,1)S(1)} collective-permute-done((bf16[32,2048]{1,0:T(8,128)(2,1)S(1)}, bf16[32,2048]{1,0:T(8,128)(2,1)S(1)}, u32[]{:S(2)}, u32[]{:S(2)}) %collective-permute-start.23) | collective-permute-done | bytes 131104 | tf_op jit(solution)/shard_map/ppermute | solution.py:20
  90.8 0.1 collective-permute-start.29
  90.8 1.9 %collective-permute-done.29.refs_1_ = bf16[128,2048]{1,0:T(8,128)(2,1)S(1)} collective-permute-done((bf16[128,2048]{1,0:T(8,128)(2,1)S(1)}, bf16[128,2048]{1,0:T(8,128)(2,1)S(1)}, u32[]{:S(2)}, u32[]{:S(2)}) %collective-permute-start.29) | collective-permute-done | bytes 524320 | tf_op jit(solution)/shard_map/ppermute | solution.py:20
  92.7 0.1 add_core.3
  92.8 1.9 %collective-permute-start.30 = (bf16[32,2048]{1,0:T(8,128)(2,1)S(1)}, bf16[32,2048]{1,0:T(8,128)(2,1)S(1)}, u32[]{:S(2)}, u32[]{:S(2)}) collective-permute-start(bf16[32,2048]{1,0:T(8,128)(2,1)S(1)} %get-tuple-element.49), channel_id=1, source_target_pairs={{0,3},{1,2},{2,1},{3,0},{4,7},{5,6},{6,5},{7,4},{8,11},{9,10},{10,... | collective-permute-start | bytes 393224 | tf_op jit(solution)/shard_map/ppermute | solution.py:20
  94.7 2.6 %collective-permute-start.32 = (bf16[32,2048]{1,0:T(8,128)(2,1)S(1)}, bf16[32,2048]{1,0:T(8,128)(2,1)S(1)}, u32[]{:S(2)}, u32[]{:S(2)}) collective-permute-start(bf16[32,2048]{1,0:T(8,128)(2,1)S(1)} %get-tuple-element.51), channel_id=1, source_target_pairs={{0,1},{1,0},{2,3},{3,2},{4,5},{5,4},{6,7},{7,6},{8,9},{9,8},{10,11... | collective-permute-start | bytes 393224 | tf_op jit(solution)/shard_map/ppermute | solution.py:20
  97.3 0.7 add_convert_fusion.1
  98.0 3.2 %collective-permute-done.30 = bf16[32,2048]{1,0:T(8,128)(2,1)S(1)} collective-permute-done((bf16[32,2048]{1,0:T(8,128)(2,1)S(1)}, bf16[32,2048]{1,0:T(8,128)(2,1)S(1)}, u32[]{:S(2)}, u32[]{:S(2)}) %collective-permute-start.30) | collective-permute-done | bytes 131104 | tf_op jit(solution)/shard_map/ppermute | solution.py:20
  101.2 4.7 %collective-permute-done.31 = bf16[32,2048]{1,0:T(8,128)(2,1)S(1)} collective-permute-done((bf16[32,2048]{1,0:T(8,128)(2,1)S(1)}, bf16[32,2048]{1,0:T(8,128)(2,1)S(1)}, u32[]{:S(2)}, u32[]{:S(2)}) %collective-permute-start.31) | collective-permute-done | bytes 131104 | tf_op jit(solution)/shard_map/ppermute | solution.py:20
  105.9 0.7 add_convert_fusion
  (28 shorter events, 0.2 us)
Async XLA Ops:
  0.6 22.0 %copy-start.2 = (bf16[32,2048]{1,0:T(8,128)(2,1)S(1)}, bf16[32,2048]{1,0:T(8,128)(2,1)}, u32[]{:S(2)}) copy-start(bf16[32,2048]{1,0:T(8,128)(2,1)} %refs_0_.3) | copy-start | bytes 393220
  0.6 17.5 %copy-start.3 = (bf16[32,2048]{1,0:T(8,128)(2,1)S(1)}, bf16[32,2048]{1,0:T(8,128)(2,1)}, u32[]{:S(2)}) copy-start(bf16[32,2048]{1,0:T(8,128)(2,1)} %refs_0_.5) | copy-start | bytes 393220
  0.7 14.7 %collective-permute-start.2 = (bf16[32,2048]{1,0:T(8,128)(2,1)}, bf16[32,2048]{1,0:T(8,128)(2,1)S(1)}, u32[]{:S(2)}, u32[]{:S(2)}) collective-permute-start(bf16[32,2048]{1,0:T(8,128)(2,1)} %refs_0_.3), channel_id=1, source_target_pairs={{0,3},{1,2},{2,1},{3,0},{4,7},{5,6},{6,5},{7,4},{8,11},{9,10},{10,... | collective-permute-start | bytes 393224 | tf_op jit(solution)/shard_map/ppermute | solution.py:20
  5.8 11.4 %collective-permute-start.1 = (bf16[32,2048]{1,0:T(8,128)(2,1)}, bf16[32,2048]{1,0:T(8,128)(2,1)S(1)}, u32[]{:S(2)}, u32[]{:S(2)}) collective-permute-start(bf16[32,2048]{1,0:T(8,128)(2,1)} %refs_0_.3), channel_id=1, source_target_pairs={{0,2},{1,3},{2,0},{3,1},{4,6},{5,7},{6,4},{7,5},{8,10},{9,11},{10,... | collective-permute-start | bytes 393224 | tf_op jit(solution)/shard_map/ppermute | solution.py:20
  5.8 11.4 %collective-permute-start = (bf16[32,2048]{1,0:T(8,128)(2,1)}, bf16[32,2048]{1,0:T(8,128)(2,1)S(1)}, u32[]{:S(2)}, u32[]{:S(2)}) collective-permute-start(bf16[32,2048]{1,0:T(8,128)(2,1)} %refs_0_.3), channel_id=1, source_target_pairs={{0,1},{1,0},{2,3},{3,2},{4,5},{5,4},{6,7},{7,6},{8,9},{9,8},{10,11... | collective-permute-start | bytes 393224 | tf_op jit(solution)/shard_map/ppermute | solution.py:20
  6.4 10.8 %collective-permute-start.3 = (bf16[32,2048]{1,0:T(8,128)(2,1)}, bf16[32,2048]{1,0:T(8,128)(2,1)S(1)}, u32[]{:S(2)}, u32[]{:S(2)}) collective-permute-start(bf16[32,2048]{1,0:T(8,128)(2,1)} %refs_0_.3), channel_id=1, source_target_pairs={{0,16},{16,0},{1,17},{17,1},{2,18},{18,2},{3,19},{19,3},{4,20},{20... | collective-permute-start | bytes 393224 | tf_op jit(solution)/shard_map/ppermute | solution.py:20
  6.4 11.6 %collective-permute-start.4 = (bf16[32,2048]{1,0:T(8,128)(2,1)}, bf16[32,2048]{1,0:T(8,128)(2,1)S(1)}, u32[]{:S(2)}, u32[]{:S(2)}) collective-permute-start(bf16[32,2048]{1,0:T(8,128)(2,1)} %refs_0_.5), channel_id=1, source_target_pairs={{0,1},{1,0},{2,3},{3,2},{4,5},{5,4},{6,7},{7,6},{8,9},{9,8},{10,11... | collective-permute-start | bytes 393224 | tf_op jit(solution)/shard_map/ppermute | solution.py:20
  15.4 16.2 %copy-start = (bf16[32,3584]{1,0:T(8,128)(2,1)S(1)}, bf16[32,3584]{1,0:T(8,128)(2,1)}, u32[]{:S(2)}) copy-start(bf16[32,3584]{1,0:T(8,128)(2,1)} %refs_0_.4) | copy-start | bytes 688132
  15.4 16.2 %copy-start.1 = (bf16[32,3584]{1,0:T(8,128)(2,1)S(1)}, bf16[32,3584]{1,0:T(8,128)(2,1)}, u32[]{:S(2)}) copy-start(bf16[32,3584]{1,0:T(8,128)(2,1)} %refs_1_.1) | copy-start | bytes 688132
  18.0 4.6 %collective-permute-start.5 = (bf16[96,2048]{1,0:T(8,128)(2,1)S(1)}, bf16[96,2048]{1,0:T(8,128)(2,1)S(1)}, u32[]{:S(2)}, u32[]{:S(2)}) collective-permute-start(bf16[96,2048]{1,0:T(8,128)(2,1)S(1)} %assemble.2.refs_1_), channel_id=1, source_target_pairs={{0,16},{16,0},{1,17},{17,1},{2,18},{18,2},{3,19},{19,3},{4,20},{20... | collective-permute-start | bytes 1179656 | tf_op jit(solution)/shard_map/ppermute | solution.py:20
  18.1 4.5 %collective-permute-start.6 = (bf16[32,2048]{1,0:T(8,128)(2,1)S(1)}, bf16[32,2048]{1,0:T(8,128)(2,1)S(1)}, u32[]{:S(2)}, u32[]{:S(2)}) collective-permute-start(bf16[32,2048]{1,0:T(8,128)(2,1)S(1)} %copy-done.3), channel_id=1, source_target_pairs={{0,16},{16,0},{1,17},{17,1},{2,18},{18,2},{3,19},{19,3},{4,20},{20... | collective-permute-start | bytes 393224 | tf_op jit(solution)/shard_map/ppermute | solution.py:20
  18.6 12.9 %collective-permute-start.9 = (bf16[32,2048]{1,0:T(8,128)(2,1)S(1)}, bf16[32,2048]{1,0:T(8,128)(2,1)S(1)}, u32[]{:S(2)}, u32[]{:S(2)}) collective-permute-start(bf16[32,2048]{1,0:T(8,128)(2,1)S(1)} %copy-done.3), channel_id=1, source_target_pairs={{0,2},{1,3},{2,0},{3,1},{4,6},{5,7},{6,4},{7,5},{8,10},{9,11},{10,... | collective-permute-start | bytes 393224 | tf_op jit(solution)/shard_map/ppermute | solution.py:20
  20.2 11.3 %collective-permute-start.10 = (bf16[32,2048]{1,0:T(8,128)(2,1)S(1)}, bf16[32,2048]{1,0:T(8,128)(2,1)S(1)}, u32[]{:S(2)}, u32[]{:S(2)}) collective-permute-start(bf16[32,2048]{1,0:T(8,128)(2,1)S(1)} %copy-done.3), channel_id=1, source_target_pairs={{0,3},{1,2},{2,1},{3,0},{4,7},{5,6},{6,5},{7,4},{8,11},{9,10},{10,... | collective-permute-start | bytes 393224 | tf_op jit(solution)/shard_map/ppermute | solution.py:20
  26.7 12.0 %collective-permute-start.7 = (bf16[2,64,1792]{2,1,0:T(8,128)(2,1)S(1)}, bf16[2,64,1792]{2,1,0:T(8,128)(2,1)S(1)}, u32[]{:S(2)}, u32[]{:S(2)}) collective-permute-start(bf16[2,64,1792]{2,1,0:T(8,128)(2,1)S(1)} %get-tuple-element.30), channel_id=1, source_target_pairs={{0,4},{4,0},{8,12},{12,8},{1,5},{5,1},{9,13},{13,9},{2,6},{6,2},{1... | collective-permute-start | bytes 1376264 | tf_op jit(solution)/shard_map/ppermute | solution.py:20
  28.2 11.7 %collective-permute-start.8 = (bf16[2,64,1792]{2,1,0:T(8,128)(2,1)S(1)}, bf16[2,64,1792]{2,1,0:T(8,128)(2,1)S(1)}, u32[]{:S(2)}, u32[]{:S(2)}) collective-permute-start(bf16[2,64,1792]{2,1,0:T(8,128)(2,1)S(1)} %get-tuple-element.31), channel_id=1, source_target_pairs={{0,8},{4,12},{8,0},{12,4},{1,9},{5,13},{9,1},{13,5},{2,10},{6,14},... | collective-permute-start | bytes 1376264 | tf_op jit(solution)/shard_map/ppermute | solution.py:20
  31.5 2.1 %collective-permute-start.11 = (bf16[96,2048]{1,0:T(8,128)(2,1)S(1)}, bf16[96,2048]{1,0:T(8,128)(2,1)S(1)}, u32[]{:S(2)}, u32[]{:S(2)}) collective-permute-start(bf16[96,2048]{1,0:T(8,128)(2,1)S(1)} %assemble.3.refs_1_), channel_id=1, source_target_pairs={{0,16},{16,0},{1,17},{17,1},{2,18},{18,2},{3,19},{19,3},{4,20},{20... | collective-permute-start | bytes 1179656 | tf_op jit(solution)/shard_map/ppermute | solution.py:20
  31.7 2.0 %collective-permute-start.12 = (bf16[2,32,1792]{2,1,0:T(8,128)(2,1)S(1)}, bf16[2,32,1792]{2,1,0:T(8,128)(2,1)S(1)}, u32[]{:S(2)}, u32[]{:S(2)}) collective-permute-start(bf16[2,32,1792]{2,1,0:T(8,128)(2,1)S(1)} %get-tuple-element.32), channel_id=1, source_target_pairs={{0,16},{16,0},{1,17},{17,1},{2,18},{18,2},{3,19},{19,3},{4,20},{20... | collective-permute-start | bytes 688136 | tf_op jit(solution)/shard_map/ppermute | solution.py:20
  40.0 8.6 %collective-permute-start.13 = (bf16[2,32,1792]{2,1,0:T(8,128)(2,1)S(1)}, bf16[2,32,1792]{2,1,0:T(8,128)(2,1)S(1)}, u32[]{:S(2)}, u32[]{:S(2)}) collective-permute-start(bf16[2,32,1792]{2,1,0:T(8,128)(2,1)S(1)} %get-tuple-element.34), channel_id=1, source_target_pairs={{0,4},{4,0},{8,12},{12,8},{1,5},{5,1},{9,13},{13,9},{2,6},{6,2},{1... | collective-permute-start | bytes 688136 | tf_op jit(solution)/shard_map/ppermute | solution.py:20
  40.6 12.9 %collective-permute-start.14 = (bf16[2,32,1792]{2,1,0:T(8,128)(2,1)S(1)}, bf16[2,32,1792]{2,1,0:T(8,128)(2,1)S(1)}, u32[]{:S(2)}, u32[]{:S(2)}) collective-permute-start(bf16[2,32,1792]{2,1,0:T(8,128)(2,1)S(1)} %get-tuple-element.35), channel_id=1, source_target_pairs={{0,8},{4,12},{8,0},{12,4},{1,9},{5,13},{9,1},{13,5},{2,10},{6,14},... | collective-permute-start | bytes 688136 | tf_op jit(solution)/shard_map/ppermute | solution.py:20
  42.1 15.2 %collective-permute-start.18 = (bf16[1,64,1792]{2,1,0:T(8,128)(2,1)S(1)}, bf16[1,64,1792]{2,1,0:T(8,128)(2,1)S(1)}, u32[]{:S(2)}, u32[]{:S(2)}) collective-permute-start(bf16[1,64,1792]{2,1,0:T(8,128)(2,1)S(1)} %get-tuple-element.36), channel_id=1, source_target_pairs={{0,12},{4,8},{8,4},{12,0},{1,13},{5,9},{9,5},{13,1},{2,14},{6,10},... | collective-permute-start | bytes 688136 | tf_op jit(solution)/shard_map/ppermute | solution.py:20
  43.5 14.9 %collective-permute-start.19 = (bf16[1,64,1792]{2,1,0:T(8,128)(2,1)S(1)}, bf16[1,64,1792]{2,1,0:T(8,128)(2,1)S(1)}, u32[]{:S(2)}, u32[]{:S(2)}) collective-permute-start(bf16[1,64,1792]{2,1,0:T(8,128)(2,1)S(1)} %get-tuple-element.37), channel_id=1, source_target_pairs={{0,4},{4,0},{8,12},{12,8},{1,5},{5,1},{9,13},{13,9},{2,6},{6,2},{1... | collective-permute-start | bytes 688136 | tf_op jit(solution)/shard_map/ppermute | solution.py:20
  44.1 19.2 %collective-permute-start.20 = (bf16[1,64,1792]{2,1,0:T(8,128)(2,1)S(1)}, bf16[1,64,1792]{2,1,0:T(8,128)(2,1)S(1)}, u32[]{:S(2)}, u32[]{:S(2)}) collective-permute-start(bf16[1,64,1792]{2,1,0:T(8,128)(2,1)S(1)} %get-tuple-element.38), channel_id=1, source_target_pairs={{0,8},{4,12},{8,0},{12,4},{1,9},{5,13},{9,1},{13,5},{2,10},{6,14},... | collective-permute-start | bytes 688136 | tf_op jit(solution)/shard_map/ppermute | solution.py:20
  53.7 11.7 %collective-permute-start.17 = (bf16[1,64,1792]{2,1,0:T(8,128)(2,1)S(1)}, bf16[1,64,1792]{2,1,0:T(8,128)(2,1)S(1)}, u32[]{:S(2)}, u32[]{:S(2)}) collective-permute-start(bf16[1,64,1792]{2,1,0:T(8,128)(2,1)S(1)} %hidden.1.refs_6_.refs_0_), channel_id=1, source_target_pairs={{0,12},{4,8},{8,4},{12,0},{1,13},{5,9},{9,5},{13,1},{2,14},{6,10},... | collective-permute-start | bytes 688136 | tf_op jit(solution)/shard_map/ppermute | solution.py:20
  56.8 11.9 %collective-permute-start.16 = (bf16[1,64,1792]{2,1,0:T(8,128)(2,1)S(1)}, bf16[1,64,1792]{2,1,0:T(8,128)(2,1)S(1)}, u32[]{:S(2)}, u32[]{:S(2)}) collective-permute-start(bf16[1,64,1792]{2,1,0:T(8,128)(2,1)S(1)} %hidden.1.refs_6_.refs_0_), channel_id=1, source_target_pairs={{0,8},{4,12},{8,0},{12,4},{1,9},{5,13},{9,1},{13,5},{2,10},{6,14},... | collective-permute-start | bytes 688136 | tf_op jit(solution)/shard_map/ppermute | solution.py:20
  57.3 11.5 %collective-permute-start.15 = (bf16[1,64,1792]{2,1,0:T(8,128)(2,1)S(1)}, bf16[1,64,1792]{2,1,0:T(8,128)(2,1)S(1)}, u32[]{:S(2)}, u32[]{:S(2)}) collective-permute-start(bf16[1,64,1792]{2,1,0:T(8,128)(2,1)S(1)} %hidden.1.refs_6_.refs_0_), channel_id=1, source_target_pairs={{0,4},{4,0},{8,12},{12,8},{1,5},{5,1},{9,13},{13,9},{2,6},{6,2},{1... | collective-permute-start | bytes 688136 | tf_op jit(solution)/shard_map/ppermute | solution.py:20
  63.6 12.2 %collective-permute-start.26 = (bf16[2,64,1792]{2,1,0:T(8,128)(2,1)S(1)}, bf16[2,64,1792]{2,1,0:T(8,128)(2,1)S(1)}, u32[]{:S(2)}, u32[]{:S(2)}) collective-permute-start(bf16[2,64,1792]{2,1,0:T(8,128)(2,1)S(1)} %slopes.1.refs_5_.refs_0_), channel_id=1, source_target_pairs={{0,8},{4,12},{8,0},{12,4},{1,9},{5,13},{9,1},{13,5},{2,10},{6,14},... | collective-permute-start | bytes 1376264 | tf_op jit(solution)/shard_map/ppermute | solution.py:20
  64.8 12.4 %collective-permute-start.25 = (bf16[2,64,1792]{2,1,0:T(8,128)(2,1)S(1)}, bf16[2,64,1792]{2,1,0:T(8,128)(2,1)S(1)}, u32[]{:S(2)}, u32[]{:S(2)}) collective-permute-start(bf16[2,64,1792]{2,1,0:T(8,128)(2,1)S(1)} %slopes.1.refs_5_.refs_0_), channel_id=1, source_target_pairs={{0,4},{4,0},{8,12},{12,8},{1,5},{5,1},{9,13},{13,9},{2,6},{6,2},{1... | collective-permute-start | bytes 1376264 | tf_op jit(solution)/shard_map/ppermute | solution.py:20
  70.9 7.9 %collective-permute-start.21 = (bf16[128,2048]{1,0:T(8,128)(2,1)S(1)}, bf16[128,2048]{1,0:T(8,128)(2,1)S(1)}, u32[]{:S(2)}, u32[]{:S(2)}) collective-permute-start(bf16[128,2048]{1,0:T(8,128)(2,1)S(1)} %get-tuple-element.41), channel_id=1, source_target_pairs={{0,16},{16,0},{1,17},{17,1},{2,18},{18,2},{3,19},{19,3},{4,20},{20... | collective-permute-start | bytes 1572872 | tf_op jit(solution)/shard_map/ppermute | solution.py:20
  75.9 7.5 %collective-permute-start.28 = (bf16[2,32,1792]{2,1,0:T(8,128)(2,1)S(1)}, bf16[2,32,1792]{2,1,0:T(8,128)(2,1)S(1)}, u32[]{:S(2)}, u32[]{:S(2)}) collective-permute-start(bf16[2,32,1792]{2,1,0:T(8,128)(2,1)S(1)} %slice.9), channel_id=1, source_target_pairs={{0,4},{4,0},{8,12},{12,8},{1,5},{5,1},{9,13},{13,9},{2,6},{6,2},{1... | collective-permute-start | bytes 688136 | tf_op jit(solution)/shard_map/ppermute | solution.py:20
  77.2 6.1 %collective-permute-start.27 = (bf16[2,32,1792]{2,1,0:T(8,128)(2,1)S(1)}, bf16[2,32,1792]{2,1,0:T(8,128)(2,1)S(1)}, u32[]{:S(2)}, u32[]{:S(2)}) collective-permute-start(bf16[2,32,1792]{2,1,0:T(8,128)(2,1)S(1)} %slice.8), channel_id=1, source_target_pairs={{0,8},{4,12},{8,0},{12,4},{1,9},{5,13},{9,1},{13,5},{2,10},{6,14},... | collective-permute-start | bytes 688136 | tf_op jit(solution)/shard_map/ppermute | solution.py:20
  78.9 8.5 %collective-permute-start.22 = (bf16[32,2048]{1,0:T(8,128)(2,1)S(1)}, bf16[32,2048]{1,0:T(8,128)(2,1)S(1)}, u32[]{:S(2)}, u32[]{:S(2)}) collective-permute-start(bf16[32,2048]{1,0:T(8,128)(2,1)S(1)} %get-tuple-element.43), channel_id=1, source_target_pairs={{0,3},{1,2},{2,1},{3,0},{4,7},{5,6},{6,5},{7,4},{8,11},{9,10},{10,... | collective-permute-start | bytes 393224 | tf_op jit(solution)/shard_map/ppermute | solution.py:20
  80.3 10.4 %collective-permute-start.23 = (bf16[32,2048]{1,0:T(8,128)(2,1)S(1)}, bf16[32,2048]{1,0:T(8,128)(2,1)S(1)}, u32[]{:S(2)}, u32[]{:S(2)}) collective-permute-start(bf16[32,2048]{1,0:T(8,128)(2,1)S(1)} %get-tuple-element.44), channel_id=1, source_target_pairs={{0,2},{1,3},{2,0},{3,1},{4,6},{5,7},{6,4},{7,5},{8,10},{9,11},{10,... | collective-permute-start | bytes 393224 | tf_op jit(solution)/shard_map/ppermute | solution.py:20
  81.1 9.7 %collective-permute-start.24 = (bf16[32,2048]{1,0:T(8,128)(2,1)S(1)}, bf16[32,2048]{1,0:T(8,128)(2,1)S(1)}, u32[]{:S(2)}, u32[]{:S(2)}) collective-permute-start(bf16[32,2048]{1,0:T(8,128)(2,1)S(1)} %get-tuple-element.45), channel_id=1, source_target_pairs={{0,1},{1,0},{2,3},{3,2},{4,5},{5,4},{6,7},{7,6},{8,9},{9,8},{10,11... | collective-permute-start | bytes 393224 | tf_op jit(solution)/shard_map/ppermute | solution.py:20
  90.8 2.0 %collective-permute-start.29 = (bf16[128,2048]{1,0:T(8,128)(2,1)S(1)}, bf16[128,2048]{1,0:T(8,128)(2,1)S(1)}, u32[]{:S(2)}, u32[]{:S(2)}) collective-permute-start(bf16[128,2048]{1,0:T(8,128)(2,1)S(1)} %hold.1), channel_id=1, source_target_pairs={{0,16},{16,0},{1,17},{17,1},{2,18},{18,2},{3,19},{19,3},{4,20},{20... | collective-permute-start | bytes 1572872 | tf_op jit(solution)/shard_map/ppermute | solution.py:20
  92.8 8.3 %collective-permute-start.30 = (bf16[32,2048]{1,0:T(8,128)(2,1)S(1)}, bf16[32,2048]{1,0:T(8,128)(2,1)S(1)}, u32[]{:S(2)}, u32[]{:S(2)}) collective-permute-start(bf16[32,2048]{1,0:T(8,128)(2,1)S(1)} %get-tuple-element.49), channel_id=1, source_target_pairs={{0,3},{1,2},{2,1},{3,0},{4,7},{5,6},{6,5},{7,4},{8,11},{9,10},{10,... | collective-permute-start | bytes 393224 | tf_op jit(solution)/shard_map/ppermute | solution.py:20
  94.7 11.2 %collective-permute-start.31 = (bf16[32,2048]{1,0:T(8,128)(2,1)S(1)}, bf16[32,2048]{1,0:T(8,128)(2,1)S(1)}, u32[]{:S(2)}, u32[]{:S(2)}) collective-permute-start(bf16[32,2048]{1,0:T(8,128)(2,1)S(1)} %get-tuple-element.50), channel_id=1, source_target_pairs={{0,2},{1,3},{2,0},{3,1},{4,6},{5,7},{6,4},{7,5},{8,10},{9,11},{10,... | collective-permute-start | bytes 393224 | tf_op jit(solution)/shard_map/ppermute | solution.py:20
  94.7 11.2 %collective-permute-start.32 = (bf16[32,2048]{1,0:T(8,128)(2,1)S(1)}, bf16[32,2048]{1,0:T(8,128)(2,1)S(1)}, u32[]{:S(2)}, u32[]{:S(2)}) collective-permute-start(bf16[32,2048]{1,0:T(8,128)(2,1)S(1)} %get-tuple-element.51), channel_id=1, source_target_pairs={{0,1},{1,0},{2,3},{3,2},{4,5},{5,4},{6,7},{7,6},{8,9},{9,8},{10,11... | collective-permute-start | bytes 393224 | tf_op jit(solution)/shard_map/ppermute | solution.py:20
where the time goes:
time: 107 us
  waiting for transfers between devices  45.1 us (42%)
  starting transfers between devices  38.5 us (36%)
  Pallas kernels  20.7 us (19%)
  other arithmetic  1.43 us (1%)
    ppermute x33, waiting for transfers between devices, exchange(): return lax.ppermute(value, axis, [(i, i ^ step) for i in range(size)])  45.1 us
    ppermute x33, starting transfers between devices, exchange(): return lax.ppermute(value, axis, [(i, i ^ step) for i in range(size)])  38.5 us
    pallas_call x1, Pallas kernels, load_weights(): pl.pallas_call(kernel, in_specs=[IN_PLACE] * 3, out_specs=[IN_VMEM] * 2,...  7.56 us
    pallas_call x2, Pallas kernels, contract(): pl.pallas_call(kernel, in_specs=[IN_VMEM] * (n_in + 1) + [IN_PLACE] * n_a...  6.13 us
    pallas_call x2, Pallas kernels, project(): pl.pallas_call(kernel, in_specs=[IN_VMEM] * (n_in + 1) + [IN_PLACE] * n_a...  6.1 us
  transfers between devices with their start and end apart: 33, of which 16 were waited for; matrix products, arithmetic and copies ran while one was open for 1% of the time, Pallas kernels for 19%

commit v1 on v0

--- a/solution.py
+++ b/solution.py
@@ -386,7 +386,7 @@
     other_grads = exchange(backward_grad, "dp", cores, 1)
     acts = gather_tokens(acts, other_acts, cores, after=[tall, other_acts, grads[1]])
     keep, for_x, for_y = project(
-        acts, wide, False, balanced_layout, n_pipe, n_tensor, after=[other_grads]
+        acts, wide, False, balanced_layout, n_pipe, n_tensor
     )
     came_x, came_y = swap(for_x, x), swap(for_y, y)
     mine, other = small_kernel(
@@ -438,7 +438,7 @@
     def copy_body(ins, outs):
         outs[0][...] = ins[0][...]
 
-    (held,) = small_kernel(copy_body, [(back[1].shape, BF16)], back[1:], "hold", after=came)
+    (held,) = small_kernel(copy_body, [(back[1].shape, BF16)], back[1:], "hold", after=came[:1])
     _, input_grad = finish([back[0], held], cores, n_tensor)
     return layer_output, input_grad
 

time: 107 us -> 109 us (1.019)
  waiting for transfers between devices: 45.1 us -> 48.1 us
    ppermute x33, waiting for transfers between devices: 45.1 us -> 48.1 us  [exchange(): return lax.ppermute(value, axis, [(i, i ^ step) for i in range(size)])]
  transfers between devices with their start and end apart: 33 -> 33, of which waited for: 16 -> 17; matrix products, arithmetic and copies ran while one was open for 1% -> 1% of each run, Pallas kernels for 19% -> 19%
where the time goes in v1:
time: 109 us
  waiting for transfers between devices  48.1 us (44%)
  starting transfers between devices  38.1 us (35%)
  Pallas kernels  20.7 us (19%)
  other arithmetic  1.43 us (1%)
    ppermute x33, waiting for transfers between devices, exchange(): return lax.ppermute(value, axis, [(i, i ^ step) for i in range(size)])  48.1 us
    ppermute x33, starting transfers between devices, exchange(): return lax.ppermute(value, axis, [(i, i ^ step) for i in range(size)])  38.1 us
    pallas_call x1, Pallas kernels, load_weights(): pl.pallas_call(kernel, in_specs=[IN_PLACE] * 3, out_specs=[IN_VMEM] * 2,...  7.56 us
    pallas_call x2, Pallas kernels, contract(): pl.pallas_call(kernel, in_specs=[IN_VMEM] * (n_in + 1) + [IN_PLACE] * n_a...  6.13 us
    pallas_call x2, Pallas kernels, project(): pl.pallas_call(kernel, in_specs=[IN_VMEM] * (n_in + 1) + [IN_PLACE] * n_a...  6.11 us
  transfers between devices with their start and end apart: 33, of which 17 were waited for; matrix products, arithmetic and copies ran while one was open for 1% of the time, Pallas kernels for 19%

profile of v1, /device:TPU:0, one launch (start us, length us, event | category | flops | bytes accessed | tf_op | source)
XLA Modules:
  0.0 109.2 jit_solution(15658931258794489955)
XLA Ops:
  0.7 5.1 %collective-permute-start.2 = (bf16[32,2048]{1,0:T(8,128)(2,1)}, bf16[32,2048]{1,0:T(8,128)(2,1)S(1)}, u32[]{:S(2)}, u32[]{:S(2)}) collective-permute-start(bf16[32,2048]{1,0:T(8,128)(2,1)} %refs_0_.3), channel_id=1, source_target_pairs={{0,3},{1,2},{2,1},{3,0},{4,7},{5,6},{6,5},{7,4},{8,11},{9,10},{10,... | collective-permute-start | bytes 393224 | tf_op jit(solution)/shard_map/ppermute | solution.py:20
  5.8 0.6 collective-permute-start
  6.4 0.0 collective-permute-start.3
  6.4 1.4 %collective-permute-start.4 = (bf16[32,2048]{1,0:T(8,128)(2,1)}, bf16[32,2048]{1,0:T(8,128)(2,1)S(1)}, u32[]{:S(2)}, u32[]{:S(2)}) collective-permute-start(bf16[32,2048]{1,0:T(8,128)(2,1)} %refs_0_.5), channel_id=1, source_target_pairs={{0,1},{1,0},{2,3},{3,2},{4,5},{5,4},{6,7},{7,6},{8,9},{9,8},{10,11... | collective-permute-start | bytes 393224 | tf_op jit(solution)/shard_map/ppermute | solution.py:20
  7.8 7.6 %load_weights.1 = (bf16[2,2048,1792]{2,1,0:T(8,128)(2,1)S(1)}, bf16[1,1792,2048]{2,1,0:T(8,128)(2,1)S(1)}) custom-call(bf16[2048,3584]{1,0:T(8,128)(2,1)} %gate.1, bf16[2048,3584]{1,0:T(8,128)(2,1)} %up.1, bf16[3584,2048]{1,0:T(8,128)(2,1)} %down.1), custom_call_target="tpu_custom_call" | custom-call | bytes 22020096 | tf_op jit(solution)/shard_map/load_weights/pallas_call | solution.py:78
  15.4 0.0 copy-start
  15.4 0.0 copy-start.1
  15.4 0.0 collective-permute-done.2.refs_2_
  15.4 1.8 %collective-permute-done.1.refs_1_ = bf16[32,2048]{1,0:T(8,128)(2,1)S(1)} collective-permute-done((bf16[32,2048]{1,0:T(8,128)(2,1)}, bf16[32,2048]{1,0:T(8,128)(2,1)S(1)}, u32[]{:S(2)}, u32[]{:S(2)}) %collective-permute-start.1) | collective-permute-done | bytes 131104 | tf_op jit(solution)/shard_map/ppermute | solution.py:20
  17.2 0.0 collective-permute-done.refs_0_
  17.2 0.0 collective-permute-done.3.refs_4_.refs_2_
  17.2 0.8 collective-permute-done.4.refs_5_.refs_0_
  18.0 0.1 collective-permute-start.5
  18.1 3.4 %collective-permute-start.9 = (bf16[32,2048]{1,0:T(8,128)(2,1)S(1)}, bf16[32,2048]{1,0:T(8,128)(2,1)S(1)}, u32[]{:S(2)}, u32[]{:S(2)}) collective-permute-start(bf16[32,2048]{1,0:T(8,128)(2,1)S(1)} %copy-done.3), channel_id=1, source_target_pairs={{0,3},{1,2},{2,1},{3,0},{4,7},{5,6},{6,5},{7,4},{8,11},{9,10},{10,... | collective-permute-start | bytes 393224 | tf_op jit(solution)/shard_map/ppermute | solution.py:20
  21.6 4.0 %project.1 = (f32[2,128,1792]{2,1,0:T(8,128)S(1)}, bf16[2,64,1792]{2,1,0:T(8,128)(2,1)S(1)}, bf16[2,64,1792]{2,1,0:T(8,128)(2,1)S(1)}) custom-call(bf16[32,2048]{1,0:T(8,128)(2,1)S(1)} %copy-done.2, bf16[96,2048]{1,0:T(8,128)(2,1)S(1)} %assemble.2.refs_1_, bf16[32,2048]{1,0:T(8,128)(2,1)S(1)} %collective-permute-done.3.refs_4_.refs_2_, ...), custom_call_target="tpu_custom_call" | custom-call | flops 3758096384 | bytes 14680064 | tf_op jit(solution)/shard_map/project/pallas_call | solution.py:150
  25.6 1.6 %collective-permute-start.6 = (bf16[2,64,1792]{2,1,0:T(8,128)(2,1)S(1)}, bf16[2,64,1792]{2,1,0:T(8,128)(2,1)S(1)}, u32[]{:S(2)}, u32[]{:S(2)}) collective-permute-start(bf16[2,64,1792]{2,1,0:T(8,128)(2,1)S(1)} %get-tuple-element.30), channel_id=1, source_target_pairs={{0,4},{4,0},{8,12},{12,8},{1,5},{5,1},{9,13},{13,9},{2,6},{6,2},{1... | collective-permute-start | bytes 1376264 | tf_op jit(solution)/shard_map/ppermute | solution.py:20
  27.1 1.5 %collective-permute-start.7 = (bf16[2,64,1792]{2,1,0:T(8,128)(2,1)S(1)}, bf16[2,64,1792]{2,1,0:T(8,128)(2,1)S(1)}, u32[]{:S(2)}, u32[]{:S(2)}) collective-permute-start(bf16[2,64,1792]{2,1,0:T(8,128)(2,1)S(1)} %get-tuple-element.31), channel_id=1, source_target_pairs={{0,8},{4,12},{8,0},{12,4},{1,9},{5,13},{9,1},{13,5},{2,10},{6,14},... | collective-permute-start | bytes 1376264 | tf_op jit(solution)/shard_map/ppermute | solution.py:20
  28.6 4.9 %collective-permute-done.8.refs_1_ = bf16[32,2048]{1,0:T(8,128)(2,1)S(1)} collective-permute-done((bf16[32,2048]{1,0:T(8,128)(2,1)S(1)}, bf16[32,2048]{1,0:T(8,128)(2,1)S(1)}, u32[]{:S(2)}, u32[]{:S(2)}) %collective-permute-start.8) | collective-permute-done | bytes 131104 | tf_op jit(solution)/shard_map/ppermute | solution.py:20
  33.6 0.1 collective-permute-start.11
  33.8 0.5 collective-permute-start.12
  34.3 0.1 collective-permute-start.10
  34.4 1.5 %collective-permute-done.10.refs_2_ = bf16[32,2048]{1,0:T(8,128)(2,1)S(1)} collective-permute-done((bf16[32,2048]{1,0:T(8,128)(2,1)S(1)}, bf16[32,2048]{1,0:T(8,128)(2,1)S(1)}, u32[]{:S(2)}, u32[]{:S(2)}) %collective-permute-start.10) | collective-permute-done | bytes 131104 | tf_op jit(solution)/shard_map/ppermute | solution.py:20
  35.9 2.1 %pull_back.1 = (f32[1,64,1792]{2,1,0:T(8,128)S(1)}, bf16[1,64,1792]{2,1,0:T(8,128)(2,1)S(1)}, bf16[1,64,1792]{2,1,0:T(8,128)(2,1)S(1)}, bf16[1,64,1792]{2,1,0:T(8,128)(2,1)S(1)}) custom-call(bf16[32,2048]{1,0:T(8,128)(2,1)S(1)} %copy-done.3, bf16[96,2048]{1,0:T(8,128)(2,1)S(1)} %assemble.3.refs_1_, bf16[32,2048]{1,0:T(8,128)(2,1)S(1)} %collective-permute-done.10.refs_2_, ...), custom_call_target="tpu_custom_call" | custom-call | tf_op jit(solution)/shard_map/pull_back/pallas_call | solution.py:150
  38.0 0.2 collective-permute-done.6.refs_1_
  38.2 1.2 %collective-permute-done.7.refs_2_ = bf16[2,64,1792]{2,1,0:T(8,128)(2,1)S(1)} collective-permute-done((bf16[2,64,1792]{2,1,0:T(8,128)(2,1)S(1)}, bf16[2,64,1792]{2,1,0:T(8,128)(2,1)S(1)}, u32[]{:S(2)}, u32[]{:S(2)}) %collective-permute-start.7) | collective-permute-done | bytes 458784 | tf_op jit(solution)/shard_map/ppermute | solution.py:20
  39.4 0.1 pass_on.1
  39.5 0.6 collective-permute-start.13
  40.1 1.5 %collective-permute-start.14 = (bf16[2,32,1792]{2,1,0:T(8,128)(2,1)S(1)}, bf16[2,32,1792]{2,1,0:T(8,128)(2,1)S(1)}, u32[]{:S(2)}, u32[]{:S(2)}) collective-permute-start(bf16[2,32,1792]{2,1,0:T(8,128)(2,1)S(1)} %get-tuple-element.35), channel_id=1, source_target_pairs={{0,8},{4,12},{8,0},{12,4},{1,9},{5,13},{9,1},{13,5},{2,10},{6,14},... | collective-permute-start | bytes 688136 | tf_op jit(solution)/shard_map/ppermute | solution.py:20
  41.6 1.4 %collective-permute-start.18 = (bf16[1,64,1792]{2,1,0:T(8,128)(2,1)S(1)}, bf16[1,64,1792]{2,1,0:T(8,128)(2,1)S(1)}, u32[]{:S(2)}, u32[]{:S(2)}) collective-permute-start(bf16[1,64,1792]{2,1,0:T(8,128)(2,1)S(1)} %get-tuple-element.36), channel_id=1, source_target_pairs={{0,12},{4,8},{8,4},{12,0},{1,13},{5,9},{9,5},{13,1},{2,14},{6,10},... | collective-permute-start | bytes 688136 | tf_op jit(solution)/shard_map/ppermute | solution.py:20
  43.1 0.5 collective-permute-start.19
  43.6 1.5 %collective-permute-start.20 = (bf16[1,64,1792]{2,1,0:T(8,128)(2,1)S(1)}, bf16[1,64,1792]{2,1,0:T(8,128)(2,1)S(1)}, u32[]{:S(2)}, u32[]{:S(2)}) collective-permute-start(bf16[1,64,1792]{2,1,0:T(8,128)(2,1)S(1)} %get-tuple-element.38), channel_id=1, source_target_pairs={{0,8},{4,12},{8,0},{12,4},{1,9},{5,13},{9,1},{13,5},{2,10},{6,14},... | collective-permute-start | bytes 688136 | tf_op jit(solution)/shard_map/ppermute | solution.py:20
  45.1 3.0 %collective-permute-done.13.refs_3_ = bf16[2,32,1792]{2,1,0:T(8,128)(2,1)S(1)} collective-permute-done((bf16[2,32,1792]{2,1,0:T(8,128)(2,1)S(1)}, bf16[2,32,1792]{2,1,0:T(8,128)(2,1)S(1)}, u32[]{:S(2)}, u32[]{:S(2)}) %collective-permute-start.13) | collective-permute-done | bytes 229408 | tf_op jit(solution)/shard_map/ppermute | solution.py:20
  48.1 5.0 %collective-permute-done.14.refs_4_ = bf16[2,32,1792]{2,1,0:T(8,128)(2,1)S(1)} collective-permute-done((bf16[2,32,1792]{2,1,0:T(8,128)(2,1)S(1)}, bf16[2,32,1792]{2,1,0:T(8,128)(2,1)S(1)}, u32[]{:S(2)}, u32[]{:S(2)}) %collective-permute-start.14) | collective-permute-done | bytes 229408 | tf_op jit(solution)/shard_map/ppermute | solution.py:20
  53.1 0.2 hidden.1.refs_6_.refs_0_
  53.3 2.9 %collective-permute-start.17 = (bf16[1,64,1792]{2,1,0:T(8,128)(2,1)S(1)}, bf16[1,64,1792]{2,1,0:T(8,128)(2,1)S(1)}, u32[]{:S(2)}, u32[]{:S(2)}) collective-permute-start(bf16[1,64,1792]{2,1,0:T(8,128)(2,1)S(1)} %hidden.1.refs_6_.refs_0_), channel_id=1, source_target_pairs={{0,12},{4,8},{8,4},{12,0},{1,13},{5,9},{9,5},{13,1},{2,14},{6,10},... | collective-permute-start | bytes 688136 | tf_op jit(solution)/shard_map/ppermute | solution.py:20
  56.2 0.5 collective-permute-start.16
  56.7 0.1 collective-permute-start.15
  56.9 1.1 collective-permute-done.19.refs_2_
  57.9 5.0 %collective-permute-done.20.refs_3_ = bf16[1,64,1792]{2,1,0:T(8,128)(2,1)S(1)} collective-permute-done((bf16[1,64,1792]{2,1,0:T(8,128)(2,1)S(1)}, bf16[1,64,1792]{2,1,0:T(8,128)(2,1)S(1)}, u32[]{:S(2)}, u32[]{:S(2)}) %collective-permute-start.20) | collective-permute-done | bytes 229408 | tf_op jit(solution)/shard_map/ppermute | solution.py:20
  63.0 0.3 slopes.1.refs_5_.refs_0_
  63.3 2.0 %collective-permute-start.26 = (bf16[2,64,1792]{2,1,0:T(8,128)(2,1)S(1)}, bf16[2,64,1792]{2,1,0:T(8,128)(2,1)S(1)}, u32[]{:S(2)}, u32[]{:S(2)}) collective-permute-start(bf16[2,64,1792]{2,1,0:T(8,128)(2,1)S(1)} %slopes.1.refs_5_.refs_0_), channel_id=1, source_target_pairs={{0,8},{4,12},{8,0},{12,4},{1,9},{5,13},{9,1},{13,5},{2,10},{6,14},... | collective-permute-start | bytes 1376264 | tf_op jit(solution)/shard_map/ppermute | solution.py:20
  65.3 1.4 %collective-permute-start.25 = (bf16[2,64,1792]{2,1,0:T(8,128)(2,1)S(1)}, bf16[2,64,1792]{2,1,0:T(8,128)(2,1)S(1)}, u32[]{:S(2)}, u32[]{:S(2)}) collective-permute-start(bf16[2,64,1792]{2,1,0:T(8,128)(2,1)S(1)} %slopes.1.refs_5_.refs_0_), channel_id=1, source_target_pairs={{0,4},{4,0},{8,12},{12,8},{1,5},{5,1},{9,13},{13,9},{2,6},{6,2},{1... | collective-permute-start | bytes 1376264 | tf_op jit(solution)/shard_map/ppermute | solution.py:20
  66.7 1.6 %collective-permute-done.16.refs_2_ = bf16[1,64,1792]{2,1,0:T(8,128)(2,1)S(1)} collective-permute-done((bf16[1,64,1792]{2,1,0:T(8,128)(2,1)S(1)}, bf16[1,64,1792]{2,1,0:T(8,128)(2,1)S(1)}, u32[]{:S(2)}, u32[]{:S(2)}) %collective-permute-start.16) | collective-permute-done | bytes 229408 | tf_op jit(solution)/shard_map/ppermute | solution.py:20
  68.3 2.1 %layer_output.1 = (f32[128,2048]{1,0:T(8,128)S(1)}, bf16[128,2048]{1,0:T(8,128)(2,1)S(1)}) custom-call(bf16[1,64,1792]{2,1,0:T(8,128)(2,1)S(1)} %hidden.1.refs_6_.refs_0_, bf16[1,64,1792]{2,1,0:T(8,128)(2,1)S(1)} %collective-permute-done.15.refs_1_, bf16[1,64,1792]{2,1,0:T(8,128)(2,1)S(1)} %collective-permute-done.16.refs_2_, ...), custom_call_target="tpu_custom_call" | custom-call | flops 1879048192 | bytes 7340032 | tf_op jit(solution)/shard_map/layer_output/pallas_call | solution.py:224
  70.4 0.1 collective-permute-start.21
  70.5 6.1 %collective-permute-done.26.refs_2_ = bf16[2,64,1792]{2,1,0:T(8,128)(2,1)S(1)} collective-permute-done((bf16[2,64,1792]{2,1,0:T(8,128)(2,1)S(1)}, bf16[2,64,1792]{2,1,0:T(8,128)(2,1)S(1)}, u32[]{:S(2)}, u32[]{:S(2)}) %collective-permute-start.26) | collective-permute-done | bytes 458784 | tf_op jit(solution)/shard_map/ppermute | solution.py:20
  76.6 0.8 collective-permute-start.28
  77.4 1.6 %collective-permute-start.27 = (bf16[2,32,1792]{2,1,0:T(8,128)(2,1)S(1)}, bf16[2,32,1792]{2,1,0:T(8,128)(2,1)S(1)}, u32[]{:S(2)}, u32[]{:S(2)}) collective-permute-start(bf16[2,32,1792]{2,1,0:T(8,128)(2,1)S(1)} %slice.8), channel_id=1, source_target_pairs={{0,8},{4,12},{8,0},{12,4},{1,9},{5,13},{9,1},{13,5},{2,10},{6,14},... | collective-permute-start | bytes 688136 | tf_op jit(solution)/shard_map/ppermute | solution.py:20
  79.0 0.1 add_core.2
  79.1 1.6 %collective-permute-start.22 = (bf16[32,2048]{1,0:T(8,128)(2,1)S(1)}, bf16[32,2048]{1,0:T(8,128)(2,1)S(1)}, u32[]{:S(2)}, u32[]{:S(2)}) collective-permute-start(bf16[32,2048]{1,0:T(8,128)(2,1)S(1)} %get-tuple-element.43), channel_id=1, source_target_pairs={{0,3},{1,2},{2,1},{3,0},{4,7},{5,6},{6,5},{7,4},{8,11},{9,10},{10,... | collective-permute-start | bytes 393224 | tf_op jit(solution)/shard_map/ppermute | solution.py:20
  80.8 1.9 %collective-permute-done.28.refs_4_ = bf16[2,32,1792]{2,1,0:T(8,128)(2,1)S(1)} collective-permute-done((bf16[2,32,1792]{2,1,0:T(8,128)(2,1)S(1)}, bf16[2,32,1792]{2,1,0:T(8,128)(2,1)S(1)}, u32[]{:S(2)}, u32[]{:S(2)}) %collective-permute-start.28) | collective-permute-done | bytes 229408 | tf_op jit(solution)/shard_map/ppermute | solution.py:20
  82.7 0.9 collective-permute-done.27.refs_3_
  83.5 4.0 %input_grad.1 = (f32[128,2048]{1,0:T(8,128)S(1)}, bf16[128,2048]{1,0:T(8,128)(2,1)S(1)}) custom-call(bf16[2,64,1792]{2,1,0:T(8,128)(2,1)S(1)} %slopes.1.refs_5_.refs_0_, bf16[2,64,1792]{2,1,0:T(8,128)(2,1)S(1)} %collective-permute-done.25.refs_1_, bf16[2,64,1792]{2,1,0:T(8,128)(2,1)S(1)} %collective-permute-done.26.refs_2_, ...), custom_call_target="tpu_custom_call" | custom-call | flops 3758096384 | bytes 14680064 | tf_op jit(solution)/shard_map/input_grad/pallas_call | solution.py:224
  87.6 0.1 collective-permute-start.29
  87.7 2.4 %collective-permute-start.23 = (bf16[32,2048]{1,0:T(8,128)(2,1)S(1)}, bf16[32,2048]{1,0:T(8,128)(2,1)S(1)}, u32[]{:S(2)}, u32[]{:S(2)}) collective-permute-start(bf16[32,2048]{1,0:T(8,128)(2,1)S(1)} %get-tuple-element.44), channel_id=1, source_target_pairs={{0,2},{1,3},{2,0},{3,1},{4,6},{5,7},{6,4},{7,5},{8,10},{9,11},{10,... | collective-permute-start | bytes 393224 | tf_op jit(solution)/shard_map/ppermute | solution.py:20
  90.1 0.1 add_core.3
  90.2 2.1 %collective-permute-start.30 = (bf16[32,2048]{1,0:T(8,128)(2,1)S(1)}, bf16[32,2048]{1,0:T(8,128)(2,1)S(1)}, u32[]{:S(2)}, u32[]{:S(2)}) collective-permute-start(bf16[32,2048]{1,0:T(8,128)(2,1)S(1)} %get-tuple-element.49), channel_id=1, source_target_pairs={{0,3},{1,2},{2,1},{3,0},{4,7},{5,6},{6,5},{7,4},{8,11},{9,10},{10,... | collective-permute-start | bytes 393224 | tf_op jit(solution)/shard_map/ppermute | solution.py:20
  92.3 1.5 %collective-permute-start.31 = (bf16[32,2048]{1,0:T(8,128)(2,1)S(1)}, bf16[32,2048]{1,0:T(8,128)(2,1)S(1)}, u32[]{:S(2)}, u32[]{:S(2)}) collective-permute-start(bf16[32,2048]{1,0:T(8,128)(2,1)S(1)} %get-tuple-element.50), channel_id=1, source_target_pairs={{0,2},{1,3},{2,0},{3,1},{4,6},{5,7},{6,4},{7,5},{8,10},{9,11},{10,... | collective-permute-start | bytes 393224 | tf_op jit(solution)/shard_map/ppermute | solution.py:20
  93.8 0.9 collective-permute-start.32
  94.7 3.1 %collective-permute-done.23 = bf16[32,2048]{1,0:T(8,128)(2,1)S(1)} collective-permute-done((bf16[32,2048]{1,0:T(8,128)(2,1)S(1)}, bf16[32,2048]{1,0:T(8,128)(2,1)S(1)}, u32[]{:S(2)}, u32[]{:S(2)}) %collective-permute-start.23) | collective-permute-done | bytes 131104 | tf_op jit(solution)/shard_map/ppermute | solution.py:20
  97.8 4.2 %collective-permute-done.24 = bf16[32,2048]{1,0:T(8,128)(2,1)S(1)} collective-permute-done((bf16[32,2048]{1,0:T(8,128)(2,1)S(1)}, bf16[32,2048]{1,0:T(8,128)(2,1)S(1)}, u32[]{:S(2)}, u32[]{:S(2)}) %collective-permute-start.24) | collective-permute-done | bytes 131104 | tf_op jit(solution)/shard_map/ppermute | solution.py:20
  102.0 0.7 add_convert_fusion.1
  102.7 5.8 %collective-permute-done.31 = bf16[32,2048]{1,0:T(8,128)(2,1)S(1)} collective-permute-done((bf16[32,2048]{1,0:T(8,128)(2,1)S(1)}, bf16[32,2048]{1,0:T(8,128)(2,1)S(1)}, u32[]{:S(2)}, u32[]{:S(2)}) %collective-permute-start.31) | collective-permute-done | bytes 131104 | tf_op jit(solution)/shard_map/ppermute | solution.py:20
  108.5 0.7 add_convert_fusion
  (28 shorter events, 0.2 us)
Async XLA Ops:
  0.6 20.9 %copy-start.2 = (bf16[32,2048]{1,0:T(8,128)(2,1)S(1)}, bf16[32,2048]{1,0:T(8,128)(2,1)}, u32[]{:S(2)}) copy-start(bf16[32,2048]{1,0:T(8,128)(2,1)} %refs_0_.3) | copy-start | bytes 393220
  0.6 17.5 %copy-start.3 = (bf16[32,2048]{1,0:T(8,128)(2,1)S(1)}, bf16[32,2048]{1,0:T(8,128)(2,1)}, u32[]{:S(2)}) copy-start(bf16[32,2048]{1,0:T(8,128)(2,1)} %refs_0_.5) | copy-start | bytes 393220
  0.7 14.7 %collective-permute-start.2 = (bf16[32,2048]{1,0:T(8,128)(2,1)}, bf16[32,2048]{1,0:T(8,128)(2,1)S(1)}, u32[]{:S(2)}, u32[]{:S(2)}) collective-permute-start(bf16[32,2048]{1,0:T(8,128)(2,1)} %refs_0_.3), channel_id=1, source_target_pairs={{0,3},{1,2},{2,1},{3,0},{4,7},{5,6},{6,5},{7,4},{8,11},{9,10},{10,... | collective-permute-start | bytes 393224 | tf_op jit(solution)/shard_map/ppermute | solution.py:20
  5.8 11.4 %collective-permute-start.1 = (bf16[32,2048]{1,0:T(8,128)(2,1)}, bf16[32,2048]{1,0:T(8,128)(2,1)S(1)}, u32[]{:S(2)}, u32[]{:S(2)}) collective-permute-start(bf16[32,2048]{1,0:T(8,128)(2,1)} %refs_0_.3), channel_id=1, source_target_pairs={{0,2},{1,3},{2,0},{3,1},{4,6},{5,7},{6,4},{7,5},{8,10},{9,11},{10,... | collective-permute-start | bytes 393224 | tf_op jit(solution)/shard_map/ppermute | solution.py:20
  5.8 11.4 %collective-permute-start = (bf16[32,2048]{1,0:T(8,128)(2,1)}, bf16[32,2048]{1,0:T(8,128)(2,1)S(1)}, u32[]{:S(2)}, u32[]{:S(2)}) collective-permute-start(bf16[32,2048]{1,0:T(8,128)(2,1)} %refs_0_.3), channel_id=1, source_target_pairs={{0,1},{1,0},{2,3},{3,2},{4,5},{5,4},{6,7},{7,6},{8,9},{9,8},{10,11... | collective-permute-start | bytes 393224 | tf_op jit(solution)/shard_map/ppermute | solution.py:20
  6.4 10.8 %collective-permute-start.3 = (bf16[32,2048]{1,0:T(8,128)(2,1)}, bf16[32,2048]{1,0:T(8,128)(2,1)S(1)}, u32[]{:S(2)}, u32[]{:S(2)}) collective-permute-start(bf16[32,2048]{1,0:T(8,128)(2,1)} %refs_0_.3), channel_id=1, source_target_pairs={{0,16},{16,0},{1,17},{17,1},{2,18},{18,2},{3,19},{19,3},{4,20},{20... | collective-permute-start | bytes 393224 | tf_op jit(solution)/shard_map/ppermute | solution.py:20
  6.4 11.6 %collective-permute-start.4 = (bf16[32,2048]{1,0:T(8,128)(2,1)}, bf16[32,2048]{1,0:T(8,128)(2,1)S(1)}, u32[]{:S(2)}, u32[]{:S(2)}) collective-permute-start(bf16[32,2048]{1,0:T(8,128)(2,1)} %refs_0_.5), channel_id=1, source_target_pairs={{0,1},{1,0},{2,3},{3,2},{4,5},{5,4},{6,7},{7,6},{8,9},{9,8},{10,11... | collective-permute-start | bytes 393224 | tf_op jit(solution)/shard_map/ppermute | solution.py:20
  15.4 18.3 %copy-start = (bf16[32,3584]{1,0:T(8,128)(2,1)S(1)}, bf16[32,3584]{1,0:T(8,128)(2,1)}, u32[]{:S(2)}) copy-start(bf16[32,3584]{1,0:T(8,128)(2,1)} %refs_0_.4) | copy-start | bytes 688132
  15.4 18.3 %copy-start.1 = (bf16[32,3584]{1,0:T(8,128)(2,1)S(1)}, bf16[32,3584]{1,0:T(8,128)(2,1)}, u32[]{:S(2)}) copy-start(bf16[32,3584]{1,0:T(8,128)(2,1)} %refs_1_.1) | copy-start | bytes 688132
  18.0 3.5 %collective-permute-start.5 = (bf16[96,2048]{1,0:T(8,128)(2,1)S(1)}, bf16[96,2048]{1,0:T(8,128)(2,1)S(1)}, u32[]{:S(2)}, u32[]{:S(2)}) collective-permute-start(bf16[96,2048]{1,0:T(8,128)(2,1)S(1)} %assemble.2.refs_1_), channel_id=1, source_target_pairs={{0,16},{16,0},{1,17},{17,1},{2,18},{18,2},{3,19},{19,3},{4,20},{20... | collective-permute-start | bytes 1179656 | tf_op jit(solution)/shard_map/ppermute | solution.py:20
  18.1 10.5 %collective-permute-start.9 = (bf16[32,2048]{1,0:T(8,128)(2,1)S(1)}, bf16[32,2048]{1,0:T(8,128)(2,1)S(1)}, u32[]{:S(2)}, u32[]{:S(2)}) collective-permute-start(bf16[32,2048]{1,0:T(8,128)(2,1)S(1)} %copy-done.3), channel_id=1, source_target_pairs={{0,3},{1,2},{2,1},{3,0},{4,7},{5,6},{6,5},{7,4},{8,11},{9,10},{10,... | collective-permute-start | bytes 393224 | tf_op jit(solution)/shard_map/ppermute | solution.py:20
  21.5 12.0 %collective-permute-start.8 = (bf16[32,2048]{1,0:T(8,128)(2,1)S(1)}, bf16[32,2048]{1,0:T(8,128)(2,1)S(1)}, u32[]{:S(2)}, u32[]{:S(2)}) collective-permute-start(bf16[32,2048]{1,0:T(8,128)(2,1)S(1)} %copy-done.3), channel_id=1, source_target_pairs={{0,2},{1,3},{2,0},{3,1},{4,6},{5,7},{6,4},{7,5},{8,10},{9,11},{10,... | collective-permute-start | bytes 393224 | tf_op jit(solution)/shard_map/ppermute | solution.py:20
  25.6 12.6 %collective-permute-start.6 = (bf16[2,64,1792]{2,1,0:T(8,128)(2,1)S(1)}, bf16[2,64,1792]{2,1,0:T(8,128)(2,1)S(1)}, u32[]{:S(2)}, u32[]{:S(2)}) collective-permute-start(bf16[2,64,1792]{2,1,0:T(8,128)(2,1)S(1)} %get-tuple-element.30), channel_id=1, source_target_pairs={{0,4},{4,0},{8,12},{12,8},{1,5},{5,1},{9,13},{13,9},{2,6},{6,2},{1... | collective-permute-start | bytes 1376264 | tf_op jit(solution)/shard_map/ppermute | solution.py:20
  27.1 12.3 %collective-permute-start.7 = (bf16[2,64,1792]{2,1,0:T(8,128)(2,1)S(1)}, bf16[2,64,1792]{2,1,0:T(8,128)(2,1)S(1)}, u32[]{:S(2)}, u32[]{:S(2)}) collective-permute-start(bf16[2,64,1792]{2,1,0:T(8,128)(2,1)S(1)} %get-tuple-element.31), channel_id=1, source_target_pairs={{0,8},{4,12},{8,0},{12,4},{1,9},{5,13},{9,1},{13,5},{2,10},{6,14},... | collective-permute-start | bytes 1376264 | tf_op jit(solution)/shard_map/ppermute | solution.py:20
  33.6 2.3 %collective-permute-start.11 = (bf16[96,2048]{1,0:T(8,128)(2,1)S(1)}, bf16[96,2048]{1,0:T(8,128)(2,1)S(1)}, u32[]{:S(2)}, u32[]{:S(2)}) collective-permute-start(bf16[96,2048]{1,0:T(8,128)(2,1)S(1)} %assemble.3.refs_1_), channel_id=1, source_target_pairs={{0,16},{16,0},{1,17},{17,1},{2,18},{18,2},{3,19},{19,3},{4,20},{20... | collective-permute-start | bytes 1179656 | tf_op jit(solution)/shard_map/ppermute | solution.py:20
  33.8 2.2 %collective-permute-start.12 = (bf16[2,32,1792]{2,1,0:T(8,128)(2,1)S(1)}, bf16[2,32,1792]{2,1,0:T(8,128)(2,1)S(1)}, u32[]{:S(2)}, u32[]{:S(2)}) collective-permute-start(bf16[2,32,1792]{2,1,0:T(8,128)(2,1)S(1)} %get-tuple-element.32), channel_id=1, source_target_pairs={{0,16},{16,0},{1,17},{17,1},{2,18},{18,2},{3,19},{19,3},{4,20},{20... | collective-permute-start | bytes 688136 | tf_op jit(solution)/shard_map/ppermute | solution.py:20
  34.3 1.6 %collective-permute-start.10 = (bf16[32,2048]{1,0:T(8,128)(2,1)S(1)}, bf16[32,2048]{1,0:T(8,128)(2,1)S(1)}, u32[]{:S(2)}, u32[]{:S(2)}) collective-permute-start(bf16[32,2048]{1,0:T(8,128)(2,1)S(1)} %copy-done.3), channel_id=1, source_target_pairs={{0,16},{16,0},{1,17},{17,1},{2,18},{18,2},{3,19},{19,3},{4,20},{20... | collective-permute-start | bytes 393224 | tf_op jit(solution)/shard_map/ppermute | solution.py:20
  39.5 8.6 %collective-permute-start.13 = (bf16[2,32,1792]{2,1,0:T(8,128)(2,1)S(1)}, bf16[2,32,1792]{2,1,0:T(8,128)(2,1)S(1)}, u32[]{:S(2)}, u32[]{:S(2)}) collective-permute-start(bf16[2,32,1792]{2,1,0:T(8,128)(2,1)S(1)} %get-tuple-element.34), channel_id=1, source_target_pairs={{0,4},{4,0},{8,12},{12,8},{1,5},{5,1},{9,13},{13,9},{2,6},{6,2},{1... | collective-permute-start | bytes 688136 | tf_op jit(solution)/shard_map/ppermute | solution.py:20
  40.1 13.0 %collective-permute-start.14 = (bf16[2,32,1792]{2,1,0:T(8,128)(2,1)S(1)}, bf16[2,32,1792]{2,1,0:T(8,128)(2,1)S(1)}, u32[]{:S(2)}, u32[]{:S(2)}) collective-permute-start(bf16[2,32,1792]{2,1,0:T(8,128)(2,1)S(1)} %get-tuple-element.35), channel_id=1, source_target_pairs={{0,8},{4,12},{8,0},{12,4},{1,9},{5,13},{9,1},{13,5},{2,10},{6,14},... | collective-permute-start | bytes 688136 | tf_op jit(solution)/shard_map/ppermute | solution.py:20
  41.6 15.1 %collective-permute-start.18 = (bf16[1,64,1792]{2,1,0:T(8,128)(2,1)S(1)}, bf16[1,64,1792]{2,1,0:T(8,128)(2,1)S(1)}, u32[]{:S(2)}, u32[]{:S(2)}) collective-permute-start(bf16[1,64,1792]{2,1,0:T(8,128)(2,1)S(1)} %get-tuple-element.36), channel_id=1, source_target_pairs={{0,12},{4,8},{8,4},{12,0},{1,13},{5,9},{9,5},{13,1},{2,14},{6,10},... | collective-permute-start | bytes 688136 | tf_op jit(solution)/shard_map/ppermute | solution.py:20
  43.1 14.9 %collective-permute-start.19 = (bf16[1,64,1792]{2,1,0:T(8,128)(2,1)S(1)}, bf16[1,64,1792]{2,1,0:T(8,128)(2,1)S(1)}, u32[]{:S(2)}, u32[]{:S(2)}) collective-permute-start(bf16[1,64,1792]{2,1,0:T(8,128)(2,1)S(1)} %get-tuple-element.37), channel_id=1, source_target_pairs={{0,4},{4,0},{8,12},{12,8},{1,5},{5,1},{9,13},{13,9},{2,6},{6,2},{1... | collective-permute-start | bytes 688136 | tf_op jit(solution)/shard_map/ppermute | solution.py:20
  43.6 19.4 %collective-permute-start.20 = (bf16[1,64,1792]{2,1,0:T(8,128)(2,1)S(1)}, bf16[1,64,1792]{2,1,0:T(8,128)(2,1)S(1)}, u32[]{:S(2)}, u32[]{:S(2)}) collective-permute-start(bf16[1,64,1792]{2,1,0:T(8,128)(2,1)S(1)} %get-tuple-element.38), channel_id=1, source_target_pairs={{0,8},{4,12},{8,0},{12,4},{1,9},{5,13},{9,1},{13,5},{2,10},{6,14},... | collective-permute-start | bytes 688136 | tf_op jit(solution)/shard_map/ppermute | solution.py:20
  53.3 13.4 %collective-permute-start.17 = (bf16[1,64,1792]{2,1,0:T(8,128)(2,1)S(1)}, bf16[1,64,1792]{2,1,0:T(8,128)(2,1)S(1)}, u32[]{:S(2)}, u32[]{:S(2)}) collective-permute-start(bf16[1,64,1792]{2,1,0:T(8,128)(2,1)S(1)} %hidden.1.refs_6_.refs_0_), channel_id=1, source_target_pairs={{0,12},{4,8},{8,4},{12,0},{1,13},{5,9},{9,5},{13,1},{2,14},{6,10},... | collective-permute-start | bytes 688136 | tf_op jit(solution)/shard_map/ppermute | solution.py:20
  56.2 12.1 %collective-permute-start.16 = (bf16[1,64,1792]{2,1,0:T(8,128)(2,1)S(1)}, bf16[1,64,1792]{2,1,0:T(8,128)(2,1)S(1)}, u32[]{:S(2)}, u32[]{:S(2)}) collective-permute-start(bf16[1,64,1792]{2,1,0:T(8,128)(2,1)S(1)} %hidden.1.refs_6_.refs_0_), channel_id=1, source_target_pairs={{0,8},{4,12},{8,0},{12,4},{1,9},{5,13},{9,1},{13,5},{2,10},{6,14},... | collective-permute-start | bytes 688136 | tf_op jit(solution)/shard_map/ppermute | solution.py:20
  56.7 11.6 %collective-permute-start.15 = (bf16[1,64,1792]{2,1,0:T(8,128)(2,1)S(1)}, bf16[1,64,1792]{2,1,0:T(8,128)(2,1)S(1)}, u32[]{:S(2)}, u32[]{:S(2)}) collective-permute-start(bf16[1,64,1792]{2,1,0:T(8,128)(2,1)S(1)} %hidden.1.refs_6_.refs_0_), channel_id=1, source_target_pairs={{0,4},{4,0},{8,12},{12,8},{1,5},{5,1},{9,13},{13,9},{2,6},{6,2},{1... | collective-permute-start | bytes 688136 | tf_op jit(solution)/shard_map/ppermute | solution.py:20
  63.3 13.3 %collective-permute-start.26 = (bf16[2,64,1792]{2,1,0:T(8,128)(2,1)S(1)}, bf16[2,64,1792]{2,1,0:T(8,128)(2,1)S(1)}, u32[]{:S(2)}, u32[]{:S(2)}) collective-permute-start(bf16[2,64,1792]{2,1,0:T(8,128)(2,1)S(1)} %slopes.1.refs_5_.refs_0_), channel_id=1, source_target_pairs={{0,8},{4,12},{8,0},{12,4},{1,9},{5,13},{9,1},{13,5},{2,10},{6,14},... | collective-permute-start | bytes 1376264 | tf_op jit(solution)/shard_map/ppermute | solution.py:20
  65.3 12.1 %collective-permute-start.25 = (bf16[2,64,1792]{2,1,0:T(8,128)(2,1)S(1)}, bf16[2,64,1792]{2,1,0:T(8,128)(2,1)S(1)}, u32[]{:S(2)}, u32[]{:S(2)}) collective-permute-start(bf16[2,64,1792]{2,1,0:T(8,128)(2,1)S(1)} %slopes.1.refs_5_.refs_0_), channel_id=1, source_target_pairs={{0,4},{4,0},{8,12},{12,8},{1,5},{5,1},{9,13},{13,9},{2,6},{6,2},{1... | collective-permute-start | bytes 1376264 | tf_op jit(solution)/shard_map/ppermute | solution.py:20
  70.4 8.6 %collective-permute-start.21 = (bf16[128,2048]{1,0:T(8,128)(2,1)S(1)}, bf16[128,2048]{1,0:T(8,128)(2,1)S(1)}, u32[]{:S(2)}, u32[]{:S(2)}) collective-permute-start(bf16[128,2048]{1,0:T(8,128)(2,1)S(1)} %get-tuple-element.41), channel_id=1, source_target_pairs={{0,16},{16,0},{1,17},{17,1},{2,18},{18,2},{3,19},{19,3},{4,20},{20... | collective-permute-start | bytes 1572872 | tf_op jit(solution)/shard_map/ppermute | solution.py:20
  76.6 6.1 %collective-permute-start.28 = (bf16[2,32,1792]{2,1,0:T(8,128)(2,1)S(1)}, bf16[2,32,1792]{2,1,0:T(8,128)(2,1)S(1)}, u32[]{:S(2)}, u32[]{:S(2)}) collective-permute-start(bf16[2,32,1792]{2,1,0:T(8,128)(2,1)S(1)} %slice.9), channel_id=1, source_target_pairs={{0,4},{4,0},{8,12},{12,8},{1,5},{5,1},{9,13},{13,9},{2,6},{6,2},{1... | collective-permute-start | bytes 688136 | tf_op jit(solution)/shard_map/ppermute | solution.py:20
  77.4 6.1 %collective-permute-start.27 = (bf16[2,32,1792]{2,1,0:T(8,128)(2,1)S(1)}, bf16[2,32,1792]{2,1,0:T(8,128)(2,1)S(1)}, u32[]{:S(2)}, u32[]{:S(2)}) collective-permute-start(bf16[2,32,1792]{2,1,0:T(8,128)(2,1)S(1)} %slice.8), channel_id=1, source_target_pairs={{0,8},{4,12},{8,0},{12,4},{1,9},{5,13},{9,1},{13,5},{2,10},{6,14},... | collective-permute-start | bytes 688136 | tf_op jit(solution)/shard_map/ppermute | solution.py:20
  79.1 8.5 %collective-permute-start.22 = (bf16[32,2048]{1,0:T(8,128)(2,1)S(1)}, bf16[32,2048]{1,0:T(8,128)(2,1)S(1)}, u32[]{:S(2)}, u32[]{:S(2)}) collective-permute-start(bf16[32,2048]{1,0:T(8,128)(2,1)S(1)} %get-tuple-element.43), channel_id=1, source_target_pairs={{0,3},{1,2},{2,1},{3,0},{4,7},{5,6},{6,5},{7,4},{8,11},{9,10},{10,... | collective-permute-start | bytes 393224 | tf_op jit(solution)/shard_map/ppermute | solution.py:20
  87.6 2.5 %collective-permute-start.29 = (bf16[128,2048]{1,0:T(8,128)(2,1)S(1)}, bf16[128,2048]{1,0:T(8,128)(2,1)S(1)}, u32[]{:S(2)}, u32[]{:S(2)}) collective-permute-start(bf16[128,2048]{1,0:T(8,128)(2,1)S(1)} %hold.1), channel_id=1, source_target_pairs={{0,16},{16,0},{1,17},{17,1},{2,18},{18,2},{3,19},{19,3},{4,20},{20... | collective-permute-start | bytes 1572872 | tf_op jit(solution)/shard_map/ppermute | solution.py:20
  87.7 10.1 %collective-permute-start.23 = (bf16[32,2048]{1,0:T(8,128)(2,1)S(1)}, bf16[32,2048]{1,0:T(8,128)(2,1)S(1)}, u32[]{:S(2)}, u32[]{:S(2)}) collective-permute-start(bf16[32,2048]{1,0:T(8,128)(2,1)S(1)} %get-tuple-element.44), channel_id=1, source_target_pairs={{0,2},{1,3},{2,0},{3,1},{4,6},{5,7},{6,4},{7,5},{8,10},{9,11},{10,... | collective-permute-start | bytes 393224 | tf_op jit(solution)/shard_map/ppermute | solution.py:20
  90.1 11.9 %collective-permute-start.24 = (bf16[32,2048]{1,0:T(8,128)(2,1)S(1)}, bf16[32,2048]{1,0:T(8,128)(2,1)S(1)}, u32[]{:S(2)}, u32[]{:S(2)}) collective-permute-start(bf16[32,2048]{1,0:T(8,128)(2,1)S(1)} %get-tuple-element.45), channel_id=1, source_target_pairs={{0,1},{1,0},{2,3},{3,2},{4,5},{5,4},{6,7},{7,6},{8,9},{9,8},{10,11... | collective-permute-start | bytes 393224 | tf_op jit(solution)/shard_map/ppermute | solution.py:20
  90.2 12.5 %collective-permute-start.30 = (bf16[32,2048]{1,0:T(8,128)(2,1)S(1)}, bf16[32,2048]{1,0:T(8,128)(2,1)S(1)}, u32[]{:S(2)}, u32[]{:S(2)}) collective-permute-start(bf16[32,2048]{1,0:T(8,128)(2,1)S(1)} %get-tuple-element.49), channel_id=1, source_target_pairs={{0,3},{1,2},{2,1},{3,0},{4,7},{5,6},{6,5},{7,4},{8,11},{9,10},{10,... | collective-permute-start | bytes 393224 | tf_op jit(solution)/shard_map/ppermute | solution.py:20
  92.3 16.2 %collective-permute-start.31 = (bf16[32,2048]{1,0:T(8,128)(2,1)S(1)}, bf16[32,2048]{1,0:T(8,128)(2,1)S(1)}, u32[]{:S(2)}, u32[]{:S(2)}) collective-permute-start(bf16[32,2048]{1,0:T(8,128)(2,1)S(1)} %get-tuple-element.50), channel_id=1, source_target_pairs={{0,2},{1,3},{2,0},{3,1},{4,6},{5,7},{6,4},{7,5},{8,10},{9,11},{10,... | collective-permute-start | bytes 393224 | tf_op jit(solution)/shard_map/ppermute | solution.py:20
  93.8 14.7 %collective-permute-start.32 = (bf16[32,2048]{1,0:T(8,128)(2,1)S(1)}, bf16[32,2048]{1,0:T(8,128)(2,1)S(1)}, u32[]{:S(2)}, u32[]{:S(2)}) collective-permute-start(bf16[32,2048]{1,0:T(8,128)(2,1)S(1)} %get-tuple-element.51), channel_id=1, source_target_pairs={{0,1},{1,0},{2,3},{3,2},{4,5},{5,4},{6,7},{7,6},{8,9},{9,8},{10,11... | collective-permute-start | bytes 393224 | tf_op jit(solution)/shard_map/ppermute | solution.py:20

commit v2 on v1

--- a/solution.py
+++ b/solution.py
@@ -233,7 +233,7 @@
             pltpu.VMEM((kinds, cores * tokens, units), BF16),
         ],
         compiler_params=params(),
-        cost_estimate=cost(2 * cores * tokens * units * width * kinds, 2 * units * width * kinds),
+        cost_estimate=cost(0, 0) if transposed else cost(2 * cores * tokens * units * width * kinds, 2 * units * width * kinds),
         name="input_grad" if transposed else "layer_output",
     )(*blocks, weights, *after)
 
@@ -379,67 +379,63 @@
                 start = pl.multiple_of((core ^ c) * units, units)
                 outs[c][k] = ins[k][:, pl.ds(start, units)]
 
+    grads = gather_first(backward_grad, n_tensor)
     acts = gather_first(forward_acts, n_tensor)
-    grads = gather_first(backward_grad, n_tensor)
     wide, tall = load_weights(gate_weight, up_weight, down_weight, cores)
+    other_grads = exchange(backward_grad, "dp", cores, 1)
     other_acts = exchange(forward_acts, "dp", cores, 1)
-    other_grads = exchange(backward_grad, "dp", cores, 1)
-    acts = gather_tokens(acts, other_acts, cores, after=[tall, other_acts, grads[1]])
+    grads = gather_tokens(grads, other_grads, cores, after=[tall, other_grads])
+    parts = project(grads, tall, True, straight, n_pipe, n_tensor)
+    parts = [parts[0]] + [swap(parts[s], s) for s in (3, 1, 2)]
+
+    mine, other = small_kernel(
+        stored_body,
+        [((2, rows, units), BF16)] * 2,
+        [stored_gate, stored_up],
+        "stored",
+        after=[parts[0]],
+    )
+    other = exchange(other, "dp", cores, 1)
+    (slopes,) = small_kernel(
+        slopes_body, [((2, cores * rows, units), BF16)], [*parts, mine, other], "slopes", after=acts[:0:-1]
+    )
+    slopes_x, slopes_y = swap(slopes, x), swap(slopes, y)
+
+    acts = gather_tokens(acts, other_acts, cores, after=[slopes])
     keep, for_x, for_y = project(
-        acts, wide, False, balanced_layout, n_pipe, n_tensor
+        acts, wide, False, balanced_layout, n_pipe, n_tensor, after=[slopes]
     )
     came_x, came_y = swap(for_x, x), swap(for_y, y)
-    mine, other = small_kernel(
-        stored_body, [((2, rows, units), BF16)] * 2, [stored_gate, stored_up], "stored", after=[keep]
-    )
-    other = exchange(other, "dp", cores, 1)
-    grads = gather_tokens(grads, other_grads, cores, after=[keep])
-    parts = project(grads, tall, True, straight, n_pipe, n_tensor, after=[other])
-    parts = [parts[0]] + [swap(parts[s], s) for s in (3, 1, 2)]
-
     half = ((2, rows, units), BF16)
+
+    def halves_body(ins, outs):
+        outs[0][...] = ins[0][:, :rows]
+        outs[1][...] = ins[1][:, rows:]
+
+    far_y, far_x = small_kernel(
+        halves_body, [half, half], [slopes_x, slopes_y], "forward_halves", after=[keep]
+    )
+    slopes_all = [slopes, slopes_x, slopes_y, swap(far_y, y), swap(far_x, x)]
+    back = contract(
+        slopes_all, balanced_pieces, wide, True, cores, n_pipe, n_tensor
+    )
     on_x, on_y = small_kernel(
-        pass_on_body, [half, half], [keep, came_x, came_y], "pass_on", after=[parts[0]]
-    )
+        pass_on_body, [half, half], [keep, came_x, came_y], "pass_on", after=[back[0]]
+    )
+    came, input_grad = finish(back, cores, n_tensor)
+
     sums = [keep, came_x, came_y, swap(on_x, x), swap(on_y, y)]
-    (hidden,) = small_kernel(hidden_body, [((1, cores * rows, units), BF16)], sums, "hidden")
+    (hidden,) = small_kernel(
+        hidden_body, [((1, cores * rows, units), BF16)], sums, "hidden"
+    )
     hidden_all = [hidden] + [swap(hidden, s) for s in range(1, n_pipe)]
-
-    (slopes,) = small_kernel(
-        slopes_body,
-        [((2, cores * rows, units), BF16)],
-        [*parts, mine, other],
-        "slopes",
-        after=[hidden],
-    )
-    slopes_x, slopes_y = swap(slopes, x), swap(slopes, y)
-
-    out = contract(
-        hidden_all, straight_pieces, tall, False, cores, n_pipe, n_tensor, after=[slopes]
-    )
-    slopes_all = [
-        slopes,
-        slopes_x,
-        slopes_y,
-        swap(slopes_x[:, :rows], y),
-        swap(slopes_y[:, rows:], x),
-    ]
-    came, layer_output = finish(out, cores, n_tensor)
-    back = contract(
-        slopes_all,
-        balanced_pieces,
-        wide,
-        True,
-        cores,
-        n_pipe,
-        n_tensor,
-    )
+    out = contract(hidden_all, straight_pieces, tall, False, cores, n_pipe, n_tensor)
 
     def copy_body(ins, outs):
         outs[0][...] = ins[0][...]
 
-    (held,) = small_kernel(copy_body, [(back[1].shape, BF16)], back[1:], "hold", after=came[:1])
-    _, input_grad = finish([back[0], held], cores, n_tensor)
+    (held,) = small_kernel(copy_body, [(out[1].shape, BF16)], out[1:], "hold", after=came)
+    _, layer_output = finish([out[0], held], cores, n_tensor)
     return layer_output, input_grad
 
 

time: 109 us -> 112 us (1.028)
  waiting for transfers between devices: 48.1 us -> 56.2 us
  starting transfers between devices: 38.1 us -> 32.5 us
    ppermute x33, waiting for transfers between devices: 48.1 us -> 56.2 us  [exchange(): return lax.ppermute(value, axis, [(i, i ^ step) for i in range(size)])]
    ppermute x33, starting transfers between devices: 38.1 us -> 32.5 us  [exchange(): return lax.ppermute(value, axis, [(i, i ^ step) for i in range(size)])]
  transfers between devices with their start and end apart: 33 -> 33, of which waited for: 17 -> 15; matrix products, arithmetic and copies ran while one was open for 1% -> 1% of each run, Pallas kernels for 19% -> 18%
where the time goes in v2:
time: 112 us
  waiting for transfers between devices  56.2 us (50%)
  starting transfers between devices  32.5 us (29%)
  Pallas kernels  20.7 us (18%)
  other arithmetic  1.43 us (1%)
    ppermute x33, waiting for transfers between devices, exchange(): return lax.ppermute(value, axis, [(i, i ^ step) for i in range(size)])  56.2 us
    ppermute x33, starting transfers between devices, exchange(): return lax.ppermute(value, axis, [(i, i ^ step) for i in range(size)])  32.5 us
    pallas_call x1, Pallas kernels, load_weights(): pl.pallas_call(kernel, in_specs=[IN_PLACE] * 3, out_specs=[IN_VMEM] * 2,...  7.56 us
    pallas_call x2, Pallas kernels, contract(): pl.pallas_call(kernel, in_specs=[IN_VMEM] * (n_in + 1) + [IN_PLACE] * n_a...  6.13 us
    pallas_call x2, Pallas kernels, project(): pl.pallas_call(kernel, in_specs=[IN_VMEM] * (n_in + 1) + [IN_PLACE] * n_a...  6.11 us
  transfers between devices with their start and end apart: 33, of which 15 were waited for; matrix products, arithmetic and copies ran while one was open for 1% of the time, Pallas kernels for 18%

profile of v2, /device:TPU:0, one launch (start us, length us, event | category | flops | bytes accessed | tf_op | source)
XLA Modules:
  0.0 111.8 jit_solution(1368915735116369324)
XLA Ops:
  0.7 5.1 %collective-permute-start.5 = (bf16[32,2048]{1,0:T(8,128)(2,1)}, bf16[32,2048]{1,0:T(8,128)(2,1)S(1)}, u32[]{:S(2)}, u32[]{:S(2)}) collective-permute-start(bf16[32,2048]{1,0:T(8,128)(2,1)} %refs_0_.3), channel_id=1, source_target_pairs={{0,3},{1,2},{2,1},{3,0},{4,7},{5,6},{6,5},{7,4},{8,11},{9,10},{10,... | collective-permute-start | bytes 393224 | tf_op jit(solution)/shard_map/ppermute | solution.py:20
  5.8 0.6 collective-permute-start.3
  6.4 0.0 collective-permute-start.6
  6.4 7.6 %load_weights.1 = (bf16[2,2048,1792]{2,1,0:T(8,128)(2,1)S(1)}, bf16[1,1792,2048]{2,1,0:T(8,128)(2,1)S(1)}) custom-call(bf16[2048,3584]{1,0:T(8,128)(2,1)} %gate.1, bf16[2048,3584]{1,0:T(8,128)(2,1)} %up.1, bf16[3584,2048]{1,0:T(8,128)(2,1)} %down.1), custom_call_target="tpu_custom_call" | custom-call | bytes 22020096 | tf_op jit(solution)/shard_map/load_weights/pallas_call | solution.py:78
  14.0 0.0 copy-start
  14.0 0.0 copy-start.1
  14.0 0.0 collective-permute-done.5.refs_2_
  14.0 3.0 %collective-permute-done.4.refs_1_ = bf16[32,2048]{1,0:T(8,128)(2,1)S(1)} collective-permute-done((bf16[32,2048]{1,0:T(8,128)(2,1)}, bf16[32,2048]{1,0:T(8,128)(2,1)S(1)}, u32[]{:S(2)}, u32[]{:S(2)}) %collective-permute-start.4) | collective-permute-done | bytes 131104 | tf_op jit(solution)/shard_map/ppermute | solution.py:20
  17.1 0.1 collective-permute-start.7
  17.2 2.5 %collective-permute-start.2 = (bf16[32,2048]{1,0:T(8,128)(2,1)S(1)}, bf16[32,2048]{1,0:T(8,128)(2,1)S(1)}, u32[]{:S(2)}, u32[]{:S(2)}) collective-permute-start(bf16[32,2048]{1,0:T(8,128)(2,1)S(1)} %copy-done.3), channel_id=1, source_target_pairs={{0,3},{1,2},{2,1},{3,0},{4,7},{5,6},{6,5},{7,4},{8,11},{9,10},{10,... | collective-permute-start | bytes 393224 | tf_op jit(solution)/shard_map/ppermute | solution.py:20
  19.7 2.1 %pull_back.1 = (f32[1,64,1792]{2,1,0:T(8,128)S(1)}, bf16[1,64,1792]{2,1,0:T(8,128)(2,1)S(1)}, bf16[1,64,1792]{2,1,0:T(8,128)(2,1)S(1)}, bf16[1,64,1792]{2,1,0:T(8,128)(2,1)S(1)}) custom-call(bf16[32,2048]{1,0:T(8,128)(2,1)S(1)} %copy-done.2, bf16[96,2048]{1,0:T(8,128)(2,1)S(1)} %assemble.2.refs_1_, ...), custom_call_target="tpu_custom_call" | custom-call | tf_op jit(solution)/shard_map/pull_back/pallas_call | solution.py:150
  21.8 2.5 %collective-permute-start.8 = (bf16[1,64,1792]{2,1,0:T(8,128)(2,1)S(1)}, bf16[1,64,1792]{2,1,0:T(8,128)(2,1)S(1)}, u32[]{:S(2)}, u32[]{:S(2)}) collective-permute-start(bf16[1,64,1792]{2,1,0:T(8,128)(2,1)S(1)} %get-tuple-element.31), channel_id=1, source_target_pairs={{0,12},{4,8},{8,4},{12,0},{1,13},{5,9},{9,5},{13,1},{2,14},{6,10},... | collective-permute-start | bytes 688136 | tf_op jit(solution)/shard_map/ppermute | solution.py:20
  24.4 0.5 collective-permute-start.9
  24.9 0.5 collective-permute-start.10
  25.4 0.0 collective-permute-done.2.refs_6_.refs_2_
  25.5 0.1 collective-permute-start.11
  25.5 5.2 %collective-permute-done.1.refs_7_.refs_1_ = bf16[32,2048]{1,0:T(8,128)(2,1)S(1)} collective-permute-done((bf16[32,2048]{1,0:T(8,128)(2,1)S(1)}, bf16[32,2048]{1,0:T(8,128)(2,1)S(1)}, u32[]{:S(2)}, u32[]{:S(2)}) %collective-permute-start.1) | collective-permute-done | bytes 131104 | tf_op jit(solution)/shard_map/ppermute | solution.py:20
  30.8 0.0 collective-permute-start
  30.8 5.4 %collective-permute-done.refs_8_.refs_0_ = bf16[32,2048]{1,0:T(8,128)(2,1)S(1)} collective-permute-done((bf16[32,2048]{1,0:T(8,128)(2,1)S(1)}, bf16[32,2048]{1,0:T(8,128)(2,1)S(1)}, u32[]{:S(2)}, u32[]{:S(2)}) %collective-permute-start) | collective-permute-done | bytes 131104 | tf_op jit(solution)/shard_map/ppermute | solution.py:20
  36.2 0.0 collective-permute-done.8.refs_1_
  36.2 0.3 slopes.1.refs_3_.refs_5_.refs_0_
  36.5 0.1 collective-permute-start.13
  36.6 0.5 collective-permute-start.12
  37.1 1.5 %collective-permute-start.17 = (bf16[2,64,1792]{2,1,0:T(8,128)(2,1)S(1)}, bf16[2,64,1792]{2,1,0:T(8,128)(2,1)S(1)}, u32[]{:S(2)}, u32[]{:S(2)}) collective-permute-start(bf16[2,64,1792]{2,1,0:T(8,128)(2,1)S(1)} %slopes.1.refs_3_.refs_5_.refs_0_), channel_id=1, source_target_pairs={{0,8},{4,12},{8,0},{12,4},{1,9},{5,13},{9,1},{13,5},{2,10},{6,14},... | collective-permute-start | bytes 1376264 | tf_op jit(solution)/shard_map/ppermute | solution.py:20
  38.6 1.5 %collective-permute-start.16 = (bf16[2,64,1792]{2,1,0:T(8,128)(2,1)S(1)}, bf16[2,64,1792]{2,1,0:T(8,128)(2,1)S(1)}, u32[]{:S(2)}, u32[]{:S(2)}) collective-permute-start(bf16[2,64,1792]{2,1,0:T(8,128)(2,1)S(1)} %slopes.1.refs_3_.refs_5_.refs_0_), channel_id=1, source_target_pairs={{0,4},{4,0},{8,12},{12,8},{1,5},{5,1},{9,13},{13,9},{2,6},{6,2},{1... | collective-permute-start | bytes 1376264 | tf_op jit(solution)/shard_map/ppermute | solution.py:20
  40.1 4.0 %project.1 = (f32[2,128,1792]{2,1,0:T(8,128)S(1)}, bf16[2,64,1792]{2,1,0:T(8,128)(2,1)S(1)}, bf16[2,64,1792]{2,1,0:T(8,128)(2,1)S(1)}) custom-call(bf16[32,2048]{1,0:T(8,128)(2,1)S(1)} %copy-done.3, bf16[96,2048]{1,0:T(8,128)(2,1)S(1)} %assemble.3.refs_1_, bf16[32,2048]{1,0:T(8,128)(2,1)S(1)} %collective-permute-done.12.refs_2_, ...), custom_call_target="tpu_custom_call" | custom-call | flops 3758096384 | bytes 14680064 | tf_op jit(solution)/shard_map/project/pallas_call | solution.py:150
  44.1 0.6 collective-permute-start.14
  44.7 0.9 collective-permute-start.15
  45.6 4.9 %collective-permute-done.17.refs_1_.refs_2_ = bf16[2,64,1792]{2,1,0:T(8,128)(2,1)S(1)} collective-permute-done((bf16[2,64,1792]{2,1,0:T(8,128)(2,1)S(1)}, bf16[2,64,1792]{2,1,0:T(8,128)(2,1)S(1)}, u32[]{:S(2)}, u32[]{:S(2)}) %collective-permute-start.17) | collective-permute-done | bytes 458784 | tf_op jit(solution)/shard_map/ppermute | solution.py:20
  50.5 1.6 %collective-permute-done.16.refs_0_.refs_1_ = bf16[2,64,1792]{2,1,0:T(8,128)(2,1)S(1)} collective-permute-done((bf16[2,64,1792]{2,1,0:T(8,128)(2,1)S(1)}, bf16[2,64,1792]{2,1,0:T(8,128)(2,1)S(1)}, u32[]{:S(2)}, u32[]{:S(2)}) %collective-permute-start.16) | collective-permute-done | bytes 458784 | tf_op jit(solution)/shard_map/ppermute | solution.py:20
  52.1 0.6 collective-permute-start.18
  52.7 1.5 %collective-permute-start.19 = (bf16[2,32,1792]{2,1,0:T(8,128)(2,1)S(1)}, bf16[2,32,1792]{2,1,0:T(8,128)(2,1)S(1)}, u32[]{:S(2)}, u32[]{:S(2)}) collective-permute-start(bf16[2,32,1792]{2,1,0:T(8,128)(2,1)S(1)} %get-tuple-element.41), channel_id=1, source_target_pairs={{0,4},{4,0},{8,12},{12,8},{1,5},{5,1},{9,13},{13,9},{2,6},{6,2},{1... | collective-permute-start | bytes 688136 | tf_op jit(solution)/shard_map/ppermute | solution.py:20
  54.2 10.2 %collective-permute-done.18.refs_3_ = bf16[2,32,1792]{2,1,0:T(8,128)(2,1)S(1)} collective-permute-done((bf16[2,32,1792]{2,1,0:T(8,128)(2,1)S(1)}, bf16[2,32,1792]{2,1,0:T(8,128)(2,1)S(1)}, u32[]{:S(2)}, u32[]{:S(2)}) %collective-permute-start.18) | collective-permute-done | bytes 229408 | tf_op jit(solution)/shard_map/ppermute | solution.py:20
  64.4 1.2 %collective-permute-done.19.refs_4_ = bf16[2,32,1792]{2,1,0:T(8,128)(2,1)S(1)} collective-permute-done((bf16[2,32,1792]{2,1,0:T(8,128)(2,1)S(1)}, bf16[2,32,1792]{2,1,0:T(8,128)(2,1)S(1)}, u32[]{:S(2)}, u32[]{:S(2)}) %collective-permute-start.19) | collective-permute-done | bytes 229408 | tf_op jit(solution)/shard_map/ppermute | solution.py:20
  65.6 4.0 %input_grad.1 = (f32[128,2048]{1,0:T(8,128)S(1)}, bf16[128,2048]{1,0:T(8,128)(2,1)S(1)}) custom-call(bf16[2,64,1792]{2,1,0:T(8,128)(2,1)S(1)} %slopes.1.refs_3_.refs_5_.refs_0_, bf16[2,64,1792]{2,1,0:T(8,128)(2,1)S(1)} %collective-permute-done.16.refs_0_.refs_1_, bf16[2,64,1792]{2,1,0:T(8,128)(2,1)S(1)} %collective-permute-done.17.refs_1_.refs_2_, ...), custom_call_target="tpu_custom_call" | custom-call | tf_op jit(solution)/shard_map/input_grad/pallas_call | solution.py:224
  69.7 0.1 collective-permute-start.25
  69.7 0.0 collective-permute-done.14.refs_1_
  69.8 0.1 pass_on.1
  69.8 1.6 %collective-permute-start.20 = (bf16[2,32,1792]{2,1,0:T(8,128)(2,1)S(1)}, bf16[2,32,1792]{2,1,0:T(8,128)(2,1)S(1)}, u32[]{:S(2)}, u32[]{:S(2)}) collective-permute-start(bf16[2,32,1792]{2,1,0:T(8,128)(2,1)S(1)} %get-tuple-element.43), channel_id=1, source_target_pairs={{0,4},{4,0},{8,12},{12,8},{1,5},{5,1},{9,13},{13,9},{2,6},{6,2},{1... | collective-permute-start | bytes 688136 | tf_op jit(solution)/shard_map/ppermute | solution.py:20
  71.4 0.5 collective-permute-start.21
  71.9 6.0 %collective-permute-done.20.refs_3_ = bf16[2,32,1792]{2,1,0:T(8,128)(2,1)S(1)} collective-permute-done((bf16[2,32,1792]{2,1,0:T(8,128)(2,1)S(1)}, bf16[2,32,1792]{2,1,0:T(8,128)(2,1)S(1)}, u32[]{:S(2)}, u32[]{:S(2)}) %collective-permute-start.20) | collective-permute-done | bytes 229408 | tf_op jit(solution)/shard_map/ppermute | solution.py:20
  77.9 1.2 %collective-permute-done.21.refs_4_ = bf16[2,32,1792]{2,1,0:T(8,128)(2,1)S(1)} collective-permute-done((bf16[2,32,1792]{2,1,0:T(8,128)(2,1)S(1)}, bf16[2,32,1792]{2,1,0:T(8,128)(2,1)S(1)}, u32[]{:S(2)}, u32[]{:S(2)}) %collective-permute-start.21) | collective-permute-done | bytes 229408 | tf_op jit(solution)/shard_map/ppermute | solution.py:20
  79.1 0.2 hidden.1.refs_0_
  79.3 0.6 collective-permute-start.24
  79.9 1.5 %collective-permute-start.23 = (bf16[1,64,1792]{2,1,0:T(8,128)(2,1)S(1)}, bf16[1,64,1792]{2,1,0:T(8,128)(2,1)S(1)}, u32[]{:S(2)}, u32[]{:S(2)}) collective-permute-start(bf16[1,64,1792]{2,1,0:T(8,128)(2,1)S(1)} %hidden.1.refs_0_), channel_id=1, source_target_pairs={{0,8},{4,12},{8,0},{12,4},{1,9},{5,13},{9,1},{13,5},{2,10},{6,14},... | collective-permute-start | bytes 688136 | tf_op jit(solution)/shard_map/ppermute | solution.py:20
  81.4 1.5 %collective-permute-start.22 = (bf16[1,64,1792]{2,1,0:T(8,128)(2,1)S(1)}, bf16[1,64,1792]{2,1,0:T(8,128)(2,1)S(1)}, u32[]{:S(2)}, u32[]{:S(2)}) collective-permute-start(bf16[1,64,1792]{2,1,0:T(8,128)(2,1)S(1)} %hidden.1.refs_0_), channel_id=1, source_target_pairs={{0,4},{4,0},{8,12},{12,8},{1,5},{5,1},{9,13},{13,9},{2,6},{6,2},{1... | collective-permute-start | bytes 688136 | tf_op jit(solution)/shard_map/ppermute | solution.py:20
  82.9 0.1 add_core.2
  83.0 2.3 %collective-permute-start.26 = (bf16[32,2048]{1,0:T(8,128)(2,1)S(1)}, bf16[32,2048]{1,0:T(8,128)(2,1)S(1)}, u32[]{:S(2)}, u32[]{:S(2)}) collective-permute-start(bf16[32,2048]{1,0:T(8,128)(2,1)S(1)} %get-tuple-element.48), channel_id=1, source_target_pairs={{0,3},{1,2},{2,1},{3,0},{4,7},{5,6},{6,5},{7,4},{8,11},{9,10},{10,... | collective-permute-start | bytes 393224 | tf_op jit(solution)/shard_map/ppermute | solution.py:20
  85.3 0.0 collective-permute-start.27
  85.3 3.5 %collective-permute-done.24.refs_3_ = bf16[1,64,1792]{2,1,0:T(8,128)(2,1)S(1)} collective-permute-done((bf16[1,64,1792]{2,1,0:T(8,128)(2,1)S(1)}, bf16[1,64,1792]{2,1,0:T(8,128)(2,1)S(1)}, u32[]{:S(2)}, u32[]{:S(2)}) %collective-permute-start.24) | collective-permute-done | bytes 229408 | tf_op jit(solution)/shard_map/ppermute | solution.py:20
  88.8 0.8 collective-permute-start.28
  89.6 1.8 %collective-permute-done.23.refs_2_ = bf16[1,64,1792]{2,1,0:T(8,128)(2,1)S(1)} collective-permute-done((bf16[1,64,1792]{2,1,0:T(8,128)(2,1)S(1)}, bf16[1,64,1792]{2,1,0:T(8,128)(2,1)S(1)}, u32[]{:S(2)}, u32[]{:S(2)}) %collective-permute-start.23) | collective-permute-done | bytes 229408 | tf_op jit(solution)/shard_map/ppermute | solution.py:20
  91.4 0.0 collective-permute-done.22.refs_1_
  91.4 2.1 %layer_output.1 = (f32[128,2048]{1,0:T(8,128)S(1)}, bf16[128,2048]{1,0:T(8,128)(2,1)S(1)}) custom-call(bf16[1,64,1792]{2,1,0:T(8,128)(2,1)S(1)} %hidden.1.refs_0_, bf16[1,64,1792]{2,1,0:T(8,128)(2,1)S(1)} %collective-permute-done.22.refs_1_, bf16[1,64,1792]{2,1,0:T(8,128)(2,1)S(1)} %collective-permute-done.23.refs_2_, ...), custom_call_target="tpu_custom_call" | custom-call | flops 1879048192 | bytes 7340032 | tf_op jit(solution)/shard_map/layer_output/pallas_call | solution.py:224
  93.6 2.3 %collective-permute-done.27.refs_2_ = bf16[32,2048]{1,0:T(8,128)(2,1)S(1)} collective-permute-done((bf16[32,2048]{1,0:T(8,128)(2,1)S(1)}, bf16[32,2048]{1,0:T(8,128)(2,1)S(1)}, u32[]{:S(2)}, u32[]{:S(2)}) %collective-permute-start.27) | collective-permute-done | bytes 131104 | tf_op jit(solution)/shard_map/ppermute | solution.py:20
  95.9 0.1 collective-permute-start.29
  96.0 1.9 %collective-permute-done.29.refs_1_ = bf16[128,2048]{1,0:T(8,128)(2,1)S(1)} collective-permute-done((bf16[128,2048]{1,0:T(8,128)(2,1)S(1)}, bf16[128,2048]{1,0:T(8,128)(2,1)S(1)}, u32[]{:S(2)}, u32[]{:S(2)}) %collective-permute-start.29) | collective-permute-done | bytes 524320 | tf_op jit(solution)/shard_map/ppermute | solution.py:20
  97.9 0.1 add_core.3
  98.0 2.3 %collective-permute-start.30 = (bf16[32,2048]{1,0:T(8,128)(2,1)S(1)}, bf16[32,2048]{1,0:T(8,128)(2,1)S(1)}, u32[]{:S(2)}, u32[]{:S(2)}) collective-permute-start(bf16[32,2048]{1,0:T(8,128)(2,1)S(1)} %get-tuple-element.52), channel_id=1, source_target_pairs={{0,3},{1,2},{2,1},{3,0},{4,7},{5,6},{6,5},{7,4},{8,11},{9,10},{10,... | collective-permute-start | bytes 393224 | tf_op jit(solution)/shard_map/ppermute | solution.py:20
  100.3 2.1 %collective-permute-start.32 = (bf16[32,2048]{1,0:T(8,128)(2,1)S(1)}, bf16[32,2048]{1,0:T(8,128)(2,1)S(1)}, u32[]{:S(2)}, u32[]{:S(2)}) collective-permute-start(bf16[32,2048]{1,0:T(8,128)(2,1)S(1)} %get-tuple-element.54), channel_id=1, source_target_pairs={{0,1},{1,0},{2,3},{3,2},{4,5},{5,4},{6,7},{7,6},{8,9},{9,8},{10,11... | collective-permute-start | bytes 393224 | tf_op jit(solution)/shard_map/ppermute | solution.py:20
  102.4 0.7 add_convert_fusion
  103.2 3.2 %collective-permute-done.30 = bf16[32,2048]{1,0:T(8,128)(2,1)S(1)} collective-permute-done((bf16[32,2048]{1,0:T(8,128)(2,1)S(1)}, bf16[32,2048]{1,0:T(8,128)(2,1)S(1)}, u32[]{:S(2)}, u32[]{:S(2)}) %collective-permute-start.30) | collective-permute-done | bytes 131104 | tf_op jit(solution)/shard_map/ppermute | solution.py:20
  106.3 4.7 %collective-permute-done.31 = bf16[32,2048]{1,0:T(8,128)(2,1)S(1)} collective-permute-done((bf16[32,2048]{1,0:T(8,128)(2,1)S(1)}, bf16[32,2048]{1,0:T(8,128)(2,1)S(1)}, u32[]{:S(2)}, u32[]{:S(2)}) %collective-permute-start.31) | collective-permute-done | bytes 131104 | tf_op jit(solution)/shard_map/ppermute | solution.py:20
  111.0 0.7 add_convert_fusion.1
  (27 shorter events, 0.2 us)
Async XLA Ops:
  0.6 19.1 %copy-start.2 = (bf16[32,2048]{1,0:T(8,128)(2,1)S(1)}, bf16[32,2048]{1,0:T(8,128)(2,1)}, u32[]{:S(2)}) copy-start(bf16[32,2048]{1,0:T(8,128)(2,1)} %refs_0_.3) | copy-start | bytes 393220
  0.6 16.5 %copy-start.3 = (bf16[32,2048]{1,0:T(8,128)(2,1)S(1)}, bf16[32,2048]{1,0:T(8,128)(2,1)}, u32[]{:S(2)}) copy-start(bf16[32,2048]{1,0:T(8,128)(2,1)} %refs_0_.5) | copy-start | bytes 393220
  0.7 13.4 %collective-permute-start.5 = (bf16[32,2048]{1,0:T(8,128)(2,1)}, bf16[32,2048]{1,0:T(8,128)(2,1)S(1)}, u32[]{:S(2)}, u32[]{:S(2)}) collective-permute-start(bf16[32,2048]{1,0:T(8,128)(2,1)} %refs_0_.3), channel_id=1, source_target_pairs={{0,3},{1,2},{2,1},{3,0},{4,7},{5,6},{6,5},{7,4},{8,11},{9,10},{10,... | collective-permute-start | bytes 393224 | tf_op jit(solution)/shard_map/ppermute | solution.py:20
  5.8 11.3 %collective-permute-start.4 = (bf16[32,2048]{1,0:T(8,128)(2,1)}, bf16[32,2048]{1,0:T(8,128)(2,1)S(1)}, u32[]{:S(2)}, u32[]{:S(2)}) collective-permute-start(bf16[32,2048]{1,0:T(8,128)(2,1)} %refs_0_.3), channel_id=1, source_target_pairs={{0,2},{1,3},{2,0},{3,1},{4,6},{5,7},{6,4},{7,5},{8,10},{9,11},{10,... | collective-permute-start | bytes 393224 | tf_op jit(solution)/shard_map/ppermute | solution.py:20
  5.8 11.3 %collective-permute-start.3 = (bf16[32,2048]{1,0:T(8,128)(2,1)}, bf16[32,2048]{1,0:T(8,128)(2,1)S(1)}, u32[]{:S(2)}, u32[]{:S(2)}) collective-permute-start(bf16[32,2048]{1,0:T(8,128)(2,1)} %refs_0_.3), channel_id=1, source_target_pairs={{0,1},{1,0},{2,3},{3,2},{4,5},{5,4},{6,7},{7,6},{8,9},{9,8},{10,11... | collective-permute-start | bytes 393224 | tf_op jit(solution)/shard_map/ppermute | solution.py:20
  6.4 10.6 %collective-permute-start.6 = (bf16[32,2048]{1,0:T(8,128)(2,1)}, bf16[32,2048]{1,0:T(8,128)(2,1)S(1)}, u32[]{:S(2)}, u32[]{:S(2)}) collective-permute-start(bf16[32,2048]{1,0:T(8,128)(2,1)} %refs_0_.3), channel_id=1, source_target_pairs={{0,16},{16,0},{1,17},{17,1},{2,18},{18,2},{3,19},{19,3},{4,20},{20... | collective-permute-start | bytes 393224 | tf_op jit(solution)/shard_map/ppermute | solution.py:20
  14.0 11.4 %copy-start = (bf16[32,3584]{1,0:T(8,128)(2,1)S(1)}, bf16[32,3584]{1,0:T(8,128)(2,1)}, u32[]{:S(2)}) copy-start(bf16[32,3584]{1,0:T(8,128)(2,1)} %refs_0_.4) | copy-start | bytes 688132
  14.0 11.4 %copy-start.1 = (bf16[32,3584]{1,0:T(8,128)(2,1)S(1)}, bf16[32,3584]{1,0:T(8,128)(2,1)}, u32[]{:S(2)}) copy-start(bf16[32,3584]{1,0:T(8,128)(2,1)} %refs_1_.1) | copy-start | bytes 688132
  17.1 2.6 %collective-permute-start.7 = (bf16[96,2048]{1,0:T(8,128)(2,1)S(1)}, bf16[96,2048]{1,0:T(8,128)(2,1)S(1)}, u32[]{:S(2)}, u32[]{:S(2)}) collective-permute-start(bf16[96,2048]{1,0:T(8,128)(2,1)S(1)} %assemble.2.refs_1_), channel_id=1, source_target_pairs={{0,16},{16,0},{1,17},{17,1},{2,18},{18,2},{3,19},{19,3},{4,20},{20... | collective-permute-start | bytes 1179656 | tf_op jit(solution)/shard_map/ppermute | solution.py:20
  17.2 8.3 %collective-permute-start.2 = (bf16[32,2048]{1,0:T(8,128)(2,1)S(1)}, bf16[32,2048]{1,0:T(8,128)(2,1)S(1)}, u32[]{:S(2)}, u32[]{:S(2)}) collective-permute-start(bf16[32,2048]{1,0:T(8,128)(2,1)S(1)} %copy-done.3), channel_id=1, source_target_pairs={{0,3},{1,2},{2,1},{3,0},{4,7},{5,6},{6,5},{7,4},{8,11},{9,10},{10,... | collective-permute-start | bytes 393224 | tf_op jit(solution)/shard_map/ppermute | solution.py:20
  19.7 11.1 %collective-permute-start.1 = (bf16[32,2048]{1,0:T(8,128)(2,1)S(1)}, bf16[32,2048]{1,0:T(8,128)(2,1)S(1)}, u32[]{:S(2)}, u32[]{:S(2)}) collective-permute-start(bf16[32,2048]{1,0:T(8,128)(2,1)S(1)} %copy-done.3), channel_id=1, source_target_pairs={{0,2},{1,3},{2,0},{3,1},{4,6},{5,7},{6,4},{7,5},{8,10},{9,11},{10,... | collective-permute-start | bytes 393224 | tf_op jit(solution)/shard_map/ppermute | solution.py:20
  21.8 14.3 %collective-permute-start.8 = (bf16[1,64,1792]{2,1,0:T(8,128)(2,1)S(1)}, bf16[1,64,1792]{2,1,0:T(8,128)(2,1)S(1)}, u32[]{:S(2)}, u32[]{:S(2)}) collective-permute-start(bf16[1,64,1792]{2,1,0:T(8,128)(2,1)S(1)} %get-tuple-element.31), channel_id=1, source_target_pairs={{0,12},{4,8},{8,4},{12,0},{1,13},{5,9},{9,5},{13,1},{2,14},{6,10},... | collective-permute-start | bytes 688136 | tf_op jit(solution)/shard_map/ppermute | solution.py:20
  24.4 11.8 %collective-permute-start.9 = (bf16[1,64,1792]{2,1,0:T(8,128)(2,1)S(1)}, bf16[1,64,1792]{2,1,0:T(8,128)(2,1)S(1)}, u32[]{:S(2)}, u32[]{:S(2)}) collective-permute-start(bf16[1,64,1792]{2,1,0:T(8,128)(2,1)S(1)} %get-tuple-element.32), channel_id=1, source_target_pairs={{0,4},{4,0},{8,12},{12,8},{1,5},{5,1},{9,13},{13,9},{2,6},{6,2},{1... | collective-permute-start | bytes 688136 | tf_op jit(solution)/shard_map/ppermute | solution.py:20
  24.9 11.3 %collective-permute-start.10 = (bf16[1,64,1792]{2,1,0:T(8,128)(2,1)S(1)}, bf16[1,64,1792]{2,1,0:T(8,128)(2,1)S(1)}, u32[]{:S(2)}, u32[]{:S(2)}) collective-permute-start(bf16[1,64,1792]{2,1,0:T(8,128)(2,1)S(1)} %get-tuple-element.33), channel_id=1, source_target_pairs={{0,8},{4,12},{8,0},{12,4},{1,9},{5,13},{9,1},{13,5},{2,10},{6,14},... | collective-permute-start | bytes 688136 | tf_op jit(solution)/shard_map/ppermute | solution.py:20
  25.5 10.7 %collective-permute-start.11 = (bf16[2,32,1792]{2,1,0:T(8,128)(2,1)S(1)}, bf16[2,32,1792]{2,1,0:T(8,128)(2,1)S(1)}, u32[]{:S(2)}, u32[]{:S(2)}) collective-permute-start(bf16[2,32,1792]{2,1,0:T(8,128)(2,1)S(1)} %get-tuple-element.35), channel_id=1, source_target_pairs={{0,16},{16,0},{1,17},{17,1},{2,18},{18,2},{3,19},{19,3},{4,20},{20... | collective-permute-start | bytes 688136 | tf_op jit(solution)/shard_map/ppermute | solution.py:20
  30.8 5.4 %collective-permute-start = (bf16[32,2048]{1,0:T(8,128)(2,1)S(1)}, bf16[32,2048]{1,0:T(8,128)(2,1)S(1)}, u32[]{:S(2)}, u32[]{:S(2)}) collective-permute-start(bf16[32,2048]{1,0:T(8,128)(2,1)S(1)} %copy-done.3), channel_id=1, source_target_pairs={{0,1},{1,0},{2,3},{3,2},{4,5},{5,4},{6,7},{7,6},{8,9},{9,8},{10,11... | collective-permute-start | bytes 393224 | tf_op jit(solution)/shard_map/ppermute | solution.py:20
  36.5 3.6 %collective-permute-start.13 = (bf16[96,2048]{1,0:T(8,128)(2,1)S(1)}, bf16[96,2048]{1,0:T(8,128)(2,1)S(1)}, u32[]{:S(2)}, u32[]{:S(2)}) collective-permute-start(bf16[96,2048]{1,0:T(8,128)(2,1)S(1)} %assemble.3.refs_1_), channel_id=1, source_target_pairs={{0,16},{16,0},{1,17},{17,1},{2,18},{18,2},{3,19},{19,3},{4,20},{20... | collective-permute-start | bytes 1179656 | tf_op jit(solution)/shard_map/ppermute | solution.py:20
  36.6 3.5 %collective-permute-start.12 = (bf16[32,2048]{1,0:T(8,128)(2,1)S(1)}, bf16[32,2048]{1,0:T(8,128)(2,1)S(1)}, u32[]{:S(2)}, u32[]{:S(2)}) collective-permute-start(bf16[32,2048]{1,0:T(8,128)(2,1)S(1)} %copy-done.3), channel_id=1, source_target_pairs={{0,16},{16,0},{1,17},{17,1},{2,18},{18,2},{3,19},{19,3},{4,20},{20... | collective-permute-start | bytes 393224 | tf_op jit(solution)/shard_map/ppermute | solution.py:20
  37.1 13.4 %collective-permute-start.17 = (bf16[2,64,1792]{2,1,0:T(8,128)(2,1)S(1)}, bf16[2,64,1792]{2,1,0:T(8,128)(2,1)S(1)}, u32[]{:S(2)}, u32[]{:S(2)}) collective-permute-start(bf16[2,64,1792]{2,1,0:T(8,128)(2,1)S(1)} %slopes.1.refs_3_.refs_5_.refs_0_), channel_id=1, source_target_pairs={{0,8},{4,12},{8,0},{12,4},{1,9},{5,13},{9,1},{13,5},{2,10},{6,14},... | collective-permute-start | bytes 1376264 | tf_op jit(solution)/shard_map/ppermute | solution.py:20
  38.6 13.4 %collective-permute-start.16 = (bf16[2,64,1792]{2,1,0:T(8,128)(2,1)S(1)}, bf16[2,64,1792]{2,1,0:T(8,128)(2,1)S(1)}, u32[]{:S(2)}, u32[]{:S(2)}) collective-permute-start(bf16[2,64,1792]{2,1,0:T(8,128)(2,1)S(1)} %slopes.1.refs_3_.refs_5_.refs_0_), channel_id=1, source_target_pairs={{0,4},{4,0},{8,12},{12,8},{1,5},{5,1},{9,13},{13,9},{2,6},{6,2},{1... | collective-permute-start | bytes 1376264 | tf_op jit(solution)/shard_map/ppermute | solution.py:20
  44.1 25.6 %collective-permute-start.14 = (bf16[2,64,1792]{2,1,0:T(8,128)(2,1)S(1)}, bf16[2,64,1792]{2,1,0:T(8,128)(2,1)S(1)}, u32[]{:S(2)}, u32[]{:S(2)}) collective-permute-start(bf16[2,64,1792]{2,1,0:T(8,128)(2,1)S(1)} %get-tuple-element.38), channel_id=1, source_target_pairs={{0,4},{4,0},{8,12},{12,8},{1,5},{5,1},{9,13},{13,9},{2,6},{6,2},{1... | collective-permute-start | bytes 1376264 | tf_op jit(solution)/shard_map/ppermute | solution.py:20
  44.7 25.0 %collective-permute-start.15 = (bf16[2,64,1792]{2,1,0:T(8,128)(2,1)S(1)}, bf16[2,64,1792]{2,1,0:T(8,128)(2,1)S(1)}, u32[]{:S(2)}, u32[]{:S(2)}) collective-permute-start(bf16[2,64,1792]{2,1,0:T(8,128)(2,1)S(1)} %get-tuple-element.39), channel_id=1, source_target_pairs={{0,8},{4,12},{8,0},{12,4},{1,9},{5,13},{9,1},{13,5},{2,10},{6,14},... | collective-permute-start | bytes 1376264 | tf_op jit(solution)/shard_map/ppermute | solution.py:20
  52.1 12.3 %collective-permute-start.18 = (bf16[2,32,1792]{2,1,0:T(8,128)(2,1)S(1)}, bf16[2,32,1792]{2,1,0:T(8,128)(2,1)S(1)}, u32[]{:S(2)}, u32[]{:S(2)}) collective-permute-start(bf16[2,32,1792]{2,1,0:T(8,128)(2,1)S(1)} %get-tuple-element.40), channel_id=1, source_target_pairs={{0,8},{4,12},{8,0},{12,4},{1,9},{5,13},{9,1},{13,5},{2,10},{6,14},... | collective-permute-start | bytes 688136 | tf_op jit(solution)/shard_map/ppermute | solution.py:20
  52.7 12.9 %collective-permute-start.19 = (bf16[2,32,1792]{2,1,0:T(8,128)(2,1)S(1)}, bf16[2,32,1792]{2,1,0:T(8,128)(2,1)S(1)}, u32[]{:S(2)}, u32[]{:S(2)}) collective-permute-start(bf16[2,32,1792]{2,1,0:T(8,128)(2,1)S(1)} %get-tuple-element.41), channel_id=1, source_target_pairs={{0,4},{4,0},{8,12},{12,8},{1,5},{5,1},{9,13},{13,9},{2,6},{6,2},{1... | collective-permute-start | bytes 688136 | tf_op jit(solution)/shard_map/ppermute | solution.py:20
  69.7 13.2 %collective-permute-start.25 = (bf16[128,2048]{1,0:T(8,128)(2,1)S(1)}, bf16[128,2048]{1,0:T(8,128)(2,1)S(1)}, u32[]{:S(2)}, u32[]{:S(2)}) collective-permute-start(bf16[128,2048]{1,0:T(8,128)(2,1)S(1)} %get-tuple-element.47), channel_id=1, source_target_pairs={{0,16},{16,0},{1,17},{17,1},{2,18},{18,2},{3,19},{19,3},{4,20},{20... | collective-permute-start | bytes 1572872 | tf_op jit(solution)/shard_map/ppermute | solution.py:20
  69.8 8.1 %collective-permute-start.20 = (bf16[2,32,1792]{2,1,0:T(8,128)(2,1)S(1)}, bf16[2,32,1792]{2,1,0:T(8,128)(2,1)S(1)}, u32[]{:S(2)}, u32[]{:S(2)}) collective-permute-start(bf16[2,32,1792]{2,1,0:T(8,128)(2,1)S(1)} %get-tuple-element.43), channel_id=1, source_target_pairs={{0,4},{4,0},{8,12},{12,8},{1,5},{5,1},{9,13},{13,9},{2,6},{6,2},{1... | collective-permute-start | bytes 688136 | tf_op jit(solution)/shard_map/ppermute | solution.py:20
  71.4 7.7 %collective-permute-start.21 = (bf16[2,32,1792]{2,1,0:T(8,128)(2,1)S(1)}, bf16[2,32,1792]{2,1,0:T(8,128)(2,1)S(1)}, u32[]{:S(2)}, u32[]{:S(2)}) collective-permute-start(bf16[2,32,1792]{2,1,0:T(8,128)(2,1)S(1)} %get-tuple-element.44), channel_id=1, source_target_pairs={{0,8},{4,12},{8,0},{12,4},{1,9},{5,13},{9,1},{13,5},{2,10},{6,14},... | collective-permute-start | bytes 688136 | tf_op jit(solution)/shard_map/ppermute | solution.py:20
  79.3 9.5 %collective-permute-start.24 = (bf16[1,64,1792]{2,1,0:T(8,128)(2,1)S(1)}, bf16[1,64,1792]{2,1,0:T(8,128)(2,1)S(1)}, u32[]{:S(2)}, u32[]{:S(2)}) collective-permute-start(bf16[1,64,1792]{2,1,0:T(8,128)(2,1)S(1)} %hidden.1.refs_0_), channel_id=1, source_target_pairs={{0,12},{4,8},{8,4},{12,0},{1,13},{5,9},{9,5},{13,1},{2,14},{6,10},... | collective-permute-start | bytes 688136 | tf_op jit(solution)/shard_map/ppermute | solution.py:20
  79.9 11.6 %collective-permute-start.23 = (bf16[1,64,1792]{2,1,0:T(8,128)(2,1)S(1)}, bf16[1,64,1792]{2,1,0:T(8,128)(2,1)S(1)}, u32[]{:S(2)}, u32[]{:S(2)}) collective-permute-start(bf16[1,64,1792]{2,1,0:T(8,128)(2,1)S(1)} %hidden.1.refs_0_), channel_id=1, source_target_pairs={{0,8},{4,12},{8,0},{12,4},{1,9},{5,13},{9,1},{13,5},{2,10},{6,14},... | collective-permute-start | bytes 688136 | tf_op jit(solution)/shard_map/ppermute | solution.py:20
  81.4 10.1 %collective-permute-start.22 = (bf16[1,64,1792]{2,1,0:T(8,128)(2,1)S(1)}, bf16[1,64,1792]{2,1,0:T(8,128)(2,1)S(1)}, u32[]{:S(2)}, u32[]{:S(2)}) collective-permute-start(bf16[1,64,1792]{2,1,0:T(8,128)(2,1)S(1)} %hidden.1.refs_0_), channel_id=1, source_target_pairs={{0,4},{4,0},{8,12},{12,8},{1,5},{5,1},{9,13},{13,9},{2,6},{6,2},{1... | collective-permute-start | bytes 688136 | tf_op jit(solution)/shard_map/ppermute | solution.py:20
  83.0 10.6 %collective-permute-start.26 = (bf16[32,2048]{1,0:T(8,128)(2,1)S(1)}, bf16[32,2048]{1,0:T(8,128)(2,1)S(1)}, u32[]{:S(2)}, u32[]{:S(2)}) collective-permute-start(bf16[32,2048]{1,0:T(8,128)(2,1)S(1)} %get-tuple-element.48), channel_id=1, source_target_pairs={{0,3},{1,2},{2,1},{3,0},{4,7},{5,6},{6,5},{7,4},{8,11},{9,10},{10,... | collective-permute-start | bytes 393224 | tf_op jit(solution)/shard_map/ppermute | solution.py:20
  85.3 10.6 %collective-permute-start.27 = (bf16[32,2048]{1,0:T(8,128)(2,1)S(1)}, bf16[32,2048]{1,0:T(8,128)(2,1)S(1)}, u32[]{:S(2)}, u32[]{:S(2)}) collective-permute-start(bf16[32,2048]{1,0:T(8,128)(2,1)S(1)} %get-tuple-element.49), channel_id=1, source_target_pairs={{0,2},{1,3},{2,0},{3,1},{4,6},{5,7},{6,4},{7,5},{8,10},{9,11},{10,... | collective-permute-start | bytes 393224 | tf_op jit(solution)/shard_map/ppermute | solution.py:20
  88.8 7.1 %collective-permute-start.28 = (bf16[32,2048]{1,0:T(8,128)(2,1)S(1)}, bf16[32,2048]{1,0:T(8,128)(2,1)S(1)}, u32[]{:S(2)}, u32[]{:S(2)}) collective-permute-start(bf16[32,2048]{1,0:T(8,128)(2,1)S(1)} %get-tuple-element.50), channel_id=1, source_target_pairs={{0,1},{1,0},{2,3},{3,2},{4,5},{5,4},{6,7},{7,6},{8,9},{9,8},{10,11... | collective-permute-start | bytes 393224 | tf_op jit(solution)/shard_map/ppermute | solution.py:20
  95.9 2.0 %collective-permute-start.29 = (bf16[128,2048]{1,0:T(8,128)(2,1)S(1)}, bf16[128,2048]{1,0:T(8,128)(2,1)S(1)}, u32[]{:S(2)}, u32[]{:S(2)}) collective-permute-start(bf16[128,2048]{1,0:T(8,128)(2,1)S(1)} %hold.1), channel_id=1, source_target_pairs={{0,16},{16,0},{1,17},{17,1},{2,18},{18,2},{3,19},{19,3},{4,20},{20... | collective-permute-start | bytes 1572872 | tf_op jit(solution)/shard_map/ppermute | solution.py:20
  98.0 8.3 %collective-permute-start.30 = (bf16[32,2048]{1,0:T(8,128)(2,1)S(1)}, bf16[32,2048]{1,0:T(8,128)(2,1)S(1)}, u32[]{:S(2)}, u32[]{:S(2)}) collective-permute-start(bf16[32,2048]{1,0:T(8,128)(2,1)S(1)} %get-tuple-element.52), channel_id=1, source_target_pairs={{0,3},{1,2},{2,1},{3,0},{4,7},{5,6},{6,5},{7,4},{8,11},{9,10},{10,... | collective-permute-start | bytes 393224 | tf_op jit(solution)/shard_map/ppermute | solution.py:20
  100.3 10.7 %collective-permute-start.31 = (bf16[32,2048]{1,0:T(8,128)(2,1)S(1)}, bf16[32,2048]{1,0:T(8,128)(2,1)S(1)}, u32[]{:S(2)}, u32[]{:S(2)}) collective-permute-start(bf16[32,2048]{1,0:T(8,128)(2,1)S(1)} %get-tuple-element.53), channel_id=1, source_target_pairs={{0,2},{1,3},{2,0},{3,1},{4,6},{5,7},{6,4},{7,5},{8,10},{9,11},{10,... | collective-permute-start | bytes 393224 | tf_op jit(solution)/shard_map/ppermute | solution.py:20
  100.3 10.7 %collective-permute-start.32 = (bf16[32,2048]{1,0:T(8,128)(2,1)S(1)}, bf16[32,2048]{1,0:T(8,128)(2,1)S(1)}, u32[]{:S(2)}, u32[]{:S(2)}) collective-permute-start(bf16[32,2048]{1,0:T(8,128)(2,1)S(1)} %get-tuple-element.54), channel_id=1, source_target_pairs={{0,1},{1,0},{2,3},{3,2},{4,5},{5,4},{6,7},{7,6},{8,9},{9,8},{10,11... | collective-permute-start | bytes 393224 | tf_op jit(solution)/shard_map/ppermute | solution.py:20

commit v3 on v1

--- a/solution.py
+++ b/solution.py
@@ -165,7 +165,7 @@
     )(*flat, weights, *after)
 
 
-def contract(blocks, pieces, weights, transposed, cores, n_pipe, n_tensor, after=()):
+def contract(blocks, pieces, weights, transposed, cores, n_pipe, n_tensor, cuts=1, after=()):
     kinds, _, units = blocks[0].shape
     n_in, n_after = len(blocks), len(after)
     from_rows = blocks[0].shape[1] // cores
@@ -174,32 +174,35 @@
     width = weights.shape[1] if transposed else weights.shape[2]
     tile = pick_tile(width)
     count = width // tile
+    cut_width = width // cuts
+    n_out = 1 + (cores - 1) * cuts
 
     def kernel(*refs):
         x_refs = refs[:n_in]
         held = refs[n_in]
-        out_refs = refs[n_in + 1 + n_after : n_in + 1 + n_after + cores]
-        natural, ordered = refs[n_in + 1 + n_after + cores :]
+        out_refs = refs[n_in + 1 + n_after : n_in + 1 + n_after + n_out]
+        natural, ordered = refs[n_in + 1 + n_after + n_out :]
         t = lax.axis_index("tensor")
         p = lax.axis_index("pipe")
 
-        def work(j, carry):
-            at = pl.multiple_of(j * tile, tile)
+        def work(j):
+            at = j * tile
             total = None
             for k in range(kinds):
                 if transposed:
                     part = lax.dot_general(
-                        ordered[k], held[k, pl.ds(at, tile), :], CONTRACT_LAST, preferred_element_type=F32
+                        ordered[k], held[k, at : at + tile, :], CONTRACT_LAST, preferred_element_type=F32
                     )
                 else:
                     part = jnp.dot(
-                        ordered[k], held[k, :, pl.ds(at, tile)], preferred_element_type=F32
+                        ordered[k], held[k, :, at : at + tile], preferred_element_type=F32
                     )
                 total = part if total is None else total + part
-            for a in range(cores):
-                part = total[a * tokens : (a + 1) * tokens]
-                out_refs[a][:, pl.ds(at, tile)] = part.astype(out_refs[a].dtype)
-            return carry
+            out_refs[0][:, at : at + tile] = total[:tokens]
+            if cores > 1:
+                ref = out_refs[1 + at // cut_width]
+                place = at % cut_width
+                ref[:, place : place + tile] = total[tokens:].astype(ref.dtype)
 
         def came(k, a, s):
             place, row = pieces[s][a]
@@ -219,15 +222,15 @@
                     start = pl.multiple_of((t ^ s) * to_rows, to_rows)
                     at = a * tokens + s * to_rows
                     ordered[k, at : at + to_rows, :] = natural[pl.ds(start, to_rows), :]
-        lax.fori_loop(0, count, work, 0, unroll=True)
+        for j in range(count):
+            work(j)
 
     return pl.pallas_call(
         kernel,
         in_specs=[IN_VMEM] * (n_in + 1) + [IN_PLACE] * n_after,
-        out_specs=[IN_VMEM] * cores,
-        out_shape=[
-            jax.ShapeDtypeStruct((tokens, width), BF16 if a else F32) for a in range(cores)
-        ],
+        out_specs=[IN_VMEM] * n_out,
+        out_shape=[jax.ShapeDtypeStruct((tokens, width), F32)]
+        + [jax.ShapeDtypeStruct((tokens, cut_width), BF16)] * (n_out - 1),
         scratch_shapes=[
             pltpu.VMEM((tokens, units), BF16),
             pltpu.VMEM((kinds, cores * tokens, units), BF16),
@@ -260,18 +263,22 @@
 
 def finish(partials, cores, n_tensor, after=()):
     if cores > 1:
-        other = exchange(partials[1], "dp", cores, 1)
-        rows, width = other.shape[0] // n_tensor, other.shape[1]
+        others = [exchange(x, "dp", cores, 1) for x in partials[1:]]
+        rows, width = partials[0].shape[0] // n_tensor, partials[0].shape[1]
+        cut = others[0].shape[1]
 
         def body(ins, outs):
             for s in range(n_tensor):
                 at = slice(s * rows, (s + 1) * rows)
-                outs[s][...] = (ins[0][at] + ins[1][at].astype(F32)).astype(outs[s].dtype)
+                for i, ref in enumerate(ins[1:]):
+                    columns = slice(i * cut, (i + 1) * cut)
+                    total = ins[0][at, columns] + ref[at].astype(F32)
+                    outs[s][:, columns] = total.astype(outs[s].dtype)
 
         parts = small_kernel(
             body,
             [((rows, width), BF16 if s else F32) for s in range(n_tensor)],
-            [partials[0], other],
+            [partials[0], *others],
             "add_core",
             after,
         )
@@ -337,7 +344,6 @@
         (BF16, [(3, 1), (2, 1)]),
     ]
     straight_pieces = [[(s, 0), (s, rows)] for s in range(n_pipe)]
-    balanced_pieces = straight_pieces[:3] + [[(3, 0), (4, 0)]]
 
 
     def swap(value, step):
@@ -412,22 +418,23 @@
         "slopes",
         after=[hidden],
     )
-    slopes_x, slopes_y = swap(slopes, x), swap(slopes, y)
+    slopes_all = [slopes] + [swap(slopes, s) for s in range(1, n_pipe)]
 
     out = contract(
-        hidden_all, straight_pieces, tall, False, cores, n_pipe, n_tensor, after=[slopes]
-    )
-    slopes_all = [
-        slopes,
-        slopes_x,
-        slopes_y,
-        swap(slopes_x[:, :rows], y),
-        swap(slopes_y[:, rows:], x),
-    ]
+        hidden_all,
+        straight_pieces,
+        tall,
+        False,
+        cores,
+        n_pipe,
+        n_tensor,
+        cuts=2,
+        after=[slopes],
+    )
     came, layer_output = finish(out, cores, n_tensor)
     back = contract(
         slopes_all,
-        balanced_pieces,
+        straight_pieces,
         wide,
         True,
         cores,
@@ -438,7 +445,7 @@
     def copy_body(ins, outs):
         outs[0][...] = ins[0][...]
 
-    (held,) = small_kernel(copy_body, [(back[1].shape, BF16)], back[1:], "hold", after=came[:1])
+    (held,) = small_kernel(copy_body, [(back[1].shape, BF16)], back[1:], "hold", after=came)
     _, input_grad = finish([back[0], held], cores, n_tensor)
     return layer_output, input_grad
 

time: 109 us -> 112 us (1.028)
  waiting for transfers between devices: 48.1 us -> 51.9 us
    ppermute x33, waiting for transfers between devices: 48.1 us -> 51.9 us  [exchange(): return lax.ppermute(value, axis, [(i, i ^ step) for i in range(size)])]
  transfers between devices with their start and end apart: 33 -> 33, of which waited for: 17 -> 18; matrix products, arithmetic and copies ran while one was open for 1% -> 1% of each run, Pallas kernels for 19% -> 18%
where the time goes in v3:
time: 112 us
  waiting for transfers between devices  51.9 us (46%)
  starting transfers between devices  37.1 us (33%)
  Pallas kernels  20.7 us (18%)
  other arithmetic  1.43 us (1%)
    ppermute x33, waiting for transfers between devices, exchange(): return lax.ppermute(value, axis, [(i, i ^ step) for i in range(size)])  51.9 us
    ppermute x33, starting transfers between devices, exchange(): return lax.ppermute(value, axis, [(i, i ^ step) for i in range(size)])  37.1 us
    pallas_call x1, Pallas kernels, load_weights(): pl.pallas_call(kernel, in_specs=[IN_PLACE] * 3, out_specs=[IN_VMEM] * 2,...  7.56 us
    pallas_call x2, Pallas kernels, contract(): pl.pallas_call(kernel, in_specs=[IN_VMEM] * (n_in + 1) + [IN_PLACE] * n_a...  6.13 us
    pallas_call x2, Pallas kernels, project(): pl.pallas_call(kernel, in_specs=[IN_VMEM] * (n_in + 1) + [IN_PLACE] * n_a...  6.11 us
  transfers between devices with their start and end apart: 33, of which 18 were waited for; matrix products, arithmetic and copies ran while one was open for 1% of the time, Pallas kernels for 18%

profile of v3, /device:TPU:0, one launch (start us, length us, event | category | flops | bytes accessed | tf_op | source)
XLA Modules:
  0.0 111.9 jit_solution(15736481932538681139)
XLA Ops:
  0.7 5.1 %collective-permute-start.2 = (bf16[32,2048]{1,0:T(8,128)(2,1)}, bf16[32,2048]{1,0:T(8,128)(2,1)S(1)}, u32[]{:S(2)}, u32[]{:S(2)}) collective-permute-start(bf16[32,2048]{1,0:T(8,128)(2,1)} %refs_0_.3), channel_id=1, source_target_pairs={{0,3},{1,2},{2,1},{3,0},{4,7},{5,6},{6,5},{7,4},{8,11},{9,10},{10,... | collective-permute-start | bytes 393224 | tf_op jit(solution)/shard_map/ppermute | solution.py:20
  5.8 0.6 collective-permute-start
  6.4 0.0 collective-permute-start.3
  6.4 1.4 %collective-permute-start.4 = (bf16[32,2048]{1,0:T(8,128)(2,1)}, bf16[32,2048]{1,0:T(8,128)(2,1)S(1)}, u32[]{:S(2)}, u32[]{:S(2)}) collective-permute-start(bf16[32,2048]{1,0:T(8,128)(2,1)} %refs_0_.5), channel_id=1, source_target_pairs={{0,1},{1,0},{2,3},{3,2},{4,5},{5,4},{6,7},{7,6},{8,9},{9,8},{10,11... | collective-permute-start | bytes 393224 | tf_op jit(solution)/shard_map/ppermute | solution.py:20
  7.8 7.6 %load_weights.1 = (bf16[2,2048,1792]{2,1,0:T(8,128)(2,1)S(1)}, bf16[1,1792,2048]{2,1,0:T(8,128)(2,1)S(1)}) custom-call(bf16[2048,3584]{1,0:T(8,128)(2,1)} %gate.1, bf16[2048,3584]{1,0:T(8,128)(2,1)} %up.1, bf16[3584,2048]{1,0:T(8,128)(2,1)} %down.1), custom_call_target="tpu_custom_call" | custom-call | bytes 22020096 | tf_op jit(solution)/shard_map/load_weights/pallas_call | solution.py:78
  15.4 0.0 copy-start
  15.4 0.0 copy-start.1
  15.4 0.0 collective-permute-done.2.refs_2_
  15.4 1.8 %collective-permute-done.1.refs_1_ = bf16[32,2048]{1,0:T(8,128)(2,1)S(1)} collective-permute-done((bf16[32,2048]{1,0:T(8,128)(2,1)}, bf16[32,2048]{1,0:T(8,128)(2,1)S(1)}, u32[]{:S(2)}, u32[]{:S(2)}) %collective-permute-start.1) | collective-permute-done | bytes 131104 | tf_op jit(solution)/shard_map/ppermute | solution.py:20
  17.2 0.0 collective-permute-done.refs_0_
  17.2 0.8 collective-permute-done.4.refs_5_.refs_0_
  18.0 0.1 collective-permute-start.5
  18.1 3.4 %collective-permute-start.9 = (bf16[32,2048]{1,0:T(8,128)(2,1)S(1)}, bf16[32,2048]{1,0:T(8,128)(2,1)S(1)}, u32[]{:S(2)}, u32[]{:S(2)}) collective-permute-start(bf16[32,2048]{1,0:T(8,128)(2,1)S(1)} %copy-done.3), channel_id=1, source_target_pairs={{0,3},{1,2},{2,1},{3,0},{4,7},{5,6},{6,5},{7,4},{8,11},{9,10},{10,... | collective-permute-start | bytes 393224 | tf_op jit(solution)/shard_map/ppermute | solution.py:20
  21.6 4.0 %project.1 = (f32[2,128,1792]{2,1,0:T(8,128)S(1)}, bf16[2,64,1792]{2,1,0:T(8,128)(2,1)S(1)}, bf16[2,64,1792]{2,1,0:T(8,128)(2,1)S(1)}) custom-call(bf16[32,2048]{1,0:T(8,128)(2,1)S(1)} %copy-done.2, bf16[96,2048]{1,0:T(8,128)(2,1)S(1)} %assemble.2.refs_1_, bf16[32,2048]{1,0:T(8,128)(2,1)S(1)} %collective-permute-done.3.refs_4_.refs_2_, ...), custom_call_target="tpu_custom_call" | custom-call | flops 3758096384 | bytes 14680064 | tf_op jit(solution)/shard_map/project/pallas_call | solution.py:150
  25.6 1.6 %collective-permute-start.6 = (bf16[2,64,1792]{2,1,0:T(8,128)(2,1)S(1)}, bf16[2,64,1792]{2,1,0:T(8,128)(2,1)S(1)}, u32[]{:S(2)}, u32[]{:S(2)}) collective-permute-start(bf16[2,64,1792]{2,1,0:T(8,128)(2,1)S(1)} %get-tuple-element.31), channel_id=1, source_target_pairs={{0,4},{4,0},{8,12},{12,8},{1,5},{5,1},{9,13},{13,9},{2,6},{6,2},{1... | collective-permute-start | bytes 1376264 | tf_op jit(solution)/shard_map/ppermute | solution.py:20
  27.1 1.5 %collective-permute-start.7 = (bf16[2,64,1792]{2,1,0:T(8,128)(2,1)S(1)}, bf16[2,64,1792]{2,1,0:T(8,128)(2,1)S(1)}, u32[]{:S(2)}, u32[]{:S(2)}) collective-permute-start(bf16[2,64,1792]{2,1,0:T(8,128)(2,1)S(1)} %get-tuple-element.32), channel_id=1, source_target_pairs={{0,8},{4,12},{8,0},{12,4},{1,9},{5,13},{9,1},{13,5},{2,10},{6,14},... | collective-permute-start | bytes 1376264 | tf_op jit(solution)/shard_map/ppermute | solution.py:20
  28.6 4.9 %collective-permute-done.8.refs_1_ = bf16[32,2048]{1,0:T(8,128)(2,1)S(1)} collective-permute-done((bf16[32,2048]{1,0:T(8,128)(2,1)S(1)}, bf16[32,2048]{1,0:T(8,128)(2,1)S(1)}, u32[]{:S(2)}, u32[]{:S(2)}) %collective-permute-start.8) | collective-permute-done | bytes 131104 | tf_op jit(solution)/shard_map/ppermute | solution.py:20
  33.6 0.1 collective-permute-start.11
  33.8 0.5 collective-permute-start.12
  34.3 0.1 collective-permute-start.10
  34.4 1.5 %collective-permute-done.10.refs_2_ = bf16[32,2048]{1,0:T(8,128)(2,1)S(1)} collective-permute-done((bf16[32,2048]{1,0:T(8,128)(2,1)S(1)}, bf16[32,2048]{1,0:T(8,128)(2,1)S(1)}, u32[]{:S(2)}, u32[]{:S(2)}) %collective-permute-start.10) | collective-permute-done | bytes 131104 | tf_op jit(solution)/shard_map/ppermute | solution.py:20
  35.9 2.1 %pull_back.1 = (f32[1,64,1792]{2,1,0:T(8,128)S(1)}, bf16[1,64,1792]{2,1,0:T(8,128)(2,1)S(1)}, bf16[1,64,1792]{2,1,0:T(8,128)(2,1)S(1)}, bf16[1,64,1792]{2,1,0:T(8,128)(2,1)S(1)}) custom-call(bf16[32,2048]{1,0:T(8,128)(2,1)S(1)} %copy-done.3, bf16[96,2048]{1,0:T(8,128)(2,1)S(1)} %assemble.3.refs_1_, bf16[32,2048]{1,0:T(8,128)(2,1)S(1)} %collective-permute-done.10.refs_2_, ...), custom_call_target="tpu_custom_call" | custom-call | tf_op jit(solution)/shard_map/pull_back/pallas_call | solution.py:150
  38.0 0.2 collective-permute-done.6.refs_1_
  38.2 1.2 %collective-permute-done.7.refs_2_ = bf16[2,64,1792]{2,1,0:T(8,128)(2,1)S(1)} collective-permute-done((bf16[2,64,1792]{2,1,0:T(8,128)(2,1)S(1)}, bf16[2,64,1792]{2,1,0:T(8,128)(2,1)S(1)}, u32[]{:S(2)}, u32[]{:S(2)}) %collective-permute-start.7) | collective-permute-done | bytes 458784 | tf_op jit(solution)/shard_map/ppermute | solution.py:20
  39.4 0.1 pass_on.1
  39.5 0.6 collective-permute-start.13
  40.1 1.5 %collective-permute-start.14 = (bf16[2,32,1792]{2,1,0:T(8,128)(2,1)S(1)}, bf16[2,32,1792]{2,1,0:T(8,128)(2,1)S(1)}, u32[]{:S(2)}, u32[]{:S(2)}) collective-permute-start(bf16[2,32,1792]{2,1,0:T(8,128)(2,1)S(1)} %get-tuple-element.36), channel_id=1, source_target_pairs={{0,8},{4,12},{8,0},{12,4},{1,9},{5,13},{9,1},{13,5},{2,10},{6,14},... | collective-permute-start | bytes 688136 | tf_op jit(solution)/shard_map/ppermute | solution.py:20
  41.6 1.4 %collective-permute-start.18 = (bf16[1,64,1792]{2,1,0:T(8,128)(2,1)S(1)}, bf16[1,64,1792]{2,1,0:T(8,128)(2,1)S(1)}, u32[]{:S(2)}, u32[]{:S(2)}) collective-permute-start(bf16[1,64,1792]{2,1,0:T(8,128)(2,1)S(1)} %get-tuple-element.37), channel_id=1, source_target_pairs={{0,12},{4,8},{8,4},{12,0},{1,13},{5,9},{9,5},{13,1},{2,14},{6,10},... | collective-permute-start | bytes 688136 | tf_op jit(solution)/shard_map/ppermute | solution.py:20
  43.1 0.5 collective-permute-start.19
  43.6 1.5 %collective-permute-start.20 = (bf16[1,64,1792]{2,1,0:T(8,128)(2,1)S(1)}, bf16[1,64,1792]{2,1,0:T(8,128)(2,1)S(1)}, u32[]{:S(2)}, u32[]{:S(2)}) collective-permute-start(bf16[1,64,1792]{2,1,0:T(8,128)(2,1)S(1)} %get-tuple-element.39), channel_id=1, source_target_pairs={{0,8},{4,12},{8,0},{12,4},{1,9},{5,13},{9,1},{13,5},{2,10},{6,14},... | collective-permute-start | bytes 688136 | tf_op jit(solution)/shard_map/ppermute | solution.py:20
  45.1 3.0 %collective-permute-done.13.refs_3_ = bf16[2,32,1792]{2,1,0:T(8,128)(2,1)S(1)} collective-permute-done((bf16[2,32,1792]{2,1,0:T(8,128)(2,1)S(1)}, bf16[2,32,1792]{2,1,0:T(8,128)(2,1)S(1)}, u32[]{:S(2)}, u32[]{:S(2)}) %collective-permute-start.13) | collective-permute-done | bytes 229408 | tf_op jit(solution)/shard_map/ppermute | solution.py:20
  48.1 5.0 %collective-permute-done.14.refs_4_ = bf16[2,32,1792]{2,1,0:T(8,128)(2,1)S(1)} collective-permute-done((bf16[2,32,1792]{2,1,0:T(8,128)(2,1)S(1)}, bf16[2,32,1792]{2,1,0:T(8,128)(2,1)S(1)}, u32[]{:S(2)}, u32[]{:S(2)}) %collective-permute-start.14) | collective-permute-done | bytes 229408 | tf_op jit(solution)/shard_map/ppermute | solution.py:20
  53.1 0.2 hidden.1.refs_6_.refs_0_
  53.3 2.9 %collective-permute-start.17 = (bf16[1,64,1792]{2,1,0:T(8,128)(2,1)S(1)}, bf16[1,64,1792]{2,1,0:T(8,128)(2,1)S(1)}, u32[]{:S(2)}, u32[]{:S(2)}) collective-permute-start(bf16[1,64,1792]{2,1,0:T(8,128)(2,1)S(1)} %hidden.1.refs_6_.refs_0_), channel_id=1, source_target_pairs={{0,12},{4,8},{8,4},{12,0},{1,13},{5,9},{9,5},{13,1},{2,14},{6,10},... | collective-permute-start | bytes 688136 | tf_op jit(solution)/shard_map/ppermute | solution.py:20
  56.2 0.5 collective-permute-start.16
  56.7 0.1 collective-permute-start.15
  56.9 1.1 collective-permute-done.19.refs_2_
  57.9 5.0 %collective-permute-done.20.refs_3_ = bf16[1,64,1792]{2,1,0:T(8,128)(2,1)S(1)} collective-permute-done((bf16[1,64,1792]{2,1,0:T(8,128)(2,1)S(1)}, bf16[1,64,1792]{2,1,0:T(8,128)(2,1)S(1)}, u32[]{:S(2)}, u32[]{:S(2)}) %collective-permute-start.20) | collective-permute-done | bytes 229408 | tf_op jit(solution)/shard_map/ppermute | solution.py:20
  63.0 0.3 slopes.1.refs_5_.refs_0_
  63.3 3.3 %collective-permute-start.28 = (bf16[2,64,1792]{2,1,0:T(8,128)(2,1)S(1)}, bf16[2,64,1792]{2,1,0:T(8,128)(2,1)S(1)}, u32[]{:S(2)}, u32[]{:S(2)}) collective-permute-start(bf16[2,64,1792]{2,1,0:T(8,128)(2,1)S(1)} %slopes.1.refs_5_.refs_0_), channel_id=1, source_target_pairs={{0,12},{4,8},{8,4},{12,0},{1,13},{5,9},{9,5},{13,1},{2,14},{6,10},... | collective-permute-start | bytes 1376264 | tf_op jit(solution)/shard_map/ppermute | solution.py:20
  66.6 0.1 collective-permute-start.27
  66.7 0.5 collective-permute-start.26
  67.2 10.4 %collective-permute-done.16.refs_2_ = bf16[1,64,1792]{2,1,0:T(8,128)(2,1)S(1)} collective-permute-done((bf16[1,64,1792]{2,1,0:T(8,128)(2,1)S(1)}, bf16[1,64,1792]{2,1,0:T(8,128)(2,1)S(1)}, u32[]{:S(2)}, u32[]{:S(2)}) %collective-permute-start.16) | collective-permute-done | bytes 229408 | tf_op jit(solution)/shard_map/ppermute | solution.py:20
  77.7 2.1 %layer_output.1 = (f32[128,2048]{1,0:T(8,128)S(1)}, bf16[128,1024]{1,0:T(8,128)(2,1)S(1)}, bf16[128,1024]{1,0:T(8,128)(2,1)S(1)}) custom-call(bf16[1,64,1792]{2,1,0:T(8,128)(2,1)S(1)} %hidden.1.refs_6_.refs_0_, bf16[1,64,1792]{2,1,0:T(8,128)(2,1)S(1)} %collective-permute-done.15.refs_1_, bf16[1,64,1792]{2,1,0:T(8,128)(2,1)S(1)} %collective-permute-done.16.refs_2_, ...), custom_call_target="tpu_custom_call" | custom-call | flops 1879048192 | bytes 7340032 | tf_op jit(solution)/shard_map/layer_output/pallas_call | solution.py:228
  79.8 0.1 collective-permute-start.21
  79.9 0.5 collective-permute-start.22
  80.4 1.0 collective-permute-done.21.refs_1_
  81.4 0.4 collective-permute-done.22.refs_2_
  81.8 0.1 add_core.2
  81.8 1.5 %collective-permute-start.23 = (bf16[32,2048]{1,0:T(8,128)(2,1)S(1)}, bf16[32,2048]{1,0:T(8,128)(2,1)S(1)}, u32[]{:S(2)}, u32[]{:S(2)}) collective-permute-start(bf16[32,2048]{1,0:T(8,128)(2,1)S(1)} %get-tuple-element.45), channel_id=1, source_target_pairs={{0,3},{1,2},{2,1},{3,0},{4,7},{5,6},{6,5},{7,4},{8,11},{9,10},{10,... | collective-permute-start | bytes 393224 | tf_op jit(solution)/shard_map/ppermute | solution.py:20
  83.3 0.3 collective-permute-start.24
  83.7 2.6 %collective-permute-start.25 = (bf16[32,2048]{1,0:T(8,128)(2,1)S(1)}, bf16[32,2048]{1,0:T(8,128)(2,1)S(1)}, u32[]{:S(2)}, u32[]{:S(2)}) collective-permute-start(bf16[32,2048]{1,0:T(8,128)(2,1)S(1)} %get-tuple-element.47), channel_id=1, source_target_pairs={{0,1},{1,0},{2,3},{3,2},{4,5},{5,4},{6,7},{7,6},{8,9},{9,8},{10,11... | collective-permute-start | bytes 393224 | tf_op jit(solution)/shard_map/ppermute | solution.py:20
  86.3 0.1 collective-permute-done.27.refs_2_
  86.4 4.0 %input_grad.1 = (f32[128,2048]{1,0:T(8,128)S(1)}, bf16[128,2048]{1,0:T(8,128)(2,1)S(1)}) custom-call(bf16[2,64,1792]{2,1,0:T(8,128)(2,1)S(1)} %slopes.1.refs_5_.refs_0_, bf16[2,64,1792]{2,1,0:T(8,128)(2,1)S(1)} %collective-permute-done.26.refs_1_, bf16[2,64,1792]{2,1,0:T(8,128)(2,1)S(1)} %collective-permute-done.27.refs_2_, ...), custom_call_target="tpu_custom_call" | custom-call | flops 3758096384 | bytes 14680064 | tf_op jit(solution)/shard_map/input_grad/pallas_call | solution.py:228
  90.4 5.4 %collective-permute-done.24.refs_2_ = bf16[32,2048]{1,0:T(8,128)(2,1)S(1)} collective-permute-done((bf16[32,2048]{1,0:T(8,128)(2,1)S(1)}, bf16[32,2048]{1,0:T(8,128)(2,1)S(1)}, u32[]{:S(2)}, u32[]{:S(2)}) %collective-permute-start.24) | collective-permute-done | bytes 131104 | tf_op jit(solution)/shard_map/ppermute | solution.py:20
  95.8 0.1 collective-permute-start.29
  95.9 1.9 %collective-permute-done.29.refs_1_ = bf16[128,2048]{1,0:T(8,128)(2,1)S(1)} collective-permute-done((bf16[128,2048]{1,0:T(8,128)(2,1)S(1)}, bf16[128,2048]{1,0:T(8,128)(2,1)S(1)}, u32[]{:S(2)}, u32[]{:S(2)}) %collective-permute-start.29) | collective-permute-done | bytes 524320 | tf_op jit(solution)/shard_map/ppermute | solution.py:20
  97.8 0.1 add_core.3
  97.9 2.7 %collective-permute-start.30 = (bf16[32,2048]{1,0:T(8,128)(2,1)S(1)}, bf16[32,2048]{1,0:T(8,128)(2,1)S(1)}, u32[]{:S(2)}, u32[]{:S(2)}) collective-permute-start(bf16[32,2048]{1,0:T(8,128)(2,1)S(1)} %get-tuple-element.51), channel_id=1, source_target_pairs={{0,3},{1,2},{2,1},{3,0},{4,7},{5,6},{6,5},{7,4},{8,11},{9,10},{10,... | collective-permute-start | bytes 393224 | tf_op jit(solution)/shard_map/ppermute | solution.py:20
  100.6 1.7 %collective-permute-start.32 = (bf16[32,2048]{1,0:T(8,128)(2,1)S(1)}, bf16[32,2048]{1,0:T(8,128)(2,1)S(1)}, u32[]{:S(2)}, u32[]{:S(2)}) collective-permute-start(bf16[32,2048]{1,0:T(8,128)(2,1)S(1)} %get-tuple-element.53), channel_id=1, source_target_pairs={{0,1},{1,0},{2,3},{3,2},{4,5},{5,4},{6,7},{7,6},{8,9},{9,8},{10,11... | collective-permute-start | bytes 393224 | tf_op jit(solution)/shard_map/ppermute | solution.py:20
  102.4 0.7 add_convert_fusion.1
  103.1 3.1 %collective-permute-done.30 = bf16[32,2048]{1,0:T(8,128)(2,1)S(1)} collective-permute-done((bf16[32,2048]{1,0:T(8,128)(2,1)S(1)}, bf16[32,2048]{1,0:T(8,128)(2,1)S(1)}, u32[]{:S(2)}, u32[]{:S(2)}) %collective-permute-start.30) | collective-permute-done | bytes 131104 | tf_op jit(solution)/shard_map/ppermute | solution.py:20
  106.2 5.0 %collective-permute-done.31 = bf16[32,2048]{1,0:T(8,128)(2,1)S(1)} collective-permute-done((bf16[32,2048]{1,0:T(8,128)(2,1)S(1)}, bf16[32,2048]{1,0:T(8,128)(2,1)S(1)}, u32[]{:S(2)}, u32[]{:S(2)}) %collective-permute-start.31) | collective-permute-done | bytes 131104 | tf_op jit(solution)/shard_map/ppermute | solution.py:20
  111.2 0.7 add_convert_fusion
  (26 shorter events, 0.2 us)
Async XLA Ops:
  0.6 20.9 %copy-start.2 = (bf16[32,2048]{1,0:T(8,128)(2,1)S(1)}, bf16[32,2048]{1,0:T(8,128)(2,1)}, u32[]{:S(2)}) copy-start(bf16[32,2048]{1,0:T(8,128)(2,1)} %refs_0_.3) | copy-start | bytes 393220
  0.6 17.5 %copy-start.3 = (bf16[32,2048]{1,0:T(8,128)(2,1)S(1)}, bf16[32,2048]{1,0:T(8,128)(2,1)}, u32[]{:S(2)}) copy-start(bf16[32,2048]{1,0:T(8,128)(2,1)} %refs_0_.5) | copy-start | bytes 393220
  0.7 14.7 %collective-permute-start.2 = (bf16[32,2048]{1,0:T(8,128)(2,1)}, bf16[32,2048]{1,0:T(8,128)(2,1)S(1)}, u32[]{:S(2)}, u32[]{:S(2)}) collective-permute-start(bf16[32,2048]{1,0:T(8,128)(2,1)} %refs_0_.3), channel_id=1, source_target_pairs={{0,3},{1,2},{2,1},{3,0},{4,7},{5,6},{6,5},{7,4},{8,11},{9,10},{10,... | collective-permute-start | bytes 393224 | tf_op jit(solution)/shard_map/ppermute | solution.py:20
  5.8 11.4 %collective-permute-start.1 = (bf16[32,2048]{1,0:T(8,128)(2,1)}, bf16[32,2048]{1,0:T(8,128)(2,1)S(1)}, u32[]{:S(2)}, u32[]{:S(2)}) collective-permute-start(bf16[32,2048]{1,0:T(8,128)(2,1)} %refs_0_.3), channel_id=1, source_target_pairs={{0,2},{1,3},{2,0},{3,1},{4,6},{5,7},{6,4},{7,5},{8,10},{9,11},{10,... | collective-permute-start | bytes 393224 | tf_op jit(solution)/shard_map/ppermute | solution.py:20
  5.8 11.4 %collective-permute-start = (bf16[32,2048]{1,0:T(8,128)(2,1)}, bf16[32,2048]{1,0:T(8,128)(2,1)S(1)}, u32[]{:S(2)}, u32[]{:S(2)}) collective-permute-start(bf16[32,2048]{1,0:T(8,128)(2,1)} %refs_0_.3), channel_id=1, source_target_pairs={{0,1},{1,0},{2,3},{3,2},{4,5},{5,4},{6,7},{7,6},{8,9},{9,8},{10,11... | collective-permute-start | bytes 393224 | tf_op jit(solution)/shard_map/ppermute | solution.py:20
  6.4 10.8 %collective-permute-start.3 = (bf16[32,2048]{1,0:T(8,128)(2,1)}, bf16[32,2048]{1,0:T(8,128)(2,1)S(1)}, u32[]{:S(2)}, u32[]{:S(2)}) collective-permute-start(bf16[32,2048]{1,0:T(8,128)(2,1)} %refs_0_.3), channel_id=1, source_target_pairs={{0,16},{16,0},{1,17},{17,1},{2,18},{18,2},{3,19},{19,3},{4,20},{20... | collective-permute-start | bytes 393224 | tf_op jit(solution)/shard_map/ppermute | solution.py:20
  6.4 11.6 %collective-permute-start.4 = (bf16[32,2048]{1,0:T(8,128)(2,1)}, bf16[32,2048]{1,0:T(8,128)(2,1)S(1)}, u32[]{:S(2)}, u32[]{:S(2)}) collective-permute-start(bf16[32,2048]{1,0:T(8,128)(2,1)} %refs_0_.5), channel_id=1, source_target_pairs={{0,1},{1,0},{2,3},{3,2},{4,5},{5,4},{6,7},{7,6},{8,9},{9,8},{10,11... | collective-permute-start | bytes 393224 | tf_op jit(solution)/shard_map/ppermute | solution.py:20
  15.4 18.3 %copy-start = (bf16[32,3584]{1,0:T(8,128)(2,1)S(1)}, bf16[32,3584]{1,0:T(8,128)(2,1)}, u32[]{:S(2)}) copy-start(bf16[32,3584]{1,0:T(8,128)(2,1)} %refs_0_.4) | copy-start | bytes 688132
  15.4 18.3 %copy-start.1 = (bf16[32,3584]{1,0:T(8,128)(2,1)S(1)}, bf16[32,3584]{1,0:T(8,128)(2,1)}, u32[]{:S(2)}) copy-start(bf16[32,3584]{1,0:T(8,128)(2,1)} %refs_1_.1) | copy-start | bytes 688132
  18.0 3.5 %collective-permute-start.5 = (bf16[96,2048]{1,0:T(8,128)(2,1)S(1)}, bf16[96,2048]{1,0:T(8,128)(2,1)S(1)}, u32[]{:S(2)}, u32[]{:S(2)}) collective-permute-start(bf16[96,2048]{1,0:T(8,128)(2,1)S(1)} %assemble.2.refs_1_), channel_id=1, source_target_pairs={{0,16},{16,0},{1,17},{17,1},{2,18},{18,2},{3,19},{19,3},{4,20},{20... | collective-permute-start | bytes 1179656 | tf_op jit(solution)/shard_map/ppermute | solution.py:20
  18.1 10.5 %collective-permute-start.9 = (bf16[32,2048]{1,0:T(8,128)(2,1)S(1)}, bf16[32,2048]{1,0:T(8,128)(2,1)S(1)}, u32[]{:S(2)}, u32[]{:S(2)}) collective-permute-start(bf16[32,2048]{1,0:T(8,128)(2,1)S(1)} %copy-done.3), channel_id=1, source_target_pairs={{0,3},{1,2},{2,1},{3,0},{4,7},{5,6},{6,5},{7,4},{8,11},{9,10},{10,... | collective-permute-start | bytes 393224 | tf_op jit(solution)/shard_map/ppermute | solution.py:20
  21.5 12.0 %collective-permute-start.8 = (bf16[32,2048]{1,0:T(8,128)(2,1)S(1)}, bf16[32,2048]{1,0:T(8,128)(2,1)S(1)}, u32[]{:S(2)}, u32[]{:S(2)}) collective-permute-start(bf16[32,2048]{1,0:T(8,128)(2,1)S(1)} %copy-done.3), channel_id=1, source_target_pairs={{0,2},{1,3},{2,0},{3,1},{4,6},{5,7},{6,4},{7,5},{8,10},{9,11},{10,... | collective-permute-start | bytes 393224 | tf_op jit(solution)/shard_map/ppermute | solution.py:20
  25.6 12.6 %collective-permute-start.6 = (bf16[2,64,1792]{2,1,0:T(8,128)(2,1)S(1)}, bf16[2,64,1792]{2,1,0:T(8,128)(2,1)S(1)}, u32[]{:S(2)}, u32[]{:S(2)}) collective-permute-start(bf16[2,64,1792]{2,1,0:T(8,128)(2,1)S(1)} %get-tuple-element.31), channel_id=1, source_target_pairs={{0,4},{4,0},{8,12},{12,8},{1,5},{5,1},{9,13},{13,9},{2,6},{6,2},{1... | collective-permute-start | bytes 1376264 | tf_op jit(solution)/shard_map/ppermute | solution.py:20
  27.1 12.3 %collective-permute-start.7 = (bf16[2,64,1792]{2,1,0:T(8,128)(2,1)S(1)}, bf16[2,64,1792]{2,1,0:T(8,128)(2,1)S(1)}, u32[]{:S(2)}, u32[]{:S(2)}) collective-permute-start(bf16[2,64,1792]{2,1,0:T(8,128)(2,1)S(1)} %get-tuple-element.32), channel_id=1, source_target_pairs={{0,8},{4,12},{8,0},{12,4},{1,9},{5,13},{9,1},{13,5},{2,10},{6,14},... | collective-permute-start | bytes 1376264 | tf_op jit(solution)/shard_map/ppermute | solution.py:20
  33.6 2.3 %collective-permute-start.11 = (bf16[96,2048]{1,0:T(8,128)(2,1)S(1)}, bf16[96,2048]{1,0:T(8,128)(2,1)S(1)}, u32[]{:S(2)}, u32[]{:S(2)}) collective-permute-start(bf16[96,2048]{1,0:T(8,128)(2,1)S(1)} %assemble.3.refs_1_), channel_id=1, source_target_pairs={{0,16},{16,0},{1,17},{17,1},{2,18},{18,2},{3,19},{19,3},{4,20},{20... | collective-permute-start | bytes 1179656 | tf_op jit(solution)/shard_map/ppermute | solution.py:20
  33.8 2.2 %collective-permute-start.12 = (bf16[2,32,1792]{2,1,0:T(8,128)(2,1)S(1)}, bf16[2,32,1792]{2,1,0:T(8,128)(2,1)S(1)}, u32[]{:S(2)}, u32[]{:S(2)}) collective-permute-start(bf16[2,32,1792]{2,1,0:T(8,128)(2,1)S(1)} %get-tuple-element.33), channel_id=1, source_target_pairs={{0,16},{16,0},{1,17},{17,1},{2,18},{18,2},{3,19},{19,3},{4,20},{20... | collective-permute-start | bytes 688136 | tf_op jit(solution)/shard_map/ppermute | solution.py:20
  34.3 1.6 %collective-permute-start.10 = (bf16[32,2048]{1,0:T(8,128)(2,1)S(1)}, bf16[32,2048]{1,0:T(8,128)(2,1)S(1)}, u32[]{:S(2)}, u32[]{:S(2)}) collective-permute-start(bf16[32,2048]{1,0:T(8,128)(2,1)S(1)} %copy-done.3), channel_id=1, source_target_pairs={{0,16},{16,0},{1,17},{17,1},{2,18},{18,2},{3,19},{19,3},{4,20},{20... | collective-permute-start | bytes 393224 | tf_op jit(solution)/shard_map/ppermute | solution.py:20
  39.5 8.6 %collective-permute-start.13 = (bf16[2,32,1792]{2,1,0:T(8,128)(2,1)S(1)}, bf16[2,32,1792]{2,1,0:T(8,128)(2,1)S(1)}, u32[]{:S(2)}, u32[]{:S(2)}) collective-permute-start(bf16[2,32,1792]{2,1,0:T(8,128)(2,1)S(1)} %get-tuple-element.35), channel_id=1, source_target_pairs={{0,4},{4,0},{8,12},{12,8},{1,5},{5,1},{9,13},{13,9},{2,6},{6,2},{1... | collective-permute-start | bytes 688136 | tf_op jit(solution)/shard_map/ppermute | solution.py:20
  40.1 13.0 %collective-permute-start.14 = (bf16[2,32,1792]{2,1,0:T(8,128)(2,1)S(1)}, bf16[2,32,1792]{2,1,0:T(8,128)(2,1)S(1)}, u32[]{:S(2)}, u32[]{:S(2)}) collective-permute-start(bf16[2,32,1792]{2,1,0:T(8,128)(2,1)S(1)} %get-tuple-element.36), channel_id=1, source_target_pairs={{0,8},{4,12},{8,0},{12,4},{1,9},{5,13},{9,1},{13,5},{2,10},{6,14},... | collective-permute-start | bytes 688136 | tf_op jit(solution)/shard_map/ppermute | solution.py:20
  41.6 15.1 %collective-permute-start.18 = (bf16[1,64,1792]{2,1,0:T(8,128)(2,1)S(1)}, bf16[1,64,1792]{2,1,0:T(8,128)(2,1)S(1)}, u32[]{:S(2)}, u32[]{:S(2)}) collective-permute-start(bf16[1,64,1792]{2,1,0:T(8,128)(2,1)S(1)} %get-tuple-element.37), channel_id=1, source_target_pairs={{0,12},{4,8},{8,4},{12,0},{1,13},{5,9},{9,5},{13,1},{2,14},{6,10},... | collective-permute-start | bytes 688136 | tf_op jit(solution)/shard_map/ppermute | solution.py:20
  43.1 14.9 %collective-permute-start.19 = (bf16[1,64,1792]{2,1,0:T(8,128)(2,1)S(1)}, bf16[1,64,1792]{2,1,0:T(8,128)(2,1)S(1)}, u32[]{:S(2)}, u32[]{:S(2)}) collective-permute-start(bf16[1,64,1792]{2,1,0:T(8,128)(2,1)S(1)} %get-tuple-element.38), channel_id=1, source_target_pairs={{0,4},{4,0},{8,12},{12,8},{1,5},{5,1},{9,13},{13,9},{2,6},{6,2},{1... | collective-permute-start | bytes 688136 | tf_op jit(solution)/shard_map/ppermute | solution.py:20
  43.6 19.4 %collective-permute-start.20 = (bf16[1,64,1792]{2,1,0:T(8,128)(2,1)S(1)}, bf16[1,64,1792]{2,1,0:T(8,128)(2,1)S(1)}, u32[]{:S(2)}, u32[]{:S(2)}) collective-permute-start(bf16[1,64,1792]{2,1,0:T(8,128)(2,1)S(1)} %get-tuple-element.39), channel_id=1, source_target_pairs={{0,8},{4,12},{8,0},{12,4},{1,9},{5,13},{9,1},{13,5},{2,10},{6,14},... | collective-permute-start | bytes 688136 | tf_op jit(solution)/shard_map/ppermute | solution.py:20
  53.3 13.4 %collective-permute-start.17 = (bf16[1,64,1792]{2,1,0:T(8,128)(2,1)S(1)}, bf16[1,64,1792]{2,1,0:T(8,128)(2,1)S(1)}, u32[]{:S(2)}, u32[]{:S(2)}) collective-permute-start(bf16[1,64,1792]{2,1,0:T(8,128)(2,1)S(1)} %hidden.1.refs_6_.refs_0_), channel_id=1, source_target_pairs={{0,12},{4,8},{8,4},{12,0},{1,13},{5,9},{9,5},{13,1},{2,14},{6,10},... | collective-permute-start | bytes 688136 | tf_op jit(solution)/shard_map/ppermute | solution.py:20
  56.2 21.4 %collective-permute-start.16 = (bf16[1,64,1792]{2,1,0:T(8,128)(2,1)S(1)}, bf16[1,64,1792]{2,1,0:T(8,128)(2,1)S(1)}, u32[]{:S(2)}, u32[]{:S(2)}) collective-permute-start(bf16[1,64,1792]{2,1,0:T(8,128)(2,1)S(1)} %hidden.1.refs_6_.refs_0_), channel_id=1, source_target_pairs={{0,8},{4,12},{8,0},{12,4},{1,9},{5,13},{9,1},{13,5},{2,10},{6,14},... | collective-permute-start | bytes 688136 | tf_op jit(solution)/shard_map/ppermute | solution.py:20
  56.7 20.9 %collective-permute-start.15 = (bf16[1,64,1792]{2,1,0:T(8,128)(2,1)S(1)}, bf16[1,64,1792]{2,1,0:T(8,128)(2,1)S(1)}, u32[]{:S(2)}, u32[]{:S(2)}) collective-permute-start(bf16[1,64,1792]{2,1,0:T(8,128)(2,1)S(1)} %hidden.1.refs_6_.refs_0_), channel_id=1, source_target_pairs={{0,4},{4,0},{8,12},{12,8},{1,5},{5,1},{9,13},{13,9},{2,6},{6,2},{1... | collective-permute-start | bytes 688136 | tf_op jit(solution)/shard_map/ppermute | solution.py:20
  63.3 20.4 %collective-permute-start.28 = (bf16[2,64,1792]{2,1,0:T(8,128)(2,1)S(1)}, bf16[2,64,1792]{2,1,0:T(8,128)(2,1)S(1)}, u32[]{:S(2)}, u32[]{:S(2)}) collective-permute-start(bf16[2,64,1792]{2,1,0:T(8,128)(2,1)S(1)} %slopes.1.refs_5_.refs_0_), channel_id=1, source_target_pairs={{0,12},{4,8},{8,4},{12,0},{1,13},{5,9},{9,5},{13,1},{2,14},{6,10},... | collective-permute-start | bytes 1376264 | tf_op jit(solution)/shard_map/ppermute | solution.py:20
  66.6 19.8 %collective-permute-start.27 = (bf16[2,64,1792]{2,1,0:T(8,128)(2,1)S(1)}, bf16[2,64,1792]{2,1,0:T(8,128)(2,1)S(1)}, u32[]{:S(2)}, u32[]{:S(2)}) collective-permute-start(bf16[2,64,1792]{2,1,0:T(8,128)(2,1)S(1)} %slopes.1.refs_5_.refs_0_), channel_id=1, source_target_pairs={{0,8},{4,12},{8,0},{12,4},{1,9},{5,13},{9,1},{13,5},{2,10},{6,14},... | collective-permute-start | bytes 1376264 | tf_op jit(solution)/shard_map/ppermute | solution.py:20
  66.7 19.7 %collective-permute-start.26 = (bf16[2,64,1792]{2,1,0:T(8,128)(2,1)S(1)}, bf16[2,64,1792]{2,1,0:T(8,128)(2,1)S(1)}, u32[]{:S(2)}, u32[]{:S(2)}) collective-permute-start(bf16[2,64,1792]{2,1,0:T(8,128)(2,1)S(1)} %slopes.1.refs_5_.refs_0_), channel_id=1, source_target_pairs={{0,4},{4,0},{8,12},{12,8},{1,5},{5,1},{9,13},{13,9},{2,6},{6,2},{1... | collective-permute-start | bytes 1376264 | tf_op jit(solution)/shard_map/ppermute | solution.py:20
  79.8 1.6 %collective-permute-start.21 = (bf16[128,1024]{1,0:T(8,128)(2,1)S(1)}, bf16[128,1024]{1,0:T(8,128)(2,1)S(1)}, u32[]{:S(2)}, u32[]{:S(2)}) collective-permute-start(bf16[128,1024]{1,0:T(8,128)(2,1)S(1)} %get-tuple-element.42), channel_id=1, source_target_pairs={{0,16},{16,0},{1,17},{17,1},{2,18},{18,2},{3,19},{19,3},{4,20},{20... | collective-permute-start | bytes 786440 | tf_op jit(solution)/shard_map/ppermute | solution.py:20
  79.9 1.9 %collective-permute-start.22 = (bf16[128,1024]{1,0:T(8,128)(2,1)S(1)}, bf16[128,1024]{1,0:T(8,128)(2,1)S(1)}, u32[]{:S(2)}, u32[]{:S(2)}) collective-permute-start(bf16[128,1024]{1,0:T(8,128)(2,1)S(1)} %get-tuple-element.43), channel_id=1, source_target_pairs={{0,16},{16,0},{1,17},{17,1},{2,18},{18,2},{3,19},{19,3},{4,20},{20... | collective-permute-start | bytes 786440 | tf_op jit(solution)/shard_map/ppermute | solution.py:20
  81.8 8.6 %collective-permute-start.23 = (bf16[32,2048]{1,0:T(8,128)(2,1)S(1)}, bf16[32,2048]{1,0:T(8,128)(2,1)S(1)}, u32[]{:S(2)}, u32[]{:S(2)}) collective-permute-start(bf16[32,2048]{1,0:T(8,128)(2,1)S(1)} %get-tuple-element.45), channel_id=1, source_target_pairs={{0,3},{1,2},{2,1},{3,0},{4,7},{5,6},{6,5},{7,4},{8,11},{9,10},{10,... | collective-permute-start | bytes 393224 | tf_op jit(solution)/shard_map/ppermute | solution.py:20
  83.3 12.5 %collective-permute-start.24 = (bf16[32,2048]{1,0:T(8,128)(2,1)S(1)}, bf16[32,2048]{1,0:T(8,128)(2,1)S(1)}, u32[]{:S(2)}, u32[]{:S(2)}) collective-permute-start(bf16[32,2048]{1,0:T(8,128)(2,1)S(1)} %get-tuple-element.46), channel_id=1, source_target_pairs={{0,2},{1,3},{2,0},{3,1},{4,6},{5,7},{6,4},{7,5},{8,10},{9,11},{10,... | collective-permute-start | bytes 393224 | tf_op jit(solution)/shard_map/ppermute | solution.py:20
  83.7 12.1 %collective-permute-start.25 = (bf16[32,2048]{1,0:T(8,128)(2,1)S(1)}, bf16[32,2048]{1,0:T(8,128)(2,1)S(1)}, u32[]{:S(2)}, u32[]{:S(2)}) collective-permute-start(bf16[32,2048]{1,0:T(8,128)(2,1)S(1)} %get-tuple-element.47), channel_id=1, source_target_pairs={{0,1},{1,0},{2,3},{3,2},{4,5},{5,4},{6,7},{7,6},{8,9},{9,8},{10,11... | collective-permute-start | bytes 393224 | tf_op jit(solution)/shard_map/ppermute | solution.py:20
  95.8 2.0 %collective-permute-start.29 = (bf16[128,2048]{1,0:T(8,128)(2,1)S(1)}, bf16[128,2048]{1,0:T(8,128)(2,1)S(1)}, u32[]{:S(2)}, u32[]{:S(2)}) collective-permute-start(bf16[128,2048]{1,0:T(8,128)(2,1)S(1)} %hold.1), channel_id=1, source_target_pairs={{0,16},{16,0},{1,17},{17,1},{2,18},{18,2},{3,19},{19,3},{4,20},{20... | collective-permute-start | bytes 1572872 | tf_op jit(solution)/shard_map/ppermute | solution.py:20
  97.9 8.3 %collective-permute-start.30 = (bf16[32,2048]{1,0:T(8,128)(2,1)S(1)}, bf16[32,2048]{1,0:T(8,128)(2,1)S(1)}, u32[]{:S(2)}, u32[]{:S(2)}) collective-permute-start(bf16[32,2048]{1,0:T(8,128)(2,1)S(1)} %get-tuple-element.51), channel_id=1, source_target_pairs={{0,3},{1,2},{2,1},{3,0},{4,7},{5,6},{6,5},{7,4},{8,11},{9,10},{10,... | collective-permute-start | bytes 393224 | tf_op jit(solution)/shard_map/ppermute | solution.py:20
  100.6 10.6 %collective-permute-start.31 = (bf16[32,2048]{1,0:T(8,128)(2,1)S(1)}, bf16[32,2048]{1,0:T(8,128)(2,1)S(1)}, u32[]{:S(2)}, u32[]{:S(2)}) collective-permute-start(bf16[32,2048]{1,0:T(8,128)(2,1)S(1)} %get-tuple-element.52), channel_id=1, source_target_pairs={{0,2},{1,3},{2,0},{3,1},{4,6},{5,7},{6,4},{7,5},{8,10},{9,11},{10,... | collective-permute-start | bytes 393224 | tf_op jit(solution)/shard_map/ppermute | solution.py:20
  100.6 10.6 %collective-permute-start.32 = (bf16[32,2048]{1,0:T(8,128)(2,1)S(1)}, bf16[32,2048]{1,0:T(8,128)(2,1)S(1)}, u32[]{:S(2)}, u32[]{:S(2)}) collective-permute-start(bf16[32,2048]{1,0:T(8,128)(2,1)S(1)} %get-tuple-element.53), channel_id=1, source_target_pairs={{0,1},{1,0},{2,3},{3,2},{4,5},{5,4},{6,7},{7,6},{8,9},{9,8},{10,11... | collective-permute-start | bytes 393224 | tf_op jit(solution)/shard_map/ppermute | solution.py:20

commit v4 on v1

--- a/solution.py
+++ b/solution.py
@@ -403,7 +403,9 @@
     )
     sums = [keep, came_x, came_y, swap(on_x, x), swap(on_y, y)]
     (hidden,) = small_kernel(hidden_body, [((1, cores * rows, units), BF16)], sums, "hidden")
-    hidden_all = [hidden] + [swap(hidden, s) for s in range(1, n_pipe)]
+    order = (2, 3, 1)
+    hidden_all = [hidden] + [swap(hidden, s) for s in order]
+    hidden_pieces = [straight_pieces[0]] + [straight_pieces[order.index(s) + 1] for s in (1, 2, 3)]
 
     (slopes,) = small_kernel(
         slopes_body,
@@ -415,7 +417,7 @@
     slopes_x, slopes_y = swap(slopes, x), swap(slopes, y)
 
     out = contract(
-        hidden_all, straight_pieces, tall, False, cores, n_pipe, n_tensor, after=[slopes]
+        hidden_all, hidden_pieces, tall, False, cores, n_pipe, n_tensor, after=[slopes]
     )
     slopes_all = [
         slopes,
@@ -438,7 +440,7 @@
     def copy_body(ins, outs):
         outs[0][...] = ins[0][...]
 
-    (held,) = small_kernel(copy_body, [(back[1].shape, BF16)], back[1:], "hold", after=came[:1])
+    (held,) = small_kernel(copy_body, [(back[1].shape, BF16)], back[1:], "hold", after=came)
     _, input_grad = finish([back[0], held], cores, n_tensor)
     return layer_output, input_grad
 

time: 109 us -> 107 us (0.982)
  waiting for transfers between devices: 48.1 us -> 45.6 us
    ppermute x33, waiting for transfers between devices: 48.1 us -> 45.6 us  [exchange(): return lax.ppermute(value, axis, [(i, i ^ step) for i in range(size)])]
  transfers between devices with their start and end apart: 33 -> 33, of which waited for: 17 -> 18; matrix products, arithmetic and copies ran while one was open for 1% -> 1% of each run, Pallas kernels for 19% -> 19%
where the time goes in v4:
time: 107 us
  waiting for transfers between devices  45.6 us (43%)
  starting transfers between devices  38.1 us (36%)
  Pallas kernels  20.7 us (19%)
  other arithmetic  1.43 us (1%)
    ppermute x33, waiting for transfers between devices, exchange(): return lax.ppermute(value, axis, [(i, i ^ step) for i in range(size)])  45.6 us
    ppermute x33, starting transfers between devices, exchange(): return lax.ppermute(value, axis, [(i, i ^ step) for i in range(size)])  38.1 us
    pallas_call x1, Pallas kernels, load_weights(): pl.pallas_call(kernel, in_specs=[IN_PLACE] * 3, out_specs=[IN_VMEM] * 2,...  7.56 us
    pallas_call x2, Pallas kernels, contract(): pl.pallas_call(kernel, in_specs=[IN_VMEM] * (n_in + 1) + [IN_PLACE] * n_a...  6.13 us
    pallas_call x2, Pallas kernels, project(): pl.pallas_call(kernel, in_specs=[IN_VMEM] * (n_in + 1) + [IN_PLACE] * n_a...  6.11 us
  transfers between devices with their start and end apart: 33, of which 18 were waited for; matrix products, arithmetic and copies ran while one was open for 1% of the time, Pallas kernels for 19%

profile of v4, /device:TPU:0, one launch (start us, length us, event | category | flops | bytes accessed | tf_op | source)
XLA Modules:
  0.0 106.7 jit_solution(11071293611396083450)
XLA Ops:
  0.7 5.1 %collective-permute-start.2 = (bf16[32,2048]{1,0:T(8,128)(2,1)}, bf16[32,2048]{1,0:T(8,128)(2,1)S(1)}, u32[]{:S(2)}, u32[]{:S(2)}) collective-permute-start(bf16[32,2048]{1,0:T(8,128)(2,1)} %refs_0_.3), channel_id=1, source_target_pairs={{0,3},{1,2},{2,1},{3,0},{4,7},{5,6},{6,5},{7,4},{8,11},{9,10},{10,... | collective-permute-start | bytes 393224 | tf_op jit(solution)/shard_map/ppermute | solution.py:20
  5.8 0.6 collective-permute-start
  6.4 0.0 collective-permute-start.3
  6.4 1.4 %collective-permute-start.4 = (bf16[32,2048]{1,0:T(8,128)(2,1)}, bf16[32,2048]{1,0:T(8,128)(2,1)S(1)}, u32[]{:S(2)}, u32[]{:S(2)}) collective-permute-start(bf16[32,2048]{1,0:T(8,128)(2,1)} %refs_0_.5), channel_id=1, source_target_pairs={{0,1},{1,0},{2,3},{3,2},{4,5},{5,4},{6,7},{7,6},{8,9},{9,8},{10,11... | collective-permute-start | bytes 393224 | tf_op jit(solution)/shard_map/ppermute | solution.py:20
  7.8 7.6 %load_weights.1 = (bf16[2,2048,1792]{2,1,0:T(8,128)(2,1)S(1)}, bf16[1,1792,2048]{2,1,0:T(8,128)(2,1)S(1)}) custom-call(bf16[2048,3584]{1,0:T(8,128)(2,1)} %gate.1, bf16[2048,3584]{1,0:T(8,128)(2,1)} %up.1, bf16[3584,2048]{1,0:T(8,128)(2,1)} %down.1), custom_call_target="tpu_custom_call" | custom-call | bytes 22020096 | tf_op jit(solution)/shard_map/load_weights/pallas_call | solution.py:78
  15.4 0.0 copy-start
  15.4 0.0 copy-start.1
  15.4 0.0 collective-permute-done.2.refs_2_
  15.4 1.8 %collective-permute-done.1.refs_1_ = bf16[32,2048]{1,0:T(8,128)(2,1)S(1)} collective-permute-done((bf16[32,2048]{1,0:T(8,128)(2,1)}, bf16[32,2048]{1,0:T(8,128)(2,1)S(1)}, u32[]{:S(2)}, u32[]{:S(2)}) %collective-permute-start.1) | collective-permute-done | bytes 131104 | tf_op jit(solution)/shard_map/ppermute | solution.py:20
  17.2 0.0 collective-permute-done.refs_0_
  17.2 0.8 collective-permute-done.4.refs_5_.refs_0_
  18.0 0.1 collective-permute-start.5
  18.1 3.4 %collective-permute-start.9 = (bf16[32,2048]{1,0:T(8,128)(2,1)S(1)}, bf16[32,2048]{1,0:T(8,128)(2,1)S(1)}, u32[]{:S(2)}, u32[]{:S(2)}) collective-permute-start(bf16[32,2048]{1,0:T(8,128)(2,1)S(1)} %copy-done.3), channel_id=1, source_target_pairs={{0,3},{1,2},{2,1},{3,0},{4,7},{5,6},{6,5},{7,4},{8,11},{9,10},{10,... | collective-permute-start | bytes 393224 | tf_op jit(solution)/shard_map/ppermute | solution.py:20
  21.6 4.0 %project.1 = (f32[2,128,1792]{2,1,0:T(8,128)S(1)}, bf16[2,64,1792]{2,1,0:T(8,128)(2,1)S(1)}, bf16[2,64,1792]{2,1,0:T(8,128)(2,1)S(1)}) custom-call(bf16[32,2048]{1,0:T(8,128)(2,1)S(1)} %copy-done.2, bf16[96,2048]{1,0:T(8,128)(2,1)S(1)} %assemble.2.refs_1_, bf16[32,2048]{1,0:T(8,128)(2,1)S(1)} %collective-permute-done.3.refs_4_.refs_2_, ...), custom_call_target="tpu_custom_call" | custom-call | flops 3758096384 | bytes 14680064 | tf_op jit(solution)/shard_map/project/pallas_call | solution.py:150
  25.6 1.6 %collective-permute-start.6 = (bf16[2,64,1792]{2,1,0:T(8,128)(2,1)S(1)}, bf16[2,64,1792]{2,1,0:T(8,128)(2,1)S(1)}, u32[]{:S(2)}, u32[]{:S(2)}) collective-permute-start(bf16[2,64,1792]{2,1,0:T(8,128)(2,1)S(1)} %get-tuple-element.30), channel_id=1, source_target_pairs={{0,4},{4,0},{8,12},{12,8},{1,5},{5,1},{9,13},{13,9},{2,6},{6,2},{1... | collective-permute-start | bytes 1376264 | tf_op jit(solution)/shard_map/ppermute | solution.py:20
  27.1 1.5 %collective-permute-start.7 = (bf16[2,64,1792]{2,1,0:T(8,128)(2,1)S(1)}, bf16[2,64,1792]{2,1,0:T(8,128)(2,1)S(1)}, u32[]{:S(2)}, u32[]{:S(2)}) collective-permute-start(bf16[2,64,1792]{2,1,0:T(8,128)(2,1)S(1)} %get-tuple-element.31), channel_id=1, source_target_pairs={{0,8},{4,12},{8,0},{12,4},{1,9},{5,13},{9,1},{13,5},{2,10},{6,14},... | collective-permute-start | bytes 1376264 | tf_op jit(solution)/shard_map/ppermute | solution.py:20
  28.6 4.9 %collective-permute-done.8.refs_1_ = bf16[32,2048]{1,0:T(8,128)(2,1)S(1)} collective-permute-done((bf16[32,2048]{1,0:T(8,128)(2,1)S(1)}, bf16[32,2048]{1,0:T(8,128)(2,1)S(1)}, u32[]{:S(2)}, u32[]{:S(2)}) %collective-permute-start.8) | collective-permute-done | bytes 131104 | tf_op jit(solution)/shard_map/ppermute | solution.py:20
  33.6 0.1 collective-permute-start.11
  33.8 0.5 collective-permute-start.12
  34.3 0.1 collective-permute-start.10
  34.4 1.5 %collective-permute-done.10.refs_2_ = bf16[32,2048]{1,0:T(8,128)(2,1)S(1)} collective-permute-done((bf16[32,2048]{1,0:T(8,128)(2,1)S(1)}, bf16[32,2048]{1,0:T(8,128)(2,1)S(1)}, u32[]{:S(2)}, u32[]{:S(2)}) %collective-permute-start.10) | collective-permute-done | bytes 131104 | tf_op jit(solution)/shard_map/ppermute | solution.py:20
  35.9 2.1 %pull_back.1 = (f32[1,64,1792]{2,1,0:T(8,128)S(1)}, bf16[1,64,1792]{2,1,0:T(8,128)(2,1)S(1)}, bf16[1,64,1792]{2,1,0:T(8,128)(2,1)S(1)}, bf16[1,64,1792]{2,1,0:T(8,128)(2,1)S(1)}) custom-call(bf16[32,2048]{1,0:T(8,128)(2,1)S(1)} %copy-done.3, bf16[96,2048]{1,0:T(8,128)(2,1)S(1)} %assemble.3.refs_1_, bf16[32,2048]{1,0:T(8,128)(2,1)S(1)} %collective-permute-done.10.refs_2_, ...), custom_call_target="tpu_custom_call" | custom-call | tf_op jit(solution)/shard_map/pull_back/pallas_call | solution.py:150
  38.0 0.2 collective-permute-done.6.refs_1_
  38.2 1.2 %collective-permute-done.7.refs_2_ = bf16[2,64,1792]{2,1,0:T(8,128)(2,1)S(1)} collective-permute-done((bf16[2,64,1792]{2,1,0:T(8,128)(2,1)S(1)}, bf16[2,64,1792]{2,1,0:T(8,128)(2,1)S(1)}, u32[]{:S(2)}, u32[]{:S(2)}) %collective-permute-start.7) | collective-permute-done | bytes 458784 | tf_op jit(solution)/shard_map/ppermute | solution.py:20
  39.4 0.1 pass_on.1
  39.5 0.6 collective-permute-start.13
  40.1 1.5 %collective-permute-start.14 = (bf16[2,32,1792]{2,1,0:T(8,128)(2,1)S(1)}, bf16[2,32,1792]{2,1,0:T(8,128)(2,1)S(1)}, u32[]{:S(2)}, u32[]{:S(2)}) collective-permute-start(bf16[2,32,1792]{2,1,0:T(8,128)(2,1)S(1)} %get-tuple-element.35), channel_id=1, source_target_pairs={{0,8},{4,12},{8,0},{12,4},{1,9},{5,13},{9,1},{13,5},{2,10},{6,14},... | collective-permute-start | bytes 688136 | tf_op jit(solution)/shard_map/ppermute | solution.py:20
  41.6 1.4 %collective-permute-start.18 = (bf16[1,64,1792]{2,1,0:T(8,128)(2,1)S(1)}, bf16[1,64,1792]{2,1,0:T(8,128)(2,1)S(1)}, u32[]{:S(2)}, u32[]{:S(2)}) collective-permute-start(bf16[1,64,1792]{2,1,0:T(8,128)(2,1)S(1)} %get-tuple-element.36), channel_id=1, source_target_pairs={{0,12},{4,8},{8,4},{12,0},{1,13},{5,9},{9,5},{13,1},{2,14},{6,10},... | collective-permute-start | bytes 688136 | tf_op jit(solution)/shard_map/ppermute | solution.py:20
  43.1 0.5 collective-permute-start.19
  43.6 1.5 %collective-permute-start.20 = (bf16[1,64,1792]{2,1,0:T(8,128)(2,1)S(1)}, bf16[1,64,1792]{2,1,0:T(8,128)(2,1)S(1)}, u32[]{:S(2)}, u32[]{:S(2)}) collective-permute-start(bf16[1,64,1792]{2,1,0:T(8,128)(2,1)S(1)} %get-tuple-element.38), channel_id=1, source_target_pairs={{0,8},{4,12},{8,0},{12,4},{1,9},{5,13},{9,1},{13,5},{2,10},{6,14},... | collective-permute-start | bytes 688136 | tf_op jit(solution)/shard_map/ppermute | solution.py:20
  45.1 3.0 %collective-permute-done.13.refs_3_ = bf16[2,32,1792]{2,1,0:T(8,128)(2,1)S(1)} collective-permute-done((bf16[2,32,1792]{2,1,0:T(8,128)(2,1)S(1)}, bf16[2,32,1792]{2,1,0:T(8,128)(2,1)S(1)}, u32[]{:S(2)}, u32[]{:S(2)}) %collective-permute-start.13) | collective-permute-done | bytes 229408 | tf_op jit(solution)/shard_map/ppermute | solution.py:20
  48.1 5.0 %collective-permute-done.14.refs_4_ = bf16[2,32,1792]{2,1,0:T(8,128)(2,1)S(1)} collective-permute-done((bf16[2,32,1792]{2,1,0:T(8,128)(2,1)S(1)}, bf16[2,32,1792]{2,1,0:T(8,128)(2,1)S(1)}, u32[]{:S(2)}, u32[]{:S(2)}) %collective-permute-start.14) | collective-permute-done | bytes 229408 | tf_op jit(solution)/shard_map/ppermute | solution.py:20
  53.1 0.2 hidden.1.refs_6_.refs_0_
  53.3 1.9 %collective-permute-start.17 = (bf16[1,64,1792]{2,1,0:T(8,128)(2,1)S(1)}, bf16[1,64,1792]{2,1,0:T(8,128)(2,1)S(1)}, u32[]{:S(2)}, u32[]{:S(2)}) collective-permute-start(bf16[1,64,1792]{2,1,0:T(8,128)(2,1)S(1)} %hidden.1.refs_6_.refs_0_), channel_id=1, source_target_pairs={{0,4},{4,0},{8,12},{12,8},{1,5},{5,1},{9,13},{13,9},{2,6},{6,2},{1... | collective-permute-start | bytes 688136 | tf_op jit(solution)/shard_map/ppermute | solution.py:20
  55.3 1.5 %collective-permute-start.16 = (bf16[1,64,1792]{2,1,0:T(8,128)(2,1)S(1)}, bf16[1,64,1792]{2,1,0:T(8,128)(2,1)S(1)}, u32[]{:S(2)}, u32[]{:S(2)}) collective-permute-start(bf16[1,64,1792]{2,1,0:T(8,128)(2,1)S(1)} %hidden.1.refs_6_.refs_0_), channel_id=1, source_target_pairs={{0,12},{4,8},{8,4},{12,0},{1,13},{5,9},{9,5},{13,1},{2,14},{6,10},... | collective-permute-start | bytes 688136 | tf_op jit(solution)/shard_map/ppermute | solution.py:20
  56.8 0.1 collective-permute-start.15
  56.9 1.1 collective-permute-done.19.refs_2_
  57.9 0.5 collective-permute-done.20.refs_3_
  58.5 0.3 slopes.1.refs_5_.refs_0_
  58.8 1.6 %collective-permute-start.26 = (bf16[2,64,1792]{2,1,0:T(8,128)(2,1)S(1)}, bf16[2,64,1792]{2,1,0:T(8,128)(2,1)S(1)}, u32[]{:S(2)}, u32[]{:S(2)}) collective-permute-start(bf16[2,64,1792]{2,1,0:T(8,128)(2,1)S(1)} %slopes.1.refs_5_.refs_0_), channel_id=1, source_target_pairs={{0,8},{4,12},{8,0},{12,4},{1,9},{5,13},{9,1},{13,5},{2,10},{6,14},... | collective-permute-start | bytes 1376264 | tf_op jit(solution)/shard_map/ppermute | solution.py:20
  60.4 1.4 %collective-permute-start.25 = (bf16[2,64,1792]{2,1,0:T(8,128)(2,1)S(1)}, bf16[2,64,1792]{2,1,0:T(8,128)(2,1)S(1)}, u32[]{:S(2)}, u32[]{:S(2)}) collective-permute-start(bf16[2,64,1792]{2,1,0:T(8,128)(2,1)S(1)} %slopes.1.refs_5_.refs_0_), channel_id=1, source_target_pairs={{0,4},{4,0},{8,12},{12,8},{1,5},{5,1},{9,13},{13,9},{2,6},{6,2},{1... | collective-permute-start | bytes 1376264 | tf_op jit(solution)/shard_map/ppermute | solution.py:20
  61.8 1.0 collective-permute-done.17.refs_3_
  62.9 5.9 %collective-permute-done.16.refs_2_ = bf16[1,64,1792]{2,1,0:T(8,128)(2,1)S(1)} collective-permute-done((bf16[1,64,1792]{2,1,0:T(8,128)(2,1)S(1)}, bf16[1,64,1792]{2,1,0:T(8,128)(2,1)S(1)}, u32[]{:S(2)}, u32[]{:S(2)}) %collective-permute-start.16) | collective-permute-done | bytes 229408 | tf_op jit(solution)/shard_map/ppermute | solution.py:20
  68.7 1.2 %collective-permute-done.15.refs_1_ = bf16[1,64,1792]{2,1,0:T(8,128)(2,1)S(1)} collective-permute-done((bf16[1,64,1792]{2,1,0:T(8,128)(2,1)S(1)}, bf16[1,64,1792]{2,1,0:T(8,128)(2,1)S(1)}, u32[]{:S(2)}, u32[]{:S(2)}) %collective-permute-start.15) | collective-permute-done | bytes 229408 | tf_op jit(solution)/shard_map/ppermute | solution.py:20
  70.0 2.1 %layer_output.1 = (f32[128,2048]{1,0:T(8,128)S(1)}, bf16[128,2048]{1,0:T(8,128)(2,1)S(1)}) custom-call(bf16[1,64,1792]{2,1,0:T(8,128)(2,1)S(1)} %hidden.1.refs_6_.refs_0_, bf16[1,64,1792]{2,1,0:T(8,128)(2,1)S(1)} %collective-permute-done.15.refs_1_, bf16[1,64,1792]{2,1,0:T(8,128)(2,1)S(1)} %collective-permute-done.16.refs_2_, ...), custom_call_target="tpu_custom_call" | custom-call | flops 1879048192 | bytes 7340032 | tf_op jit(solution)/shard_map/layer_output/pallas_call | solution.py:224
  72.1 0.1 collective-permute-start.21
  72.1 4.4 %collective-permute-done.26.refs_2_ = bf16[2,64,1792]{2,1,0:T(8,128)(2,1)S(1)} collective-permute-done((bf16[2,64,1792]{2,1,0:T(8,128)(2,1)S(1)}, bf16[2,64,1792]{2,1,0:T(8,128)(2,1)S(1)}, u32[]{:S(2)}, u32[]{:S(2)}) %collective-permute-start.26) | collective-permute-done | bytes 458784 | tf_op jit(solution)/shard_map/ppermute | solution.py:20
  76.6 0.8 collective-permute-start.28
  77.4 1.6 %collective-permute-start.27 = (bf16[2,32,1792]{2,1,0:T(8,128)(2,1)S(1)}, bf16[2,32,1792]{2,1,0:T(8,128)(2,1)S(1)}, u32[]{:S(2)}, u32[]{:S(2)}) collective-permute-start(bf16[2,32,1792]{2,1,0:T(8,128)(2,1)S(1)} %slice.8), channel_id=1, source_target_pairs={{0,8},{4,12},{8,0},{12,4},{1,9},{5,13},{9,1},{13,5},{2,10},{6,14},... | collective-permute-start | bytes 688136 | tf_op jit(solution)/shard_map/ppermute | solution.py:20
  79.0 0.1 add_core.2
  79.1 1.6 %collective-permute-start.22 = (bf16[32,2048]{1,0:T(8,128)(2,1)S(1)}, bf16[32,2048]{1,0:T(8,128)(2,1)S(1)}, u32[]{:S(2)}, u32[]{:S(2)}) collective-permute-start(bf16[32,2048]{1,0:T(8,128)(2,1)S(1)} %get-tuple-element.43), channel_id=1, source_target_pairs={{0,3},{1,2},{2,1},{3,0},{4,7},{5,6},{6,5},{7,4},{8,11},{9,10},{10,... | collective-permute-start | bytes 393224 | tf_op jit(solution)/shard_map/ppermute | solution.py:20
  80.8 0.8 collective-permute-start.23
  81.6 2.0 %collective-permute-start.24 = (bf16[32,2048]{1,0:T(8,128)(2,1)S(1)}, bf16[32,2048]{1,0:T(8,128)(2,1)S(1)}, u32[]{:S(2)}, u32[]{:S(2)}) collective-permute-start(bf16[32,2048]{1,0:T(8,128)(2,1)S(1)} %get-tuple-element.45), channel_id=1, source_target_pairs={{0,1},{1,0},{2,3},{3,2},{4,5},{5,4},{6,7},{7,6},{8,9},{9,8},{10,11... | collective-permute-start | bytes 393224 | tf_op jit(solution)/shard_map/ppermute | solution.py:20
  83.6 4.0 %input_grad.1 = (f32[128,2048]{1,0:T(8,128)S(1)}, bf16[128,2048]{1,0:T(8,128)(2,1)S(1)}) custom-call(bf16[2,64,1792]{2,1,0:T(8,128)(2,1)S(1)} %slopes.1.refs_5_.refs_0_, bf16[2,64,1792]{2,1,0:T(8,128)(2,1)S(1)} %collective-permute-done.25.refs_1_, bf16[2,64,1792]{2,1,0:T(8,128)(2,1)S(1)} %collective-permute-done.26.refs_2_, ...), custom_call_target="tpu_custom_call" | custom-call | flops 3758096384 | bytes 14680064 | tf_op jit(solution)/shard_map/input_grad/pallas_call | solution.py:224
  87.6 3.2 %collective-permute-done.23.refs_2_ = bf16[32,2048]{1,0:T(8,128)(2,1)S(1)} collective-permute-done((bf16[32,2048]{1,0:T(8,128)(2,1)S(1)}, bf16[32,2048]{1,0:T(8,128)(2,1)S(1)}, u32[]{:S(2)}, u32[]{:S(2)}) %collective-permute-start.23) | collective-permute-done | bytes 131104 | tf_op jit(solution)/shard_map/ppermute | solution.py:20
  90.9 0.1 collective-permute-start.29
  91.0 1.9 %collective-permute-done.29.refs_1_ = bf16[128,2048]{1,0:T(8,128)(2,1)S(1)} collective-permute-done((bf16[128,2048]{1,0:T(8,128)(2,1)S(1)}, bf16[128,2048]{1,0:T(8,128)(2,1)S(1)}, u32[]{:S(2)}, u32[]{:S(2)}) %collective-permute-start.29) | collective-permute-done | bytes 524320 | tf_op jit(solution)/shard_map/ppermute | solution.py:20
  92.9 0.1 add_core.3
  92.9 2.4 %collective-permute-start.30 = (bf16[32,2048]{1,0:T(8,128)(2,1)S(1)}, bf16[32,2048]{1,0:T(8,128)(2,1)S(1)}, u32[]{:S(2)}, u32[]{:S(2)}) collective-permute-start(bf16[32,2048]{1,0:T(8,128)(2,1)S(1)} %get-tuple-element.49), channel_id=1, source_target_pairs={{0,3},{1,2},{2,1},{3,0},{4,7},{5,6},{6,5},{7,4},{8,11},{9,10},{10,... | collective-permute-start | bytes 393224 | tf_op jit(solution)/shard_map/ppermute | solution.py:20
  95.4 2.0 %collective-permute-start.32 = (bf16[32,2048]{1,0:T(8,128)(2,1)S(1)}, bf16[32,2048]{1,0:T(8,128)(2,1)S(1)}, u32[]{:S(2)}, u32[]{:S(2)}) collective-permute-start(bf16[32,2048]{1,0:T(8,128)(2,1)S(1)} %get-tuple-element.51), channel_id=1, source_target_pairs={{0,1},{1,0},{2,3},{3,2},{4,5},{5,4},{6,7},{7,6},{8,9},{9,8},{10,11... | collective-permute-start | bytes 393224 | tf_op jit(solution)/shard_map/ppermute | solution.py:20
  97.4 0.7 add_convert_fusion.1
  98.1 3.2 %collective-permute-done.30 = bf16[32,2048]{1,0:T(8,128)(2,1)S(1)} collective-permute-done((bf16[32,2048]{1,0:T(8,128)(2,1)S(1)}, bf16[32,2048]{1,0:T(8,128)(2,1)S(1)}, u32[]{:S(2)}, u32[]{:S(2)}) %collective-permute-start.30) | collective-permute-done | bytes 131104 | tf_op jit(solution)/shard_map/ppermute | solution.py:20
  101.3 4.7 %collective-permute-done.31 = bf16[32,2048]{1,0:T(8,128)(2,1)S(1)} collective-permute-done((bf16[32,2048]{1,0:T(8,128)(2,1)S(1)}, bf16[32,2048]{1,0:T(8,128)(2,1)S(1)}, u32[]{:S(2)}, u32[]{:S(2)}) %collective-permute-start.31) | collective-permute-done | bytes 131104 | tf_op jit(solution)/shard_map/ppermute | solution.py:20
  106.0 0.7 add_convert_fusion
  (28 shorter events, 0.2 us)
Async XLA Ops:
  0.6 20.9 %copy-start.2 = (bf16[32,2048]{1,0:T(8,128)(2,1)S(1)}, bf16[32,2048]{1,0:T(8,128)(2,1)}, u32[]{:S(2)}) copy-start(bf16[32,2048]{1,0:T(8,128)(2,1)} %refs_0_.3) | copy-start | bytes 393220
  0.6 17.5 %copy-start.3 = (bf16[32,2048]{1,0:T(8,128)(2,1)S(1)}, bf16[32,2048]{1,0:T(8,128)(2,1)}, u32[]{:S(2)}) copy-start(bf16[32,2048]{1,0:T(8,128)(2,1)} %refs_0_.5) | copy-start | bytes 393220
  0.7 14.7 %collective-permute-start.2 = (bf16[32,2048]{1,0:T(8,128)(2,1)}, bf16[32,2048]{1,0:T(8,128)(2,1)S(1)}, u32[]{:S(2)}, u32[]{:S(2)}) collective-permute-start(bf16[32,2048]{1,0:T(8,128)(2,1)} %refs_0_.3), channel_id=1, source_target_pairs={{0,3},{1,2},{2,1},{3,0},{4,7},{5,6},{6,5},{7,4},{8,11},{9,10},{10,... | collective-permute-start | bytes 393224 | tf_op jit(solution)/shard_map/ppermute | solution.py:20
  5.8 11.4 %collective-permute-start.1 = (bf16[32,2048]{1,0:T(8,128)(2,1)}, bf16[32,2048]{1,0:T(8,128)(2,1)S(1)}, u32[]{:S(2)}, u32[]{:S(2)}) collective-permute-start(bf16[32,2048]{1,0:T(8,128)(2,1)} %refs_0_.3), channel_id=1, source_target_pairs={{0,2},{1,3},{2,0},{3,1},{4,6},{5,7},{6,4},{7,5},{8,10},{9,11},{10,... | collective-permute-start | bytes 393224 | tf_op jit(solution)/shard_map/ppermute | solution.py:20
  5.8 11.4 %collective-permute-start = (bf16[32,2048]{1,0:T(8,128)(2,1)}, bf16[32,2048]{1,0:T(8,128)(2,1)S(1)}, u32[]{:S(2)}, u32[]{:S(2)}) collective-permute-start(bf16[32,2048]{1,0:T(8,128)(2,1)} %refs_0_.3), channel_id=1, source_target_pairs={{0,1},{1,0},{2,3},{3,2},{4,5},{5,4},{6,7},{7,6},{8,9},{9,8},{10,11... | collective-permute-start | bytes 393224 | tf_op jit(solution)/shard_map/ppermute | solution.py:20
  6.4 10.8 %collective-permute-start.3 = (bf16[32,2048]{1,0:T(8,128)(2,1)}, bf16[32,2048]{1,0:T(8,128)(2,1)S(1)}, u32[]{:S(2)}, u32[]{:S(2)}) collective-permute-start(bf16[32,2048]{1,0:T(8,128)(2,1)} %refs_0_.3), channel_id=1, source_target_pairs={{0,16},{16,0},{1,17},{17,1},{2,18},{18,2},{3,19},{19,3},{4,20},{20... | collective-permute-start | bytes 393224 | tf_op jit(solution)/shard_map/ppermute | solution.py:20
  6.4 11.6 %collective-permute-start.4 = (bf16[32,2048]{1,0:T(8,128)(2,1)}, bf16[32,2048]{1,0:T(8,128)(2,1)S(1)}, u32[]{:S(2)}, u32[]{:S(2)}) collective-permute-start(bf16[32,2048]{1,0:T(8,128)(2,1)} %refs_0_.5), channel_id=1, source_target_pairs={{0,1},{1,0},{2,3},{3,2},{4,5},{5,4},{6,7},{7,6},{8,9},{9,8},{10,11... | collective-permute-start | bytes 393224 | tf_op jit(solution)/shard_map/ppermute | solution.py:20
  15.4 18.3 %copy-start = (bf16[32,3584]{1,0:T(8,128)(2,1)S(1)}, bf16[32,3584]{1,0:T(8,128)(2,1)}, u32[]{:S(2)}) copy-start(bf16[32,3584]{1,0:T(8,128)(2,1)} %refs_0_.4) | copy-start | bytes 688132
  15.4 18.3 %copy-start.1 = (bf16[32,3584]{1,0:T(8,128)(2,1)S(1)}, bf16[32,3584]{1,0:T(8,128)(2,1)}, u32[]{:S(2)}) copy-start(bf16[32,3584]{1,0:T(8,128)(2,1)} %refs_1_.1) | copy-start | bytes 688132
  18.0 3.5 %collective-permute-start.5 = (bf16[96,2048]{1,0:T(8,128)(2,1)S(1)}, bf16[96,2048]{1,0:T(8,128)(2,1)S(1)}, u32[]{:S(2)}, u32[]{:S(2)}) collective-permute-start(bf16[96,2048]{1,0:T(8,128)(2,1)S(1)} %assemble.2.refs_1_), channel_id=1, source_target_pairs={{0,16},{16,0},{1,17},{17,1},{2,18},{18,2},{3,19},{19,3},{4,20},{20... | collective-permute-start | bytes 1179656 | tf_op jit(solution)/shard_map/ppermute | solution.py:20
  18.1 10.5 %collective-permute-start.9 = (bf16[32,2048]{1,0:T(8,128)(2,1)S(1)}, bf16[32,2048]{1,0:T(8,128)(2,1)S(1)}, u32[]{:S(2)}, u32[]{:S(2)}) collective-permute-start(bf16[32,2048]{1,0:T(8,128)(2,1)S(1)} %copy-done.3), channel_id=1, source_target_pairs={{0,3},{1,2},{2,1},{3,0},{4,7},{5,6},{6,5},{7,4},{8,11},{9,10},{10,... | collective-permute-start | bytes 393224 | tf_op jit(solution)/shard_map/ppermute | solution.py:20
  21.5 12.0 %collective-permute-start.8 = (bf16[32,2048]{1,0:T(8,128)(2,1)S(1)}, bf16[32,2048]{1,0:T(8,128)(2,1)S(1)}, u32[]{:S(2)}, u32[]{:S(2)}) collective-permute-start(bf16[32,2048]{1,0:T(8,128)(2,1)S(1)} %copy-done.3), channel_id=1, source_target_pairs={{0,2},{1,3},{2,0},{3,1},{4,6},{5,7},{6,4},{7,5},{8,10},{9,11},{10,... | collective-permute-start | bytes 393224 | tf_op jit(solution)/shard_map/ppermute | solution.py:20
  25.6 12.6 %collective-permute-start.6 = (bf16[2,64,1792]{2,1,0:T(8,128)(2,1)S(1)}, bf16[2,64,1792]{2,1,0:T(8,128)(2,1)S(1)}, u32[]{:S(2)}, u32[]{:S(2)}) collective-permute-start(bf16[2,64,1792]{2,1,0:T(8,128)(2,1)S(1)} %get-tuple-element.30), channel_id=1, source_target_pairs={{0,4},{4,0},{8,12},{12,8},{1,5},{5,1},{9,13},{13,9},{2,6},{6,2},{1... | collective-permute-start | bytes 1376264 | tf_op jit(solution)/shard_map/ppermute | solution.py:20
  27.1 12.3 %collective-permute-start.7 = (bf16[2,64,1792]{2,1,0:T(8,128)(2,1)S(1)}, bf16[2,64,1792]{2,1,0:T(8,128)(2,1)S(1)}, u32[]{:S(2)}, u32[]{:S(2)}) collective-permute-start(bf16[2,64,1792]{2,1,0:T(8,128)(2,1)S(1)} %get-tuple-element.31), channel_id=1, source_target_pairs={{0,8},{4,12},{8,0},{12,4},{1,9},{5,13},{9,1},{13,5},{2,10},{6,14},... | collective-permute-start | bytes 1376264 | tf_op jit(solution)/shard_map/ppermute | solution.py:20
  33.6 2.3 %collective-permute-start.11 = (bf16[96,2048]{1,0:T(8,128)(2,1)S(1)}, bf16[96,2048]{1,0:T(8,128)(2,1)S(1)}, u32[]{:S(2)}, u32[]{:S(2)}) collective-permute-start(bf16[96,2048]{1,0:T(8,128)(2,1)S(1)} %assemble.3.refs_1_), channel_id=1, source_target_pairs={{0,16},{16,0},{1,17},{17,1},{2,18},{18,2},{3,19},{19,3},{4,20},{20... | collective-permute-start | bytes 1179656 | tf_op jit(solution)/shard_map/ppermute | solution.py:20
  33.8 2.2 %collective-permute-start.12 = (bf16[2,32,1792]{2,1,0:T(8,128)(2,1)S(1)}, bf16[2,32,1792]{2,1,0:T(8,128)(2,1)S(1)}, u32[]{:S(2)}, u32[]{:S(2)}) collective-permute-start(bf16[2,32,1792]{2,1,0:T(8,128)(2,1)S(1)} %get-tuple-element.32), channel_id=1, source_target_pairs={{0,16},{16,0},{1,17},{17,1},{2,18},{18,2},{3,19},{19,3},{4,20},{20... | collective-permute-start | bytes 688136 | tf_op jit(solution)/shard_map/ppermute | solution.py:20
  34.3 1.6 %collective-permute-start.10 = (bf16[32,2048]{1,0:T(8,128)(2,1)S(1)}, bf16[32,2048]{1,0:T(8,128)(2,1)S(1)}, u32[]{:S(2)}, u32[]{:S(2)}) collective-permute-start(bf16[32,2048]{1,0:T(8,128)(2,1)S(1)} %copy-done.3), channel_id=1, source_target_pairs={{0,16},{16,0},{1,17},{17,1},{2,18},{18,2},{3,19},{19,3},{4,20},{20... | collective-permute-start | bytes 393224 | tf_op jit(solution)/shard_map/ppermute | solution.py:20
  39.5 8.6 %collective-permute-start.13 = (bf16[2,32,1792]{2,1,0:T(8,128)(2,1)S(1)}, bf16[2,32,1792]{2,1,0:T(8,128)(2,1)S(1)}, u32[]{:S(2)}, u32[]{:S(2)}) collective-permute-start(bf16[2,32,1792]{2,1,0:T(8,128)(2,1)S(1)} %get-tuple-element.34), channel_id=1, source_target_pairs={{0,4},{4,0},{8,12},{12,8},{1,5},{5,1},{9,13},{13,9},{2,6},{6,2},{1... | collective-permute-start | bytes 688136 | tf_op jit(solution)/shard_map/ppermute | solution.py:20
  40.1 13.0 %collective-permute-start.14 = (bf16[2,32,1792]{2,1,0:T(8,128)(2,1)S(1)}, bf16[2,32,1792]{2,1,0:T(8,128)(2,1)S(1)}, u32[]{:S(2)}, u32[]{:S(2)}) collective-permute-start(bf16[2,32,1792]{2,1,0:T(8,128)(2,1)S(1)} %get-tuple-element.35), channel_id=1, source_target_pairs={{0,8},{4,12},{8,0},{12,4},{1,9},{5,13},{9,1},{13,5},{2,10},{6,14},... | collective-permute-start | bytes 688136 | tf_op jit(solution)/shard_map/ppermute | solution.py:20
  41.6 15.2 %collective-permute-start.18 = (bf16[1,64,1792]{2,1,0:T(8,128)(2,1)S(1)}, bf16[1,64,1792]{2,1,0:T(8,128)(2,1)S(1)}, u32[]{:S(2)}, u32[]{:S(2)}) collective-permute-start(bf16[1,64,1792]{2,1,0:T(8,128)(2,1)S(1)} %get-tuple-element.36), channel_id=1, source_target_pairs={{0,12},{4,8},{8,4},{12,0},{1,13},{5,9},{9,5},{13,1},{2,14},{6,10},... | collective-permute-start | bytes 688136 | tf_op jit(solution)/shard_map/ppermute | solution.py:20
  43.1 14.9 %collective-permute-start.19 = (bf16[1,64,1792]{2,1,0:T(8,128)(2,1)S(1)}, bf16[1,64,1792]{2,1,0:T(8,128)(2,1)S(1)}, u32[]{:S(2)}, u32[]{:S(2)}) collective-permute-start(bf16[1,64,1792]{2,1,0:T(8,128)(2,1)S(1)} %get-tuple-element.37), channel_id=1, source_target_pairs={{0,4},{4,0},{8,12},{12,8},{1,5},{5,1},{9,13},{13,9},{2,6},{6,2},{1... | collective-permute-start | bytes 688136 | tf_op jit(solution)/shard_map/ppermute | solution.py:20
  43.6 14.9 %collective-permute-start.20 = (bf16[1,64,1792]{2,1,0:T(8,128)(2,1)S(1)}, bf16[1,64,1792]{2,1,0:T(8,128)(2,1)S(1)}, u32[]{:S(2)}, u32[]{:S(2)}) collective-permute-start(bf16[1,64,1792]{2,1,0:T(8,128)(2,1)S(1)} %get-tuple-element.38), channel_id=1, source_target_pairs={{0,8},{4,12},{8,0},{12,4},{1,9},{5,13},{9,1},{13,5},{2,10},{6,14},... | collective-permute-start | bytes 688136 | tf_op jit(solution)/shard_map/ppermute | solution.py:20
  53.3 9.5 %collective-permute-start.17 = (bf16[1,64,1792]{2,1,0:T(8,128)(2,1)S(1)}, bf16[1,64,1792]{2,1,0:T(8,128)(2,1)S(1)}, u32[]{:S(2)}, u32[]{:S(2)}) collective-permute-start(bf16[1,64,1792]{2,1,0:T(8,128)(2,1)S(1)} %hidden.1.refs_6_.refs_0_), channel_id=1, source_target_pairs={{0,4},{4,0},{8,12},{12,8},{1,5},{5,1},{9,13},{13,9},{2,6},{6,2},{1... | collective-permute-start | bytes 688136 | tf_op jit(solution)/shard_map/ppermute | solution.py:20
  55.3 13.5 %collective-permute-start.16 = (bf16[1,64,1792]{2,1,0:T(8,128)(2,1)S(1)}, bf16[1,64,1792]{2,1,0:T(8,128)(2,1)S(1)}, u32[]{:S(2)}, u32[]{:S(2)}) collective-permute-start(bf16[1,64,1792]{2,1,0:T(8,128)(2,1)S(1)} %hidden.1.refs_6_.refs_0_), channel_id=1, source_target_pairs={{0,12},{4,8},{8,4},{12,0},{1,13},{5,9},{9,5},{13,1},{2,14},{6,10},... | collective-permute-start | bytes 688136 | tf_op jit(solution)/shard_map/ppermute | solution.py:20
  56.8 13.2 %collective-permute-start.15 = (bf16[1,64,1792]{2,1,0:T(8,128)(2,1)S(1)}, bf16[1,64,1792]{2,1,0:T(8,128)(2,1)S(1)}, u32[]{:S(2)}, u32[]{:S(2)}) collective-permute-start(bf16[1,64,1792]{2,1,0:T(8,128)(2,1)S(1)} %hidden.1.refs_6_.refs_0_), channel_id=1, source_target_pairs={{0,8},{4,12},{8,0},{12,4},{1,9},{5,13},{9,1},{13,5},{2,10},{6,14},... | collective-permute-start | bytes 688136 | tf_op jit(solution)/shard_map/ppermute | solution.py:20
  58.8 17.8 %collective-permute-start.26 = (bf16[2,64,1792]{2,1,0:T(8,128)(2,1)S(1)}, bf16[2,64,1792]{2,1,0:T(8,128)(2,1)S(1)}, u32[]{:S(2)}, u32[]{:S(2)}) collective-permute-start(bf16[2,64,1792]{2,1,0:T(8,128)(2,1)S(1)} %slopes.1.refs_5_.refs_0_), channel_id=1, source_target_pairs={{0,8},{4,12},{8,0},{12,4},{1,9},{5,13},{9,1},{13,5},{2,10},{6,14},... | collective-permute-start | bytes 1376264 | tf_op jit(solution)/shard_map/ppermute | solution.py:20
  60.4 17.1 %collective-permute-start.25 = (bf16[2,64,1792]{2,1,0:T(8,128)(2,1)S(1)}, bf16[2,64,1792]{2,1,0:T(8,128)(2,1)S(1)}, u32[]{:S(2)}, u32[]{:S(2)}) collective-permute-start(bf16[2,64,1792]{2,1,0:T(8,128)(2,1)S(1)} %slopes.1.refs_5_.refs_0_), channel_id=1, source_target_pairs={{0,4},{4,0},{8,12},{12,8},{1,5},{5,1},{9,13},{13,9},{2,6},{6,2},{1... | collective-permute-start | bytes 1376264 | tf_op jit(solution)/shard_map/ppermute | solution.py:20
  72.1 7.0 %collective-permute-start.21 = (bf16[128,2048]{1,0:T(8,128)(2,1)S(1)}, bf16[128,2048]{1,0:T(8,128)(2,1)S(1)}, u32[]{:S(2)}, u32[]{:S(2)}) collective-permute-start(bf16[128,2048]{1,0:T(8,128)(2,1)S(1)} %get-tuple-element.41), channel_id=1, source_target_pairs={{0,16},{16,0},{1,17},{17,1},{2,18},{18,2},{3,19},{19,3},{4,20},{20... | collective-permute-start | bytes 1572872 | tf_op jit(solution)/shard_map/ppermute | solution.py:20
  76.6 7.0 %collective-permute-start.28 = (bf16[2,32,1792]{2,1,0:T(8,128)(2,1)S(1)}, bf16[2,32,1792]{2,1,0:T(8,128)(2,1)S(1)}, u32[]{:S(2)}, u32[]{:S(2)}) collective-permute-start(bf16[2,32,1792]{2,1,0:T(8,128)(2,1)S(1)} %slice.9), channel_id=1, source_target_pairs={{0,4},{4,0},{8,12},{12,8},{1,5},{5,1},{9,13},{13,9},{2,6},{6,2},{1... | collective-permute-start | bytes 688136 | tf_op jit(solution)/shard_map/ppermute | solution.py:20
  77.4 6.1 %collective-permute-start.27 = (bf16[2,32,1792]{2,1,0:T(8,128)(2,1)S(1)}, bf16[2,32,1792]{2,1,0:T(8,128)(2,1)S(1)}, u32[]{:S(2)}, u32[]{:S(2)}) collective-permute-start(bf16[2,32,1792]{2,1,0:T(8,128)(2,1)S(1)} %slice.8), channel_id=1, source_target_pairs={{0,8},{4,12},{8,0},{12,4},{1,9},{5,13},{9,1},{13,5},{2,10},{6,14},... | collective-permute-start | bytes 688136 | tf_op jit(solution)/shard_map/ppermute | solution.py:20
  79.1 8.5 %collective-permute-start.22 = (bf16[32,2048]{1,0:T(8,128)(2,1)S(1)}, bf16[32,2048]{1,0:T(8,128)(2,1)S(1)}, u32[]{:S(2)}, u32[]{:S(2)}) collective-permute-start(bf16[32,2048]{1,0:T(8,128)(2,1)S(1)} %get-tuple-element.43), channel_id=1, source_target_pairs={{0,3},{1,2},{2,1},{3,0},{4,7},{5,6},{6,5},{7,4},{8,11},{9,10},{10,... | collective-permute-start | bytes 393224 | tf_op jit(solution)/shard_map/ppermute | solution.py:20
  80.8 10.1 %collective-permute-start.23 = (bf16[32,2048]{1,0:T(8,128)(2,1)S(1)}, bf16[32,2048]{1,0:T(8,128)(2,1)S(1)}, u32[]{:S(2)}, u32[]{:S(2)}) collective-permute-start(bf16[32,2048]{1,0:T(8,128)(2,1)S(1)} %get-tuple-element.44), channel_id=1, source_target_pairs={{0,2},{1,3},{2,0},{3,1},{4,6},{5,7},{6,4},{7,5},{8,10},{9,11},{10,... | collective-permute-start | bytes 393224 | tf_op jit(solution)/shard_map/ppermute | solution.py:20
  81.6 9.3 %collective-permute-start.24 = (bf16[32,2048]{1,0:T(8,128)(2,1)S(1)}, bf16[32,2048]{1,0:T(8,128)(2,1)S(1)}, u32[]{:S(2)}, u32[]{:S(2)}) collective-permute-start(bf16[32,2048]{1,0:T(8,128)(2,1)S(1)} %get-tuple-element.45), channel_id=1, source_target_pairs={{0,1},{1,0},{2,3},{3,2},{4,5},{5,4},{6,7},{7,6},{8,9},{9,8},{10,11... | collective-permute-start | bytes 393224 | tf_op jit(solution)/shard_map/ppermute | solution.py:20
  90.9 2.0 %collective-permute-start.29 = (bf16[128,2048]{1,0:T(8,128)(2,1)S(1)}, bf16[128,2048]{1,0:T(8,128)(2,1)S(1)}, u32[]{:S(2)}, u32[]{:S(2)}) collective-permute-start(bf16[128,2048]{1,0:T(8,128)(2,1)S(1)} %hold.1), channel_id=1, source_target_pairs={{0,16},{16,0},{1,17},{17,1},{2,18},{18,2},{3,19},{19,3},{4,20},{20... | collective-permute-start | bytes 1572872 | tf_op jit(solution)/shard_map/ppermute | solution.py:20
  92.9 8.3 %collective-permute-start.30 = (bf16[32,2048]{1,0:T(8,128)(2,1)S(1)}, bf16[32,2048]{1,0:T(8,128)(2,1)S(1)}, u32[]{:S(2)}, u32[]{:S(2)}) collective-permute-start(bf16[32,2048]{1,0:T(8,128)(2,1)S(1)} %get-tuple-element.49), channel_id=1, source_target_pairs={{0,3},{1,2},{2,1},{3,0},{4,7},{5,6},{6,5},{7,4},{8,11},{9,10},{10,... | collective-permute-start | bytes 393224 | tf_op jit(solution)/shard_map/ppermute | solution.py:20
  95.4 10.6 %collective-permute-start.31 = (bf16[32,2048]{1,0:T(8,128)(2,1)S(1)}, bf16[32,2048]{1,0:T(8,128)(2,1)S(1)}, u32[]{:S(2)}, u32[]{:S(2)}) collective-permute-start(bf16[32,2048]{1,0:T(8,128)(2,1)S(1)} %get-tuple-element.50), channel_id=1, source_target_pairs={{0,2},{1,3},{2,0},{3,1},{4,6},{5,7},{6,4},{7,5},{8,10},{9,11},{10,... | collective-permute-start | bytes 393224 | tf_op jit(solution)/shard_map/ppermute | solution.py:20
  95.4 10.6 %collective-permute-start.32 = (bf16[32,2048]{1,0:T(8,128)(2,1)S(1)}, bf16[32,2048]{1,0:T(8,128)(2,1)S(1)}, u32[]{:S(2)}, u32[]{:S(2)}) collective-permute-start(bf16[32,2048]{1,0:T(8,128)(2,1)S(1)} %get-tuple-element.51), channel_id=1, source_target_pairs={{0,1},{1,0},{2,3},{3,2},{4,5},{5,4},{6,7},{7,6},{8,9},{9,8},{10,11... | collective-permute-start | bytes 393224 | tf_op jit(solution)/shard_map/ppermute | solution.py:20
